TPU v7x, 256 devices: a whole 4x4x8 slice. The times are simulated.
256 devices in a mesh: dp: 32 (over x, z), expert: 8 (over y, core).
Axes of the slice: x: 4, y: 4, z: 8, core: 2. Of those that a mesh axis runs over, the one named last changes fastest.
Arguments:
- queries: bfloat16 [512, 6144], P('dp', 'expert'), may hold values from -48 to 48
- new_keys: bfloat16 [512, 1024], P('dp', 'expert'), may hold values from -6 to 6
- new_values: bfloat16 [512, 1024], P('dp', 'expert'), may hold values from -6 to 6
- k_cache: bfloat16 [512, 8, 128, 128], P('dp', 'expert'), may hold values from -48 to 48
- v_cache: bfloat16 [512, 8, 128, 128], P('dp', 'expert'), may hold values from -6 to 6
- lengths: int32 [512], P('dp'), may hold values from 2 to 128, as said below
- residual: bfloat16 [512, 6144], P(None, 'dp'), may hold values from -6 to 6
- w_out: bfloat16 [6144, 6144], P('expert', 'dp'), may hold values from -0.078125 to 0.078125
- router: bfloat16 [6144, 8], replicated, may hold values from -0.078125 to 0.078125
- gain_moe: float32 [6144], replicated, may hold values from 0.5 to 1.5
- w_gate: bfloat16 [8, 6144, 8192], P('expert', None, 'dp'), may hold values from -0.078125 to 0.078125
- w_up: bfloat16 [8, 6144, 8192], P('expert', None, 'dp'), may hold values from -0.078125 to 0.078125
- w_down: bfloat16 [8, 8192, 6144], P('expert', 'dp'), may hold values from -0.0625 to 0.0625
- expert_ids: int32 [512, 2], replicated, may hold values from 0 to 7, all different within a row; in each aligned block of 512 rows (0 to 511, 512 to 1023, ...) at most 256 rows name the same one
- gain_final: float32 [6144], replicated, may hold values from 0.5 to 1.5
- w_vocab: bfloat16 [6144, 32768], P(None, ('dp', 'expert')), may hold values from -12 to 12
- tokens: int32 [512], replicated, may hold values from 0 to 32767
- mu: float32 [512], P(('dp', 'expert')), may hold values from 6 to 12
Outputs:
- hidden_out: bfloat16 [512, 6144], P(('dp', 'expert'))
- surprise: float32 [512], P(('dp', 'expert'))
- mu_next: float32 [512], P(('dp', 'expert'))
Inputs may be any that keep to these rules, and one draw needn't show every extreme that they name: `expert_ids`: no expert is named by more than 256 requests, a bound that some block reaches; the two experts of a request differ. `lengths`: some request holds exactly 128 cached positions.
All inputs are finite; a program needn't handle non-finite values.
Results may differ from a plain program's by a relative error of at most 0.008.
Values may be sent and summed in bfloat16 or wider, within the bound.
No kernel may reach another device: no remote copies, remote signals or barrier semaphores. Data moves between devices by JAX's collectives and lax.ppermute only.
A program may use at most 128 MiB of HBM per device.

v0:
```python
import jax
import jax.numpy as jnp
from jax import lax
from jax.sharding import PartitionSpec as P

EPS = 1e-05
TARGET = 5.0
RATE = 0.1
LOG_TWO = 0.6931471805599453


def attend(queries, new_keys, new_values, k_cache, v_cache, lengths):
    rows, heads_kv, span, width = k_cache.shape
    group = queries.shape[1] // (heads_kv * width)
    query = queries.reshape(rows, heads_kv, group, width)
    scale = width ** (-0.5)
    cached = (
        jnp.einsum("rkgd,rkld->rkgl", query, k_cache, preferred_element_type=jnp.float32) * scale
    )
    fresh_key = new_keys.reshape(rows, heads_kv, width)
    fresh = (
        jnp.einsum("rkgd,rkd->rkg", query, fresh_key, preferred_element_type=jnp.float32) * scale
    )
    live = jnp.arange(span, dtype=jnp.int32)[None, :] < lengths[:, None]
    cached = jnp.where(live[:, None, None, :], cached, -1e30)
    top = jnp.maximum(jnp.max(cached, axis=-1), fresh)
    part_cached = jnp.exp(cached - top[..., None])
    part_fresh = jnp.exp(fresh - top)
    total = jnp.sum(part_cached, axis=-1) + part_fresh
    weight_cached = (part_cached / total[..., None]).astype(jnp.bfloat16)
    weight_fresh = (part_fresh / total).astype(jnp.bfloat16)
    fresh_value = new_values.reshape(rows, heads_kv, 1, width).astype(jnp.float32)
    out = jnp.einsum("rkgl,rkld->rkgd", weight_cached, v_cache, preferred_element_type=jnp.float32)
    out = out + weight_fresh.astype(jnp.float32)[..., None] * fresh_value
    return out.reshape(rows, group * heads_kv * width).astype(jnp.bfloat16)


def shards(
    queries,
    new_keys,
    new_values,
    k_cache,
    v_cache,
    lengths,
    residual,
    w_out,
    router,
    gain_moe,
    w_gate,
    w_up,
    w_down,
    expert_ids,
    gain_final,
    w_vocab,
    tokens,
    mu,
):
    attended = attend(queries, new_keys, new_values, k_cache, v_cache, lengths)
    partial_heads = jnp.dot(
        lax.all_gather(attended, "dp", axis=0, tiled=True),
        w_out,
        preferred_element_type=jnp.float32,
    )
    summed_heads = lax.psum(partial_heads, "expert")
    hidden = (residual.astype(jnp.float32) + summed_heads).astype(jnp.bfloat16)
    total_rows, width_dev = hidden.shape
    width_all = gain_moe.shape[0]
    expert = lax.axis_index("expert")
    experts_all = lax.axis_size("expert")
    capacity = 4 * total_rows // experts_all
    first = expert_ids[:, 0]
    second = expert_ids[:, 1]
    hit = (first == expert) | (second == expert)
    slot = jnp.cumsum(hit.astype(jnp.int32)) - 1
    positions = jnp.arange(total_rows, dtype=jnp.int32)
    order = (
        jnp.zeros((capacity,), jnp.int32)
        .at[jnp.where(hit, slot, capacity)]
        .set(positions, mode="drop")
    )
    valid = (jnp.arange(capacity, dtype=jnp.int32) < jnp.sum(hit.astype(jnp.int32))).astype(
        jnp.float32
    )
    gate_local = w_gate[0]
    up_local = w_up[0]
    piece_f = jnp.take(lax.all_gather(hidden, "dp", axis=1, tiled=True), order, axis=0).astype(
        jnp.float32
    )
    scaled = (piece_f * gain_moe[None, :]).astype(jnp.bfloat16)
    gate = jnp.dot(scaled, gate_local, preferred_element_type=jnp.float32)
    up = jnp.dot(scaled, up_local, preferred_element_type=jnp.float32)
    route = jnp.dot(scaled, router, preferred_element_type=jnp.float32)
    squares = jnp.sum(piece_f * piece_f, axis=1)
    gate, up, route, squares = (gate, up, route, squares)
    scale_moe = lax.rsqrt(squares / width_all + EPS)
    gate = scale_moe[:, None] * gate
    up = scale_moe[:, None] * up
    route = scale_moe[:, None] * route
    act = (jax.nn.silu(gate) * up).astype(jnp.bfloat16)
    slot_first = jnp.take(first, order)
    slot_second = jnp.take(second, order)
    first_logit = jnp.take_along_axis(route, slot_first[:, None], axis=1)[:, 0]
    second_logit = jnp.take_along_axis(route, slot_second[:, None], axis=1)[:, 0]
    weight = jnp.where(
        slot_first == expert,
        1.0 / (1.0 + jnp.exp(second_logit - first_logit)),
        1.0 / (1.0 + jnp.exp(first_logit - second_logit)),
    )
    slot_out = (weight * valid)[:, None] * jnp.dot(
        act, w_down[0], preferred_element_type=jnp.float32
    )
    dp_index = lax.axis_index("dp")
    dp_size = lax.axis_size("dp")
    column_start = dp_index * width_dev
    owners = dp_size * experts_all
    own_rows = total_rows // owners
    row_slot = jnp.where(hit, slot, 0)
    keep_own = (expert == 0).astype(jnp.float32)
    hits_here = hit.astype(jnp.float32)
    term = jnp.take(slot_out, row_slot, axis=0) * hits_here[:, None]
    own_part = hidden.astype(jnp.float32) * keep_own
    current = lax.dynamic_slice(
        term, (0, column_start), (own_rows * lax.axis_size(("dp", "expert")), width_dev)
    )
    summed_rows = lax.psum_scatter(
        lax.dynamic_update_slice(term, current + own_part, (0, column_start)),
        ("dp", "expert"),
        scatter_dimension=0,
        tiled=True,
    )
    hidden_out = summed_rows.astype(jnp.bfloat16)
    out_f = hidden_out.astype(jnp.float32)
    scale_final = lax.rsqrt(jnp.mean(out_f * out_f, axis=1) + EPS)
    final = (out_f * scale_final[:, None] * gain_final[None, :]).astype(jnp.bfloat16)
    logits = jnp.dot(
        lax.all_gather(final, ("dp", "expert"), axis=0, tiled=True),
        w_vocab,
        preferred_element_type=jnp.float32,
    )
    vocab_dev = w_vocab.shape[1]
    owner = lax.axis_index(("dp", "expert"))
    local_token = tokens - owner * vocab_dev
    inside = (local_token >= 0) & (local_token < vocab_dev)
    picked_logit = jnp.take_along_axis(
        logits, jnp.clip(local_token, 0, vocab_dev - 1)[:, None], axis=1
    )[:, 0]
    top = lax.pmax(jnp.max(logits, axis=1), ("dp", "expert"))
    summed, chosen = lax.psum(
        (jnp.sum(jnp.exp(logits - top[:, None]), axis=1), jnp.where(inside, picked_logit, 0.0)),
        ("dp", "expert"),
    )
    surprise_all = (top + jnp.log(summed) - chosen) / LOG_TWO
    surprise = lax.dynamic_slice_in_dim(surprise_all, owner * own_rows, own_rows)
    mu_next = mu - RATE * (surprise - TARGET)
    return (hidden_out, surprise, mu_next)


def solution(mesh):
    return jax.shard_map(
        shards,
        mesh=mesh,
        in_specs=(
            P("dp", "expert"),
            P("dp", "expert"),
            P("dp", "expert"),
            P("dp", "expert", None, None),
            P("dp", "expert", None, None),
            P("dp"),
            P(None, "dp"),
            P("expert", "dp"),
            P(),
            P(),
            P("expert", None, "dp"),
            P("expert", None, "dp"),
            P("expert", "dp", None),
            P(),
            P(),
            P(None, ("dp", "expert")),
            P(),
            P(("dp", "expert")),
        ),
        out_specs=(P(("dp", "expert"), None), P(("dp", "expert")), P(("dp", "expert"))),
        check_vma=False,
    )
```

profile of v0, /device:TPU:1, one launch (start us, length us, event | category | flops | bytes accessed | tf_op | source)
XLA Modules:
  0.0 757.4 jit_solution(9785874159247229766)
XLA Ops:
  7.2 0.9 reshape.216
  8.2 0.8 iota_compare_fusion
  9.0 0.8 fusion.56
  9.8 1.5 fusion.78
  11.3 0.2 fusion.53
  11.5 0.7 convert_element_type.72
  12.2 1.3 fusion.40
  13.6 42.4 %all_gather.9 = bf16[512,768]{1,0:T(8,128)(2,1)S(1)} all-gather(bf16[16,768]{1,0:T(8,128)(2,1)S(1)} %bitcast.79), channel_id=1, replica_groups=mesh['dp'=32,'expert'=8] {'dp'}, dimensions={0}, use_global_device_ids=true | all-gather | bytes 811008 | tf_op jit(solution)/shard_map/all_gather | solution.py:60
  55.9 2.1 fusion.80
  58.1 0.0 all-gather.4.cloned.1.call-start
  58.1 72.6 %all-reduce.5.cloned.1.call-done = f32[512,192]{0,1:T(8,128)} async-done(((f32[512,192]{0,1:T(8,128)}), f32[512,192]{0,1:T(8,128)}) %all-reduce.5.cloned.1.call-update) | async-done | bytes 393232 | tf_op jit(solution)/shard_map/psum | solution.py:64
  130.7 1.7 add_convert_fusion
  132.5 0.0 all-gather.6.cloned.1.call-start
  132.6 0.3 reduce-window.9
  132.9 0.1 slice.15
  133.0 0.1 slice_reduce_fusion
  133.1 0.1 add_add_fusion
  133.2 2.6 scatter_custom_fusion
  135.9 1.9 gather_fusion.3
  137.8 1.9 gather_fusion.4
  139.9 0.6 convert_reduce_fusion
  140.6 82.6 %all-gather.4.cloned.1.call-done = bf16[512,6144]{0,1:T(8,128)(2,1)} async-done(((bf16[512,192]{0,1:T(8,128)(2,1)}), bf16[512,6144]{0,1:T(8,128)(2,1)}) %all-gather.4.cloned.1.call-update) | async-done | bytes 6291472 | tf_op jit(solution)/shard_map/all_gather | solution.py:86
  223.2 8.7 %copy.28 = bf16[512,6144]{1,0:T(8,128)(2,1)} copy(bf16[512,6144]{0,1:T(8,128)(2,1)} %all-gather.4.cloned.1.call-done) | data formatting | bytes 12582912 | tf_op jit(solution)/shard_map/all_gather | solution.py:86
  231.9 10.8 %gather_fusion = bf16[256,6144]{1,0:T(8,128)(2,1)} fusion(bf16[512,6144]{1,0:T(8,128)(2,1)} %copy.28, s32[1024]{0:T(1024)S(1)} %pad_clamp_fusion.1), kind=kCustom, calls=%fused_computation.4 | custom fusion | bytes 6292480 | tf_op jit(solution)/shard_map/jit(_take)/gather | solution.py:86
  242.7 3.0 fusion
  245.7 3.0 fusion.15
  248.7 1.0 fusion.41
  249.7 1.8 gather_fusion.5
  251.6 2.0 gather_fusion.6
  253.7 0.7 compare_select_fusion.7
  254.3 9.0 %convolution_multiply_fusion = f32[256,6144]{1,0:T(8,128)} fusion(bf16[1,256,6144]{2,1,0:T(8,128)(2,1)S(1)} %copy-done, f32[256]{0:T(256)S(1)} %compare_select_fusion.7, bf16[1,6144,256]{2,1,0:T(8,128)(2,1)} %param.33, f32[6144]{0:T(1024)S(1)} %copy-done.10, f32[256,256]{1,0:T(8,128)S(1)} %fusion.15, f32[256]{0:T(256)S(1)} %add_rsqrt_fusion, ...), kind=kOutput, calls=%fused_computation.9 | convolution fusion | flops 1618935808 | bytes 16017664 | tf_op jit(solution)/shard_map/dot_general | solution.py:109
  263.3 15.4 %gather_fusion.1 = f32[512,6144]{1,0:T(8,128)} fusion(f32[256,6144]{1,0:T(8,128)} %convolution_multiply_fusion, s32[1024]{0:T(1024)S(1)} %pad_clamp_fusion), kind=kCustom, calls=%fused_computation.5 | custom fusion | bytes 25167872 | tf_op jit(solution)/shard_map/jit(_take)/gather | solution.py:120
  278.7 12.6 %copy.29 = f32[512,6144]{0,1:T(8,128)} copy(f32[512,6144]{1,0:T(8,128)} %gather_fusion.1) | data formatting | bytes 25165824 | tf_op jit(solution)/shard_map/jit(_take)/gather | solution.py:120
  291.2 10.8 %select_multiply_fusion = f32[512,6144]{0,1:T(8,128)} fusion(f32[512,6144]{0,1:T(8,128)} %copy.29, f32[512]{0:T(512)S(1)} %bitcast.89, pred[512]{0:T(512)(128)(4,1)S(1)} %get-tuple-element.20), kind=kLoop, calls=%fused_computation.8 | loop fusion | flops 6291456 | bytes 25168384 | tf_op jit(solution)/shard_map/mul | solution.py:120
  302.1 1.8 add_dynamic-update-slice_fusion
  303.9 157.0 %all-reduce.6 = bf16[512,6144]{0,1:T(8,128)(2,1)} all-reduce(f32[512,6144]{0,1:T(8,128)} %add_dynamic-update-slice_fusion), channel_id=2, replica_groups=mesh['dp'=32,'expert'=8] {'dp','expert'}, use_global_device_ids=true, to_apply=%region_8.11.clone | all-reduce | flops 3145728 | bytes 18874368
  460.9 2.3 fusion.2
  463.2 1.0 fusion.14
  464.2 1.3 copy.30
  465.6 1.3 copy.31
  467.0 111.8 %all-gather.6.cloned.1.call-done = bf16[256,2,6144]{2,1,0:T(2,128)(2,1)} async-done(((bf16[1,2,6144]{2,1,0:T(2,128)(2,1)}), bf16[256,2,6144]{2,1,0:T(2,128)(2,1)}) %all-gather.6.cloned.1.call-update) | async-done | bytes 6291472 | tf_op jit(solution)/shard_map/all_gather | solution.py:136
  578.7 13.3 %reshape.292 = bf16[512,6144]{1,0:T(8,128)(2,1)} reshape(bf16[256,2,6144]{2,1,0:T(2,128)(2,1)} %all-gather.6.cloned.1.call-done) | data formatting | bytes 12582912
  592.0 5.6 fusion.79
  597.6 75.3 %pmax.7 = f32[512]{0:T(512)S(1)} all-reduce(f32[512]{0:T(512)S(1)} %get-tuple-element.37), channel_id=1, replica_groups=mesh['dp'=32,'expert'=8] {'dp','expert'}, use_global_device_ids=true, to_apply=%region_11.14 | all-reduce | flops 512 | bytes 4096 | tf_op jit(solution)/shard_map/pmax | solution.py:147
  672.9 0.1 exponential_reduce_fusion
  672.9 4.5 gather_fusion.2
  677.5 72.8 %all-reduce.1 = (f32[512]{0:T(512)S(1)}, f32[512]{0:T(512)S(1)}) all-reduce(f32[512]{0:T(512)S(1)} %select_select_fusion, f32[512]{0:T(512)S(1)} %exponential_reduce_fusion), channel_id=1, replica_groups=mesh['dp'=32,'expert'=8] {'dp','expert'}, use_global_device_ids=true, to_apply=%region_14.17 | all-reduce | flops 1024 | bytes 8192 | tf_op jit(solution)/shard_map/psum | solution.py:148
  750.3 0.6 multiply_subtract_fusion
  (56 shorter events, 0.4 us)
Async XLA Ops:
  7.2 247.2 %copy-start = (bf16[1,256,6144]{2,1,0:T(8,128)(2,1)S(1)}, bf16[1,256,6144]{2,1,0:T(8,128)(2,1)}, u32[]{:S(2)}) copy-start(bf16[1,256,6144]{2,1,0:T(8,128)(2,1)} %param.34) | copy-start | bytes 9437188
  7.2 123.6 %copy-start.4 = (bf16[512,192]{0,1:T(8,128)(2,1)S(1)}, bf16[512,192]{0,1:T(8,128)(2,1)}, u32[]{:S(2)}) copy-start(bf16[512,192]{0,1:T(8,128)(2,1)} %param.28) | copy-start | bytes 589828
  7.2 125.4 %copy-start.6 = (s32[512,2]{0,1:T(2,128)S(1)}, s32[512,2]{0,1:T(2,128)}, u32[]{:S(2)}) copy-start(s32[512,2]{0,1:T(2,128)} %param.35) | copy-start | bytes 12292
  7.2 123.5 %all-reduce.5.cloned.1.call-start = ((), (), s32[]{:S(2)}) async-start(), calls=%async_computation | async-start | bytes 786432 | tf_op jit(solution)/shard_map/psum | solution.py:64
  58.1 165.2 %all-gather.4.cloned.1.call-start = ((), (), s32[]{:S(2)}) async-start(), calls=%async_computation.1 | async-start | bytes 6488064 | tf_op jit(solution)/shard_map/all_gather | solution.py:86
  132.5 446.2 %all-gather.6.cloned.1.call-start = ((), (), s32[]{:S(2)}) async-start(), calls=%async_computation.2 | async-start | bytes 6316032 | tf_op jit(solution)/shard_map/all_gather | solution.py:136
  231.9 13.8 %copy-start.10 = (f32[6144]{0:T(1024)S(1)}, f32[6144]{0:T(1024)}, u32[]{:S(2)}) copy-start(f32[6144]{0:T(1024)} %param.31) | copy-start | bytes 73732
  242.7 3.0 copy-start.2
  245.7 3.0 copy-start.9
  291.2 10.8 %copy-start.3 = (bf16[512,192]{0,1:T(8,128)(2,1)S(1)}, bf16[512,192]{0,1:T(8,128)(2,1)}, u32[]{:S(2)}) copy-start(bf16[512,192]{0,1:T(8,128)(2,1)} %add_convert_fusion) | copy-start | bytes 589828
  460.9 2.3 copy-start.5
  463.2 2.4 copy-start.7
  592.0 158.3 %copy-start.8 = (f32[2]{0:T(128)S(1)}, f32[2]{0:T(128)}, u32[]{:S(2)}) copy-start(f32[2]{0:T(128)} %param.39) | copy-start | bytes 28
  592.0 158.8 %copy-start.1 = (bf16[1,256,6144]{2,1,0:T(8,128)(2,1)S(1)}, bf16[1,256,6144]{2,1,0:T(8,128)(2,1)}, u32[]{:S(2)}) copy-start(bf16[1,256,6144]{2,1,0:T(8,128)(2,1)} %param.34) | copy-start | bytes 9437188
Sparse Core Ops, SparseCore 0:
  58.2 72.5 all-reduce.4
  133.6 89.5 all-gather.3
  465.7 113.0 all-gather.5
where the time goes:
time: 759 us; the launch traced here: 757 us
  blocking collectives  347 us (46%)
  waiting for transfers between devices  267 us (35%)
  local copies, waits for them, and re-layouts  79.5 us (10%)
  other arithmetic  24.9 us (3%)
  matrix products  24.3 us (3%)
  between operations  14.2 us (2%)
    unnamed x1, blocking collectives  157 us
    all_gather x1, waiting for transfers between devices, shards(): lax.all_gather(final, ('dp', 'expert'), axis=0, tiled=True)  112 us
    all_gather x1, waiting for transfers between devices, shards(): lax.all_gather(hidden, 'dp', axis=1, tiled=True)  82.6 us
    pmax x1, blocking collectives, shards(): top = lax.pmax(jnp.max(logits, axis=1), ('dp', 'expert'))  75.3 us
    psum x1, blocking collectives, shards(): lax.psum((jnp.sum(jnp.exp(logits - top[:, None]), axis=1), jnp.where(insi...  72.8 us
    psum x1, waiting for transfers between devices, shards(): summed_heads = lax.psum(partial_heads, 'expert')  72.6 us
    all_gather x1, blocking collectives, shards(): lax.all_gather(attended, 'dp', axis=0, tiled=True)  42.4 us
    gather x2, local copies, waits for them, and re-layouts, shards(): term = jnp.take(slot_out, row_slot, axis=0) * hits_here[:, None]  28 us
  transfers between devices with their start and end apart: 3, of which 3 were waited for; matrix products, arithmetic and copies ran while one was open for 1% of the time, Pallas kernels for 0%

commit v1 on v0

v1 whole, which is shorter than its diff:
```python
import jax
import jax.numpy as jnp
from jax import lax
from jax.experimental import pallas as pl
from jax.experimental.pallas import tpu as pltpu
from jax.sharding import Mesh
from jax.sharding import PartitionSpec as P

EPS = 1e-05
TARGET = 5.0
RATE = 0.1
LOG_TWO = 0.6931471805599453
F32 = jnp.float32
BF16 = jnp.bfloat16
NX, NZ, NY, NC = 4, 8, 4, 2
NXY = NX * NY
XY = ("x", "y")
EX = ("y", "c")
ALL = ("x", "z", "y", "c")


def swap_cores(value):
    return lax.ppermute(value, "c", [(0, 1), (1, 0)])


def exchange(value, axes):
    return lax.all_to_all(value, axes, split_axis=0, concat_axis=0, tiled=True)


def spread(value, axes, count):
    return exchange(jnp.broadcast_to(value[None], (count,) + value.shape), axes)


def attend(queries, new_keys, new_values, k_cache, v_cache, lengths):
    rows, heads_kv, span, width = k_cache.shape
    group = queries.shape[1] // (heads_kv * width)
    query = queries.reshape(rows, heads_kv, group, width)
    scale = width ** (-0.5)
    cached = (
        jnp.einsum("rkgd,rkld->rkgl", query, k_cache, preferred_element_type=F32) * scale
    )
    fresh_key = new_keys.reshape(rows, heads_kv, width)
    fresh = jnp.einsum("rkgd,rkd->rkg", query, fresh_key, preferred_element_type=F32) * scale
    live = jnp.arange(span, dtype=jnp.int32)[None, :] < lengths[:, None]
    cached = jnp.where(live[:, None, None, :], cached, -1e30)
    top = jnp.maximum(jnp.max(cached, axis=-1), fresh)
    part_cached = jnp.exp(cached - top[..., None])
    part_fresh = jnp.exp(fresh - top)
    total = jnp.sum(part_cached, axis=-1) + part_fresh
    weight_cached = (part_cached / total[..., None]).astype(BF16)
    weight_fresh = (part_fresh / total).astype(BF16)
    fresh_value = new_values.reshape(rows, heads_kv, 1, width).astype(F32)
    out = jnp.einsum("rkgl,rkld->rkgd", weight_cached, v_cache, preferred_element_type=F32)
    out = out + weight_fresh.astype(F32)[..., None] * fresh_value
    return out.reshape(rows, group * heads_kv * width).astype(BF16)


def expert_kernel(
    place, own, other, gate_w, up_w, router_w, gain, ids, act, gate_sum, up_sum, route_sum, squares
):
    step = pl.program_id(0)
    width = own.shape[-1]
    half = own.shape[0] * own.shape[2]
    hidden = jnp.concatenate(
        [own[...].reshape(half, width), other[...].reshape(half, width)], axis=0
    ).astype(F32)
    scaled = (hidden * gain[0]).astype(BF16)
    gate = jnp.dot(scaled, gate_w[...].reshape(width, -1), preferred_element_type=F32)
    up = jnp.dot(scaled, up_w[...].reshape(width, -1), preferred_element_type=F32)
    route = lax.dot_general(
        scaled, router_w[0], (((1,), (1,)), ((), ())), preferred_element_type=F32
    )
    square = jnp.sum(hidden * hidden, axis=1, keepdims=True)

    @pl.when(step == 0)
    def _():
        gate_sum[...] = gate
        up_sum[...] = up
        route_sum[...] = route
        squares[...] = square

    @pl.when(step > 0)
    def _():
        gate_sum[...] += gate
        up_sum[...] += up
        route_sum[...] += route
        squares[...] += square

    @pl.when(step == pl.num_programs(0) - 1)
    def _():
        expert = place[0]
        scale = lax.rsqrt(squares[...] / (width * NZ) + EPS)
        logits = route_sum[...] * scale
        lanes = lax.broadcasted_iota(jnp.int32, logits.shape, 1)
        first = ids[:, 0:1]
        second = ids[:, 1:2]
        first_logit = jnp.sum(jnp.where(lanes == first, logits, 0.0), axis=1, keepdims=True)
        second_logit = jnp.sum(jnp.where(lanes == second, logits, 0.0), axis=1, keepdims=True)
        is_first = first == expert
        gap = second_logit - first_logit
        weight = 1.0 / (1.0 + jnp.exp(jnp.where(is_first, gap, -gap)))
        weight = jnp.where(is_first | (second == expert), weight, 0.0)
        gated = gate_sum[...] * scale
        value = jax.nn.silu(gated) * (up_sum[...] * scale)
        act[...] = (weight * value).astype(BF16)


def experts(place, own, other, gate_w, up_w, router_w, gain, ids):
    _, _, rows, width = own.shape
    total = 2 * NXY * rows
    hidden_units = gate_w.shape[-1]
    unit = width // NX
    block = pl.BlockSpec((NXY, 1, rows, width), lambda z, p: (0, z, 0, 0))
    weights = pl.BlockSpec((NX, 1, unit, hidden_units), lambda z, p: (0, z, 0, 0))
    count = router_w.shape[1]
    return pl.pallas_call(
        expert_kernel,
        out_shape=jax.ShapeDtypeStruct((total, hidden_units), BF16),
        grid_spec=pltpu.PrefetchScalarGridSpec(
            num_scalar_prefetch=1,
            grid=(NZ,),
            in_specs=[
                block,
                block,
                weights,
                weights,
                pl.BlockSpec((1, count, width), lambda z, p: (z, 0, 0)),
                pl.BlockSpec((1, 1, width), lambda z, p: (z, 0, 0)),
                pl.BlockSpec((total, 2), lambda z, p: (0, 0)),
            ],
            out_specs=pl.BlockSpec((total, hidden_units), lambda z, p: (0, 0)),
            scratch_shapes=[
                pltpu.VMEM((total, hidden_units), F32),
                pltpu.VMEM((total, hidden_units), F32),
                pltpu.VMEM((total, count), F32),
                pltpu.VMEM((total, 1), F32),
            ],
        ),
        compiler_params=pltpu.CompilerParams(
            dimension_semantics=("arbitrary",), vmem_limit_bytes=48 << 20
        ),
        cost_estimate=pl.CostEstimate(
            flops=2 * total * width * NZ * 2 * hidden_units,
            bytes_accessed=13 << 20,
            transcendentals=total * hidden_units,
        ),
        name="experts",
    )(
        place,
        own,
        other,
        gate_w.reshape(NX, NZ, unit, hidden_units),
        up_w.reshape(NX, NZ, unit, hidden_units),
        router_w,
        gain,
        ids,
    )


def down_kernel(place, mine, theirs, w_mine, w_theirs, out):
    half = mine.shape[0] // 2
    rows = half // NXY
    width = out.shape[-1]
    core = place[1]
    for part in range(2):
        here = mine[part * half : (part + 1) * half, :]
        there = theirs[(1 - part) * half : (2 - part) * half, :]
        total = jnp.dot(here, w_mine[...], preferred_element_type=F32)
        total += jnp.dot(there, w_theirs[...], preferred_element_type=F32)
        start = pl.multiple_of((core if part == 0 else 1 - core) * rows, rows)
        out[:, 0, pl.ds(start, rows), :] = total.astype(BF16).reshape(NXY, rows, width)


def down(place, mine, theirs, w_mine, w_theirs):
    total, units = mine.shape
    width = w_theirs.shape[1] // NZ
    rows = total // NXY
    return pl.pallas_call(
        down_kernel,
        out_shape=jax.ShapeDtypeStruct((NXY, NZ, rows, width), BF16),
        grid_spec=pltpu.PrefetchScalarGridSpec(
            num_scalar_prefetch=1,
            grid=(NZ,),
            in_specs=[
                pl.BlockSpec((total, units), lambda z, p: (0, 0)),
                pl.BlockSpec((total, units), lambda z, p: (0, 0)),
                pl.BlockSpec((units, width), lambda z, p: (0, p[1] * NZ + z)),
                pl.BlockSpec((units, width), lambda z, p: (0, z)),
            ],
            out_specs=pl.BlockSpec((NXY, 1, rows, width), lambda z, p: (0, z, 0, 0)),
        ),
        compiler_params=pltpu.CompilerParams(
            dimension_semantics=("arbitrary",), vmem_limit_bytes=48 << 20
        ),
        cost_estimate=pl.CostEstimate(
            flops=2 * total * units * 2 * width * NZ, bytes_accessed=7 << 20, transcendentals=0
        ),
        name="down",
    )(place, mine, theirs, w_mine, w_theirs)


def head_kernel(place, own, other, weights, gain, token, stats, acc, squares):
    step = pl.program_id(0)
    width = own.shape[-1]
    total = acc.shape[0]

    @pl.when(step == 0)
    def _():
        acc[...] = jnp.zeros_like(acc)
        squares[...] = jnp.zeros_like(squares)

    def add(block):
        hidden = block[...].reshape(total, width).astype(F32)
        scaled = (hidden * gain[0]).astype(BF16)
        acc[...] += jnp.dot(scaled, weights[...], preferred_element_type=F32)
        squares[...] += jnp.sum(hidden * hidden, axis=1, keepdims=True)

    @pl.when(step < NZ)
    def _():
        add(own)

    @pl.when(step >= NZ)
    def _():
        add(other)

    @pl.when(step == pl.num_programs(0) - 1)
    def _():
        logits = acc[...] * lax.rsqrt(squares[...] / (width * NZ * NC) + EPS)
        lanes = lax.broadcasted_iota(jnp.int32, logits.shape, 1)
        top = jnp.max(logits, axis=1, keepdims=True)
        summed = jnp.sum(jnp.exp(logits - top), axis=1, keepdims=True)
        local = token[...] - place[2] * logits.shape[1]
        chosen = jnp.sum(jnp.where(lanes == local, logits, 0.0), axis=1, keepdims=True)
        stats[...] = jnp.where(lanes == 0, top, jnp.where(lanes == 1, summed, chosen))


def head(place, own, other, w_vocab, gain, token):
    _, _, rows, width = own.shape
    total = NXY * rows
    vocab = w_vocab.shape[1]

    def at(s, p):
        flip = s // NZ
        return (p[1] + flip - 2 * p[1] * flip) * NZ + s % NZ

    return pl.pallas_call(
        head_kernel,
        out_shape=jax.ShapeDtypeStruct((total, vocab), F32),
        grid_spec=pltpu.PrefetchScalarGridSpec(
            num_scalar_prefetch=1,
            grid=(NC * NZ,),
            in_specs=[
                pl.BlockSpec(
                    (NXY, 1, rows, width), lambda s, p: (0, jnp.minimum(s, NZ - 1), 0, 0)
                ),
                pl.BlockSpec(
                    (NXY, 1, rows, width), lambda s, p: (0, jnp.maximum(s - NZ, 0), 0, 0)
                ),
                pl.BlockSpec((width, vocab), lambda s, p: (at(s, p), 0)),
                pl.BlockSpec((1, 1, width), lambda s, p: (at(s, p), 0, 0)),
                pl.BlockSpec((total, 1), lambda s, p: (0, 0)),
            ],
            out_specs=pl.BlockSpec((total, vocab), lambda s, p: (0, 0)),
            scratch_shapes=[pltpu.VMEM((total, vocab), F32), pltpu.VMEM((total, 1), F32)],
        ),
        compiler_params=pltpu.CompilerParams(
            dimension_semantics=("arbitrary",), vmem_limit_bytes=48 << 20
        ),
        cost_estimate=pl.CostEstimate(
            flops=2 * total * width * NZ * NC * vocab,
            bytes_accessed=8 << 20,
            transcendentals=total * vocab,
        ),
        name="head",
    )(place, own, other, w_vocab, gain, token)


def shards(
    queries,
    new_keys,
    new_values,
    k_cache,
    v_cache,
    lengths,
    residual,
    w_out,
    router,
    gain_moe,
    w_gate,
    w_up,
    w_down,
    expert_ids,
    gain_final,
    w_vocab,
    tokens,
    mu,
):
    x, z, y, core = (lax.axis_index(name) for name in ("x", "z", "y", "c"))
    expert = y * NC + core
    owner = lax.axis_index(ALL)
    place = jnp.stack([expert, core, owner]).astype(jnp.int32)
    width_all = gain_moe.shape[0]
    unit = w_out.shape[1]
    total_rows = residual.shape[0]
    part_rows = total_rows // (NX * NY * NC)

    packs = []
    for shift in range(NX):
        target = (x + shift) % NX
        rows = lax.dynamic_slice_in_dim(
            residual, (target * NY * NC + expert) * part_rows, part_rows
        )
        pack = jnp.concatenate([w_out, rows], axis=0)
        if shift:
            pack = lax.ppermute(pack, "x", [(i, (i + shift) % NX) for i in range(NX)])
        packs.append(pack)
    depth = w_out.shape[0]
    w_wide = jnp.concatenate([pack[:depth] for pack in packs], axis=1)
    residual_wide = jnp.concatenate([pack[depth:] for pack in packs], axis=1)

    half = width_all // NC
    down_sent = lax.dynamic_slice_in_dim(w_down[0], (1 - core) * half, half, axis=1)
    down_other = swap_cores(down_sent)

    attended = attend(queries, new_keys, new_values, k_cache, v_cache, lengths)
    attended_x = spread(attended, "z", NZ).reshape(-1, depth)
    partial_heads = jnp.dot(attended_x, w_wide, preferred_element_type=F32).astype(BF16)
    pieces = exchange(partial_heads.reshape(NY * NC, part_rows, NX * unit), EX)
    summed = jnp.sum(pieces.astype(F32), axis=0) + residual_wide.astype(F32)
    turned = summed.astype(BF16).reshape(part_rows, NX, unit)
    hidden = jnp.concatenate(
        [lax.dynamic_index_in_dim(turned, (x - i) % NX, 1, keepdims=False) for i in range(NX)],
        axis=1,
    )

    hidden_z = spread(hidden, "z", NZ)
    own = spread(hidden_z, XY, NXY)
    other = swap_cores(own)

    order = expert_ids.reshape(NXY, NC, part_rows, 2).transpose(1, 0, 2, 3)
    order = jnp.where(core == 0, order, order[::-1]).reshape(total_rows, 2)
    router_z = router.T.reshape(-1, NX, NZ, unit).transpose(2, 0, 1, 3).reshape(NZ, -1, NX * unit)
    gain_z = gain_moe.reshape(NX, NZ, unit).transpose(1, 0, 2).reshape(NZ, 1, NX * unit)
    act = experts(place, own, other, w_gate[0], w_up[0], router_z, gain_z, order)
    act_other = swap_cores(act)
    sent = down(place, act, act_other, w_down[0], down_other)
    sums = jnp.sum(exchange(sent, XY).astype(F32), axis=0).astype(BF16)
    sums = jnp.sum(exchange(sums, "z").astype(F32), axis=0)

    block_rows = NC * part_rows
    block = half // NZ
    place_xy = x * NY + y
    mine = lax.dynamic_index_in_dim(own, place_xy, 0, keepdims=False)
    theirs = lax.dynamic_index_in_dim(other, place_xy, 0, keepdims=False)
    rows_here = jnp.where(
        core == 0,
        jnp.concatenate([mine, theirs], axis=1),
        jnp.concatenate([theirs, mine], axis=1),
    )
    first_unit = core * (half // unit) + z * (block // unit)
    cut = []
    for i in range(block // unit):
        at = first_unit + i
        slab = lax.dynamic_index_in_dim(rows_here, at % NZ, 0, keepdims=False)
        slab = slab.reshape(block_rows, NX, unit)
        cut.append(lax.dynamic_index_in_dim(slab, at // NZ, 1, keepdims=False))
    hidden_here = jnp.concatenate(cut, axis=1).astype(F32)
    moved = (hidden_here + sums).astype(BF16)

    final_own = spread(spread(moved, "z", NZ), XY, NXY)
    final_other = swap_cores(final_own)
    stats = head(
        place,
        final_own,
        final_other,
        w_vocab,
        gain_final.reshape(NC * NZ, 1, block),
        tokens[:, None],
    )
    own_rows = total_rows // (NX * NZ * NY * NC)
    low = (z % 2) * part_rows + expert * own_rows
    start = (x * NY + z // 2, 0, low, 0)
    size = (1, NZ, own_rows, block)
    near = lax.dynamic_slice(final_own, start, size)[0].transpose(1, 0, 2).reshape(own_rows, half)
    far = lax.dynamic_slice(final_other, start, size)[0].transpose(1, 0, 2).reshape(own_rows, half)
    hidden_out = jnp.where(
        core == 0,
        jnp.concatenate([near, far], axis=1),
        jnp.concatenate([far, near], axis=1),
    )

    flat = stats[:, :4].reshape(-1, own_rows * 4)
    flat = jnp.pad(flat, ((0, 0), (0, 128 - own_rows * 4)))
    got = exchange(flat, ALL)[:, : own_rows * 4].reshape(-1, own_rows, 4)
    top = jnp.max(got[:, :, 0], axis=0)
    summed_all = jnp.sum(got[:, :, 1] * jnp.exp(got[:, :, 0] - top[None]), axis=0)
    chosen = jnp.sum(got[:, :, 2], axis=0)
    surprise = (top + jnp.log(summed_all) - chosen) / LOG_TWO
    mu_next = mu - RATE * (surprise - TARGET)
    return (hidden_out, surprise, mu_next)


def solution(mesh):
    fine = Mesh(mesh.devices.reshape(NX, NZ, NY, NC), ALL)
    dp = ("x", "z")
    return jax.shard_map(
        shards,
        mesh=fine,
        in_specs=(
            P(dp, EX),
            P(dp, EX),
            P(dp, EX),
            P(dp, EX, None, None),
            P(dp, EX, None, None),
            P(dp),
            P(None, dp),
            P(EX, dp),
            P(),
            P(),
            P(EX, None, dp),
            P(EX, None, dp),
            P(EX, dp, None),
            P(),
            P(),
            P(None, ALL),
            P(),
            P(ALL),
        ),
        out_specs=(P(ALL, None), P(ALL), P(ALL)),
        check_vma=False,
    )
```

time: 759 us -> 293 us (0.39)
  blocking collectives: 347 us -> 109 us
  waiting for transfers between devices: 267 us -> 80.9 us
  local copies, waits for them, and re-layouts: 79.5 us -> 14.6 us
  starting transfers between devices: 0.12 us -> 45.1 us
  Pallas kernels: 0 us -> 30.6 us
  matrix products: 24.3 us -> 4.17 us
  other arithmetic: 24.9 us -> 5.4 us
  between operations: 14.2 us -> 1.32 us
    all_gather x2 -> x0, waiting for transfers between devices: 194 us -> none  [the longest x1 112 us: shards(): lax.all_gather(final, ('dp', 'expert'), axis=0, tiled=True)]
    unnamed x1 -> x0, blocking collectives: 157 us -> none
    all_to_all x0 -> x4, blocking collectives: none -> 109 us  [exchange(): return lax.all_to_all(value, axes, split_axis=0, concat_axis=0, tiled=True)]
    pmax x1 -> x0, blocking collectives: 75.3 us -> none  [shards(): top = lax.pmax(jnp.max(logits, axis=1), ('dp', 'expert'))]
    psum x1 -> x0, blocking collectives: 72.8 us -> none  [shards(): lax.psum((jnp.sum(jnp.exp(logits - top[:, None]), axis=1), jnp.where(insi...]
    psum x1 -> x0, waiting for transfers between devices: 72.6 us -> none  [shards(): summed_heads = lax.psum(partial_heads, 'expert')]
    all_to_all x0 -> x5, waiting for transfers between devices: none -> 68.6 us  [exchange(): return lax.all_to_all(value, axes, split_axis=0, concat_axis=0, tiled=True)]
    gather x8 -> x0, local copies, waits for them, and re-layouts: 51 us -> none  [the longest x2 28 us: shards(): term = jnp.take(slot_out, row_slot, axis=0) * hits_here[:, None]]
  transfers between devices with their start and end apart: 3 -> 12, of which waited for: 3 -> 9; matrix products, arithmetic and copies ran while one was open for 1% -> 4% of each run, Pallas kernels for 0% -> 4%
where the time goes in v1:
time: 293 us; the launch traced here: 291 us
  blocking collectives  109 us (37%)
  waiting for transfers between devices  80.9 us (28%)
  starting transfers between devices  45.1 us (15%)
  Pallas kernels  30.6 us (10%)
  local copies, waits for them, and re-layouts  14.6 us (5%)
  other arithmetic  5.4 us (2%)
  matrix products  4.17 us (1%)
    all_to_all x4, blocking collectives, exchange(): return lax.all_to_all(value, axes, split_axis=0, concat_axis=0, tiled=True)  109 us
    all_to_all x5, waiting for transfers between devices, exchange(): return lax.all_to_all(value, axes, split_axis=0, concat_axis=0, tiled=True)  68.6 us
    all_to_all x5, starting transfers between devices, exchange(): return lax.all_to_all(value, axes, split_axis=0, concat_axis=0, tiled=True)  28.8 us
    pallas_call x1, Pallas kernels, head(): pl.pallas_call(head_kernel, out_shape=jax.ShapeDtypeStruct((total, vocab)...  12.2 us
    pallas_call x1, Pallas kernels, experts(): pl.pallas_call(expert_kernel, out_shape=jax.ShapeDtypeStruct((total, hidd...  11.6 us
    ppermute x4, starting transfers between devices, swap_cores(): return lax.ppermute(value, 'c', [(0, 1), (1, 0)])  10.5 us
    ppermute x4, waiting for transfers between devices, swap_cores(): return lax.ppermute(value, 'c', [(0, 1), (1, 0)])  7.56 us
    pallas_call x1, Pallas kernels, down(): pl.pallas_call(down_kernel, out_shape=jax.ShapeDtypeStruct((NXY, NZ, rows...  6.79 us
  transfers between devices with their start and end apart: 12, of which 9 were waited for; matrix products, arithmetic and copies ran while one was open for 4% of the time, Pallas kernels for 4%

profile of v1, /device:TPU:1, one launch (start us, length us, event | category | flops | bytes accessed | tf_op | source)
XLA Modules:
  0.0 291.4 jit_solution(4204520515071984833)
XLA Ops:
  0.8 1.1 constant_dynamic-slice_fusion.10
  2.1 1.2 copy.137
  3.3 2.1 collective-permute-start
  5.5 2.5 collective-permute-start.1
  7.9 1.2 collective-permute-start.2
  9.3 0.5 fusion.26
  10.0 1.4 fusion.12
  11.4 0.7 broadcast_in_dim.26
  12.1 8.2 %all-to-all-start = ((bf16[8,16,768]{2,1,0:T(8,128)(2,1)}), bf16[8,16,768]{2,1,0:T(8,128)(2,1)}, u32[]{:S(2)}, u32[]{:S(2)}) async-start(bf16[8,16,768]{2,1,0:T(8,128)(2,1)} %broadcast_in_dim.26), calls=%async_computation | async-start | bytes 393216 | tf_op jit(solution)/shard_map/all_to_all | solution.py:27
  20.5 4.7 %collective-permute-done.1 = bf16[784,192]{1,0:T(8,128)(2,1)S(1)} collective-permute-done((bf16[784,192]{1,0:T(8,128)(2,1)S(1)}, bf16[784,192]{1,0:T(8,128)(2,1)S(1)}, u32[]{:S(2)}, u32[]{:S(2)}) %collective-permute-start.1) | collective-permute-done | bytes 301088 | tf_op jit(solution)/shard_map/ppermute | solution.py:315
  25.3 3.8 %all-to-all-done = bf16[8,16,768]{2,1,0:T(8,128)(2,1)} async-done(((bf16[8,16,768]{2,1,0:T(8,128)(2,1)}), bf16[8,16,768]{2,1,0:T(8,128)(2,1)}, u32[]{:S(2)}, u32[]{:S(2)}) %all-to-all-start) | async-done | bytes 196640 | tf_op jit(solution)/shard_map/all_to_all | solution.py:27
  29.1 2.2 fusion.8
  31.3 7.3 %all-to-all-start.1 = ((bf16[8,16,768]{2,1,0:T(8,128)(2,1)}), bf16[8,16,768]{2,1,0:T(8,128)(2,1)S(1)}, u32[]{:S(2)}, u32[]{:S(2)}) async-start(bf16[8,16,768]{2,1,0:T(8,128)(2,1)} %bitcast.6), calls=%async_computation.1 | async-start | bytes 393216 | tf_op jit(solution)/shard_map/all_to_all | solution.py:27
  38.7 5.9 %all-to-all-done.1 = bf16[8,16,768]{2,1,0:T(8,128)(2,1)S(1)} async-done(((bf16[8,16,768]{2,1,0:T(8,128)(2,1)}), bf16[8,16,768]{2,1,0:T(8,128)(2,1)S(1)}, u32[]{:S(2)}, u32[]{:S(2)}) %all-to-all-start.1) | async-done | bytes 196640 | tf_op jit(solution)/shard_map/all_to_all | solution.py:27
  45.0 11.4 %all_to_all.52 = bf16[8,16,768]{2,1,0:T(8,128)(2,1)S(1)} all-to-all(bf16[8,16,768]{2,1,0:T(8,128)(2,1)S(1)} %broadcast_in_dim.27), channel_id=1, replica_groups=mesh['x'=4,'z'=8,'y'=4,'c'=2] {'z'}, dimensions={0} | all-to-all | bytes 393216 | tf_op jit(solution)/shard_map/all_to_all | solution.py:27
  56.4 0.3 broadcast_in_dim.28
  56.7 39.7 %all_to_all.53.own = bf16[16,8,16,768]{3,2,1,0:T(8,128)(2,1)} all-to-all(bf16[16,8,16,768]{3,2,1,0:T(8,128)(2,1)S(1)} %broadcast_in_dim.28), channel_id=1, replica_groups=mesh['x'=4,'z'=8,'y'=4,'c'=2] {'x','y'}, dimensions={0} | all-to-all | bytes 6291456 | tf_op jit(solution)/shard_map/all_to_all | solution.py:27
  96.5 5.0 %collective-permute-start.3 = (bf16[16,8,16,768]{3,2,1,0:T(8,128)(2,1)}, bf16[16,8,16,768]{3,2,1,0:T(8,128)(2,1)}, u32[]{:S(2)}, u32[]{:S(2)}) collective-permute-start(bf16[16,8,16,768]{3,2,1,0:T(8,128)(2,1)} %all_to_all.53.own), channel_id=1, source_target_pairs={{0,1},{1,0},{2,3},{3,2},{4,5},{5,4},{6,7},{7,6},{8,9},{9,8},{10,11... | collective-permute-start | bytes 9437192 | tf_op jit(solution)/shard_map/ppermute | solution.py:23
  101.5 2.7 dynamic-slice_bitcast_fusion
  104.3 0.3 copy.145
  104.6 0.2 reshape.181
  105.3 1.8 collective-permute-done.3.other
  107.1 11.6 %experts.1.mine = bf16[512,256]{1,0:T(8,128)(2,1)S(1)} custom-call(s32[3]{0:T(128)S(1)} %pad_add_fusion.place, bf16[16,8,16,768]{3,2,1,0:T(8,128)(2,1)} %all_to_all.53.own, bf16[16,8,16,768]{3,2,1,0:T(8,128)(2,1)} %collective-permute-done.3.other, bf16[4,8,192,256]{3,2,1,0:T(8,128)(2,1)} %bitcast.102, bf16[4,8,192,256]{3,2,1,0:T(8,128)(2,1)} %bitcast.103, ...), custom_call_target="tpu_custom_call" | custom-call | flops 3221225472 | bytes 13631488 | tf_op jit(solution)/shard_map/experts/pallas_call | solution.py:116
  118.6 0.5 collective-permute-start.4
  119.1 1.2 collective-permute-done.4.theirs
  120.3 6.8 %down.1 = bf16[16,8,32,384]{3,2,1,0:T(8,128)(2,1)S(1)} custom-call(s32[3]{0:T(128)S(1)} %pad_add_fusion.place, bf16[512,256]{1,0:T(8,128)(2,1)S(1)} %experts.1.mine, bf16[512,256]{1,0:T(8,128)(2,1)S(1)} %collective-permute-done.4.theirs, bf16[256,6144]{1,0:T(8,128)(2,1)} %bitcast.101, bf16[256,3072]{1,0:T(8,128)(2,1)S(1)} %collective-permute-done.5.w_theirs), custom_call_target="tpu_custom_call" | custom-call | flops 1610612736 | bytes 7340032 | tf_op jit(solution)/shard_map/down/pallas_call | solution.py:178
  127.1 1.7 copy-done.1
  128.7 4.5 %all-to-all-start.4 = ((bf16[16,8,32,384]{3,2,1,0:T(8,128)(2,1)}), bf16[16,8,32,384]{3,2,1,0:T(8,128)(2,1)}, u32[]{:S(2)}, u32[]{:S(2)}) async-start(bf16[16,8,32,384]{3,2,1,0:T(8,128)(2,1)} %copy-done.1), calls=%async_computation.4 | async-start | bytes 6291456 | tf_op jit(solution)/shard_map/all_to_all | solution.py:27
  133.3 0.9 dynamic-slice_bitcast_fusion.2
  134.2 0.9 dynamic-slice_bitcast_fusion.1
  135.2 39.4 %all-to-all-done.4 = bf16[16,8,32,384]{3,2,1,0:T(8,128)(2,1)} async-done(((bf16[16,8,32,384]{3,2,1,0:T(8,128)(2,1)}), bf16[16,8,32,384]{3,2,1,0:T(8,128)(2,1)}, u32[]{:S(2)}, u32[]{:S(2)}) %all-to-all-start.4) | async-done | bytes 3145760 | tf_op jit(solution)/shard_map/all_to_all | solution.py:27
  174.6 3.1 %reduce_sum.62 = bf16[8,32,384]{2,1,0:T(8,128)(2,1)} reduce(bf16[16,8,32,384]{3,2,1,0:T(8,128)(2,1)} %all-to-all-done.4, bf16[]{:T(256)} %constant.173.clone.1), dimensions={0}, to_apply=%region_3.4 | reduce | flops 1474560 | bytes 3342338 | tf_op jit(solution)/shard_map/reduce_sum | solution.py:347
  177.7 3.4 %all-to-all-start.5 = ((bf16[8,32,384]{2,1,0:T(8,128)(2,1)}), bf16[8,32,384]{2,1,0:T(8,128)(2,1)S(1)}, u32[]{:S(2)}, u32[]{:S(2)}) async-start(bf16[8,32,384]{2,1,0:T(8,128)(2,1)} %reduce_sum.62), calls=%async_computation.5 | async-start | bytes 393216 | tf_op jit(solution)/shard_map/all_to_all | solution.py:27
  181.5 8.1 %all-to-all-done.5 = bf16[8,32,384]{2,1,0:T(8,128)(2,1)S(1)} async-done(((bf16[8,32,384]{2,1,0:T(8,128)(2,1)}), bf16[8,32,384]{2,1,0:T(8,128)(2,1)S(1)}, u32[]{:S(2)}, u32[]{:S(2)}) %all-to-all-start.5) | async-done | bytes 196640 | tf_op jit(solution)/shard_map/all_to_all | solution.py:27
  189.8 11.1 %all_to_all.54 = bf16[8,32,384]{2,1,0:T(8,128)(2,1)S(1)} all-to-all(bf16[8,32,384]{2,1,0:T(8,128)(2,1)S(1)} %broadcast_in_dim.29), channel_id=1, replica_groups=mesh['x'=4,'z'=8,'y'=4,'c'=2] {'z'}, dimensions={0} | all-to-all | bytes 393216 | tf_op jit(solution)/shard_map/all_to_all | solution.py:27
  200.9 0.4 broadcast_in_dim.30
  201.4 47.1 %all_to_all.55.own = bf16[16,8,32,384]{3,2,1,0:T(8,128)(2,1)} all-to-all(bf16[16,8,32,384]{3,2,1,0:T(8,128)(2,1)S(1)} %broadcast_in_dim.30), channel_id=1, replica_groups=mesh['x'=4,'z'=8,'y'=4,'c'=2] {'x','y'}, dimensions={0} | all-to-all | bytes 6291456 | tf_op jit(solution)/shard_map/all_to_all | solution.py:27
  248.4 5.0 %collective-permute-start.6 = (bf16[16,8,32,384]{3,2,1,0:T(8,128)(2,1)}, bf16[16,8,32,384]{3,2,1,0:T(8,128)(2,1)}, u32[]{:S(2)}, u32[]{:S(2)}) collective-permute-start(bf16[16,8,32,384]{3,2,1,0:T(8,128)(2,1)} %all_to_all.55.own), channel_id=1, source_target_pairs={{0,1},{1,0},{2,3},{3,2},{4,5},{5,4},{6,7},{7,6},{8,9},{9,8},{10,11... | collective-permute-start | bytes 9437192 | tf_op jit(solution)/shard_map/ppermute | solution.py:23
  253.6 0.8 constant_dynamic-slice_fusion.1
  254.5 4.6 %collective-permute-done.6.other = bf16[16,8,32,384]{3,2,1,0:T(8,128)(2,1)} collective-permute-done((bf16[16,8,32,384]{3,2,1,0:T(8,128)(2,1)}, bf16[16,8,32,384]{3,2,1,0:T(8,128)(2,1)}, u32[]{:S(2)}, u32[]{:S(2)}) %collective-permute-start.6) | collective-permute-done | bytes 3145760 | tf_op jit(solution)/shard_map/ppermute | solution.py:23
  259.1 12.2 %head.1 = f32[512,128]{1,0:T(8,128)S(1)} custom-call(s32[3]{0:T(128)S(1)} %pad_add_fusion.place, bf16[16,8,32,384]{3,2,1,0:T(8,128)(2,1)} %all_to_all.55.own, bf16[16,8,32,384]{3,2,1,0:T(8,128)(2,1)} %collective-permute-done.6.other, bf16[6144,128]{1,0:T(8,128)(2,1)S(1)} %copy-done.2, f32[16,1,384]{2,1,0:T(1,128)S(1)} %bitcast.100, s32[512,1]{1,0:T(8,128)S(1)} %copy.148.token), custom_call_target="tpu_custom_call" | custom-call | flops 805306368 | bytes 8388608 | tf_op jit(solution)/shard_map/head/pallas_call | solution.py:246
  271.4 0.7 pad.4
  272.1 5.4 %all-to-all-start.8 = ((f32[256,1,128]{2,1,0:T(1,128)}), f32[256,1,128]{2,1,0:T(1,128)S(1)}, u32[]{:S(2)}, u32[]{:S(2)}) async-start(f32[256,1,128]{2,1,0:T(1,128)} %bitcast.32), calls=%async_computation.8 | async-start | bytes 262144 | tf_op jit(solution)/shard_map/all_to_all | solution.py:27
  277.5 0.8 constant_dynamic-slice_fusion
  278.4 0.6 broadcast_select_fusion
  279.0 11.5 %all-to-all-done.8 = f32[256,1,128]{2,1,0:T(1,128)S(1)} async-done(((f32[256,1,128]{2,1,0:T(1,128)}), f32[256,1,128]{2,1,0:T(1,128)S(1)}, u32[]{:S(2)}, u32[]{:S(2)}) %all-to-all-start.8) | async-done | bytes 131104 | tf_op jit(solution)/shard_map/all_to_all | solution.py:27
  290.7 0.2 fusion.24
  290.9 0.5 multiply_subtract_fusion
  (88 shorter events, 3.2 us)
Async XLA Ops:
  0.6 8.7 %copy-start = (bf16[16,1,128,128]{3,2,1,0:T(8,128)(2,1)S(1)}, bf16[16,1,128,128]{3,2,1,0:T(8,128)(2,1)}, u32[]{:S(2)}) copy-start(bf16[16,1,128,128]{3,2,1,0:T(8,128)(2,1)} %param.21) | copy-start | bytes 1572868
  0.6 8.4 %copy-start.5 = (bf16[16,768]{1,0:T(8,128)(2,1)S(1)}, bf16[16,768]{1,0:T(8,128)(2,1)}, u32[]{:S(2)}) copy-start(bf16[16,768]{1,0:T(8,128)(2,1)} %param.18) | copy-start | bytes 73732
  0.7 8.5 %copy-start.10 = (s32[16]{0:T(128)S(1)}, s32[16]{0:T(128)}, u32[]{:S(2)}) copy-start(s32[16]{0:T(128)} %param.23) | copy-start | bytes 196
  0.7 8.5 %copy-start.12 = (bf16[16,128]{1,0:T(8,128)(2,1)S(1)}, bf16[16,128]{1,0:T(8,128)(2,1)}, u32[]{:S(2)}) copy-start(bf16[16,128]{1,0:T(8,128)(2,1)} %param.19) | copy-start | bytes 12292
  0.7 9.3 %copy-start.7 = (bf16[16,128]{1,0:T(8,128)(2,1)S(1)}, bf16[16,128]{1,0:T(8,128)(2,1)}, u32[]{:S(2)}) copy-start(bf16[16,128]{1,0:T(8,128)(2,1)} %param.20) | copy-start | bytes 12292
  3.3 17.1 %collective-permute-start = (bf16[784,192]{1,0:T(8,128)(2,1)S(1)}, bf16[784,192]{1,0:T(8,128)(2,1)S(1)}, u32[]{:S(2)}, u32[]{:S(2)}) collective-permute-start(bf16[784,192]{1,0:T(8,128)(2,1)S(1)} %get-tuple-element.9), channel_id=1, source_target_pairs={{0,64},{64,128},{128,192},{192,0},{1,65},{65,129},{129,193},{193,1... | collective-permute-start | bytes 903176 | tf_op jit(solution)/shard_map/ppermute | solution.py:315
  5.5 19.7 %collective-permute-start.1 = (bf16[784,192]{1,0:T(8,128)(2,1)S(1)}, bf16[784,192]{1,0:T(8,128)(2,1)S(1)}, u32[]{:S(2)}, u32[]{:S(2)}) collective-permute-start(bf16[784,192]{1,0:T(8,128)(2,1)S(1)} %get-tuple-element.10), channel_id=1, source_target_pairs={{0,128},{64,192},{128,0},{192,64},{1,129},{65,193},{129,1},{193,65... | collective-permute-start | bytes 903176 | tf_op jit(solution)/shard_map/ppermute | solution.py:315
  7.9 17.4 %collective-permute-start.2 = (bf16[784,192]{1,0:T(8,128)(2,1)S(1)}, bf16[784,192]{1,0:T(8,128)(2,1)S(1)}, u32[]{:S(2)}, u32[]{:S(2)}) collective-permute-start(bf16[784,192]{1,0:T(8,128)(2,1)S(1)} %get-tuple-element.11), channel_id=1, source_target_pairs={{0,192},{64,0},{128,64},{192,128},{1,193},{65,1},{129,65},{193,129... | collective-permute-start | bytes 903176 | tf_op jit(solution)/shard_map/ppermute | solution.py:315
  12.1 17.0 %all-to-all-start = ((bf16[8,16,768]{2,1,0:T(8,128)(2,1)}), bf16[8,16,768]{2,1,0:T(8,128)(2,1)}, u32[]{:S(2)}, u32[]{:S(2)}) async-start(bf16[8,16,768]{2,1,0:T(8,128)(2,1)} %broadcast_in_dim.26), calls=%async_computation | async-start | bytes 393216 | tf_op jit(solution)/shard_map/all_to_all | solution.py:27
  31.3 13.2 %all-to-all-start.1 = ((bf16[8,16,768]{2,1,0:T(8,128)(2,1)}), bf16[8,16,768]{2,1,0:T(8,128)(2,1)S(1)}, u32[]{:S(2)}, u32[]{:S(2)}) async-start(bf16[8,16,768]{2,1,0:T(8,128)(2,1)} %bitcast.6), calls=%async_computation.1 | async-start | bytes 393216 | tf_op jit(solution)/shard_map/all_to_all | solution.py:27
  96.5 7.7 %copy-start.8 = (s32[512,2]{0,1:T(2,128)S(1)}, s32[512,2]{0,1:T(2,128)}, u32[]{:S(2)}) copy-start(s32[512,2]{0,1:T(2,128)} %param.31) | copy-start | bytes 12292
  96.5 8.1 %copy-start.4 = (bf16[6144,8]{0,1:T(8,128)(2,1)S(1)}, bf16[6144,8]{0,1:T(8,128)(2,1)}, u32[]{:S(2)}) copy-start(bf16[6144,8]{0,1:T(8,128)(2,1)} %param.26) | copy-start | bytes 294916
  96.5 8.5 %copy-start.6 = (f32[6144]{0:T(1024)S(1)}, f32[6144]{0:T(1024)}, u32[]{:S(2)}) copy-start(f32[6144]{0:T(1024)} %param.27) | copy-start | bytes 73732
  96.5 10.6 %collective-permute-start.3 = (bf16[16,8,16,768]{3,2,1,0:T(8,128)(2,1)}, bf16[16,8,16,768]{3,2,1,0:T(8,128)(2,1)}, u32[]{:S(2)}, u32[]{:S(2)}) collective-permute-start(bf16[16,8,16,768]{3,2,1,0:T(8,128)(2,1)} %all_to_all.53.own), channel_id=1, source_target_pairs={{0,1},{1,0},{2,3},{3,2},{4,5},{5,4},{6,7},{7,6},{8,9},{9,8},{10,11... | collective-permute-start | bytes 9437192 | tf_op jit(solution)/shard_map/ppermute | solution.py:23
  104.1 15.0 %collective-permute-start.5 = (bf16[256,3072]{1,0:T(8,128)(2,1)}, bf16[256,3072]{1,0:T(8,128)(2,1)S(1)}, u32[]{:S(2)}, u32[]{:S(2)}) collective-permute-start(bf16[256,3072]{1,0:T(8,128)(2,1)} %dynamic-slice_bitcast_fusion), channel_id=1, source_target_pairs={{0,1},{1,0},{2,3},{3,2},{4,5},{5,4},{6,7},{7,6},{8,9},{9,8},{10,11... | collective-permute-start | bytes 4718600 | tf_op jit(solution)/shard_map/ppermute | solution.py:23
  118.6 1.6 collective-permute-start.4
  127.1 1.7 copy-start.1
  128.7 45.9 %all-to-all-start.4 = ((bf16[16,8,32,384]{3,2,1,0:T(8,128)(2,1)}), bf16[16,8,32,384]{3,2,1,0:T(8,128)(2,1)}, u32[]{:S(2)}, u32[]{:S(2)}) async-start(bf16[16,8,32,384]{3,2,1,0:T(8,128)(2,1)} %copy-done.1), calls=%async_computation.4 | async-start | bytes 6291456 | tf_op jit(solution)/shard_map/all_to_all | solution.py:27
  177.7 12.0 %all-to-all-start.5 = ((bf16[8,32,384]{2,1,0:T(8,128)(2,1)}), bf16[8,32,384]{2,1,0:T(8,128)(2,1)S(1)}, u32[]{:S(2)}, u32[]{:S(2)}) async-start(bf16[8,32,384]{2,1,0:T(8,128)(2,1)} %reduce_sum.62), calls=%async_computation.5 | async-start | bytes 393216 | tf_op jit(solution)/shard_map/all_to_all | solution.py:27
  201.3 52.1 %copy-start.9 = (s32[512]{0:T(512)S(1)}, s32[512]{0:T(512)}, u32[]{:S(2)}) copy-start(s32[512]{0:T(512)} %param.34) | copy-start | bytes 6148
  201.3 57.7 %copy-start.2 = (bf16[6144,128]{1,0:T(8,128)(2,1)S(1)}, bf16[6144,128]{1,0:T(8,128)(2,1)}, u32[]{:S(2)}) copy-start(bf16[6144,128]{1,0:T(8,128)(2,1)} %weights.1) | copy-start | bytes 4718596
  201.3 57.7 %copy-start.3 = (f32[6144]{0:T(1024)S(1)}, f32[6144]{0:T(1024)}, u32[]{:S(2)}) copy-start(f32[6144]{0:T(1024)} %param.32) | copy-start | bytes 73732
  248.4 10.6 %collective-permute-start.6 = (bf16[16,8,32,384]{3,2,1,0:T(8,128)(2,1)}, bf16[16,8,32,384]{3,2,1,0:T(8,128)(2,1)}, u32[]{:S(2)}, u32[]{:S(2)}) collective-permute-start(bf16[16,8,32,384]{3,2,1,0:T(8,128)(2,1)} %all_to_all.55.own), channel_id=1, source_target_pairs={{0,1},{1,0},{2,3},{3,2},{4,5},{5,4},{6,7},{7,6},{8,9},{9,8},{10,11... | collective-permute-start | bytes 9437192 | tf_op jit(solution)/shard_map/ppermute | solution.py:23
  259.1 31.8 %copy-start.11 = (f32[2]{0:T(128)S(1)}, f32[2]{0:T(128)}, u32[]{:S(2)}) copy-start(f32[2]{0:T(128)} %param.35) | copy-start | bytes 28
  272.1 18.4 %all-to-all-start.8 = ((f32[256,1,128]{2,1,0:T(1,128)}), f32[256,1,128]{2,1,0:T(1,128)S(1)}, u32[]{:S(2)}, u32[]{:S(2)}) async-start(f32[256,1,128]{2,1,0:T(1,128)} %bitcast.32), calls=%async_computation.8 | async-start | bytes 262144 | tf_op jit(solution)/shard_map/all_to_all | solution.py:27

commit v2 on v1

v2 whole, which is shorter than its diff:
```python
import jax
import jax.numpy as jnp
from jax import lax
from jax.experimental import pallas as pl
from jax.experimental.pallas import tpu as pltpu
from jax.sharding import Mesh
from jax.sharding import PartitionSpec as P

EPS = 1e-05
TARGET = 5.0
RATE = 0.1
LOG_TWO = 0.6931471805599453
F32 = jnp.float32
BF16 = jnp.bfloat16
NX, NZ, NY, NC = 4, 8, 4, 2
NXY = NX * NY
XY = ("x", "y")
EX = ("y", "c")
ALL = ("x", "z", "y", "c")


def swap_cores(value):
    return lax.ppermute(value, "c", [(0, 1), (1, 0)])


def exchange(value, axes):
    return lax.all_to_all(value, axes, split_axis=0, concat_axis=0, tiled=True)


def spread(value, axes, count):
    return exchange(jnp.broadcast_to(value[None], (count,) + value.shape), axes)


def attend(queries, new_keys, new_values, k_cache, v_cache, lengths):
    rows, heads_kv, span, width = k_cache.shape
    group = queries.shape[1] // (heads_kv * width)
    query = queries.reshape(rows, heads_kv, group, width)
    scale = width ** (-0.5)
    cached = (
        jnp.einsum("rkgd,rkld->rkgl", query, k_cache, preferred_element_type=F32) * scale
    )
    fresh_key = new_keys.reshape(rows, heads_kv, width)
    fresh = jnp.einsum("rkgd,rkd->rkg", query, fresh_key, preferred_element_type=F32) * scale
    live = jnp.arange(span, dtype=jnp.int32)[None, :] < lengths[:, None]
    cached = jnp.where(live[:, None, None, :], cached, -1e30)
    top = jnp.maximum(jnp.max(cached, axis=-1), fresh)
    part_cached = jnp.exp(cached - top[..., None])
    part_fresh = jnp.exp(fresh - top)
    total = jnp.sum(part_cached, axis=-1) + part_fresh
    weight_cached = (part_cached / total[..., None]).astype(BF16)
    weight_fresh = (part_fresh / total).astype(BF16)
    fresh_value = new_values.reshape(rows, heads_kv, 1, width).astype(F32)
    out = jnp.einsum("rkgl,rkld->rkgd", weight_cached, v_cache, preferred_element_type=F32)
    out = out + weight_fresh.astype(F32)[..., None] * fresh_value
    return out.reshape(rows, group * heads_kv * width).astype(BF16)


def expert_kernel(
    place, state, gate_w, up_w, router_w, ids, act, gate_sum, up_sum, route_sum, squares
):
    step = pl.program_id(0)
    width = state.shape[-1]
    hidden = state[...].reshape(-1, width)
    gate = jnp.dot(hidden, gate_w[...].reshape(width, -1), preferred_element_type=F32)
    up = jnp.dot(hidden, up_w[...].reshape(width, -1), preferred_element_type=F32)
    route = lax.dot_general(
        hidden, router_w[0], (((1,), (1,)), ((), ())), preferred_element_type=F32
    )
    wide = hidden.astype(F32)
    square = jnp.zeros(squares.shape, F32)
    for start in range(0, width, 128):
        piece = wide[:, start : start + 128]
        square += piece * piece

    @pl.when(step == 0)
    def _():
        gate_sum[...] = gate
        up_sum[...] = up
        route_sum[...] = route
        squares[...] = square

    @pl.when(step > 0)
    def _():
        gate_sum[...] += gate
        up_sum[...] += up
        route_sum[...] += route
        squares[...] += square

    @pl.when(step == pl.num_programs(0) - 1)
    def _():
        expert = place[0]
        mean = jnp.sum(squares[...], axis=1, keepdims=True) / (width * NZ)
        scale = lax.rsqrt(mean + EPS)
        logits = route_sum[...] * scale
        lanes = lax.broadcasted_iota(jnp.int32, logits.shape, 1)
        first = ids[:, 0:1]
        second = ids[:, 1:2]
        first_logit = jnp.sum(jnp.where(lanes == first, logits, 0.0), axis=1, keepdims=True)
        second_logit = jnp.sum(jnp.where(lanes == second, logits, 0.0), axis=1, keepdims=True)
        is_first = first == expert
        gap = second_logit - first_logit
        weight = 1.0 / (1.0 + jnp.exp(jnp.where(is_first, gap, -gap)))
        weight = jnp.where(is_first | (second == expert), weight, 0.0)
        gated = gate_sum[...] * scale
        value = jax.nn.silu(gated) * (up_sum[...] * scale)
        act[...] = (weight * value).astype(BF16)


def experts(place, state, gate_w, up_w, router_w, ids):
    _, _, rows, width = state.shape
    total = NXY * rows
    hidden_units = gate_w.shape[-1]
    unit = width // NX
    weights = pl.BlockSpec((NX, 1, unit, hidden_units), lambda z, p: (0, z, 0, 0))
    count = router_w.shape[1]
    return pl.pallas_call(
        expert_kernel,
        out_shape=jax.ShapeDtypeStruct((total, hidden_units), BF16),
        grid_spec=pltpu.PrefetchScalarGridSpec(
            num_scalar_prefetch=1,
            grid=(NZ,),
            in_specs=[
                pl.BlockSpec((NXY, 1, rows, width), lambda z, p: (0, z, 0, 0)),
                weights,
                weights,
                pl.BlockSpec((1, count, width), lambda z, p: (z, 0, 0)),
                pl.BlockSpec((total, 2), lambda z, p: (0, 0)),
            ],
            out_specs=pl.BlockSpec((total, hidden_units), lambda z, p: (0, 0)),
            scratch_shapes=[
                pltpu.VMEM((total, hidden_units), F32),
                pltpu.VMEM((total, hidden_units), F32),
                pltpu.VMEM((total, count), F32),
                pltpu.VMEM((total, 128), F32),
            ],
        ),
        compiler_params=pltpu.CompilerParams(
            dimension_semantics=("arbitrary",), vmem_limit_bytes=32 << 20
        ),
        cost_estimate=pl.CostEstimate(
            flops=2 * total * width * NZ * 2 * hidden_units,
            bytes_accessed=10 << 20,
            transcendentals=total * hidden_units,
        ),
        name="experts",
    )(
        place,
        state,
        gate_w.reshape(NX, NZ, unit, hidden_units),
        up_w.reshape(NX, NZ, unit, hidden_units),
        router_w,
        ids,
    )


def down_kernel(
    place, mine_own, mine_other, theirs_own, theirs_other, w_mine, w_theirs, out
):
    width = out.shape[-1]
    core = place[1]
    for mine, theirs, which in (
        (mine_own, theirs_own, core),
        (mine_other, theirs_other, 1 - core),
    ):
        total = jnp.dot(mine[...], w_mine[...], preferred_element_type=F32)
        total += jnp.dot(theirs[...], w_theirs[...], preferred_element_type=F32)
        out[0, :, pl.ds(which, 1), :, :] = total.astype(BF16).reshape(NXY, 1, -1, width)


def down(place, acts, w_mine, w_theirs):
    total, units = acts[0].shape
    rows = total // NXY
    width = w_theirs.shape[1] // NX
    steps = 2
    block = width // steps
    return pl.pallas_call(
        down_kernel,
        out_shape=jax.ShapeDtypeStruct((NX, NXY, NC, rows, width), BF16),
        grid_spec=pltpu.PrefetchScalarGridSpec(
            num_scalar_prefetch=1,
            grid=(NX, steps),
            in_specs=[pl.BlockSpec((total, units), lambda x, s, p: (0, 0))] * 4
            + [
                pl.BlockSpec((units, block), lambda x, s, p: (0, (p[1] * NX + x) * steps + s)),
                pl.BlockSpec((units, block), lambda x, s, p: (0, x * steps + s)),
            ],
            out_specs=pl.BlockSpec(
                (1, NXY, NC, rows, block), lambda x, s, p: (x, 0, 0, 0, s)
            ),
        ),
        compiler_params=pltpu.CompilerParams(
            dimension_semantics=("arbitrary", "arbitrary"), vmem_limit_bytes=32 << 20
        ),
        cost_estimate=pl.CostEstimate(
            flops=8 * total * units * width * NX, bytes_accessed=7 << 20, transcendentals=0
        ),
        name="down",
    )(place, *acts, w_mine, w_theirs)


def head_kernel(own, other, w_own, w_other, out):
    width = own.shape[-1]
    vocab = w_own.shape[1]
    rows = out.shape[1]
    near = own[...].reshape(-1, width)
    far = other[...].reshape(-1, width)
    logits = jnp.dot(near, w_own[...], preferred_element_type=F32)
    logits += jnp.dot(far, w_other[...], preferred_element_type=F32)
    square = jnp.zeros((near.shape[0], 128), F32)
    for part in (near.astype(F32), far.astype(F32)):
        for start in range(0, width, 128):
            piece = part[:, start : start + 128]
            square += piece * piece
    square = jnp.sum(square, axis=1, keepdims=True)
    high = square.astype(BF16).astype(F32)
    lanes = lax.broadcasted_iota(jnp.int32, (near.shape[0], 128), 1)
    extra = jnp.where(lanes == 0, high, jnp.where(lanes == 1, square - high, 0.0))
    count = near.shape[0] // NX
    out[:, :count, :vocab] = logits.astype(BF16).reshape(NX, count, vocab)
    out[:, :count, vocab:] = extra.astype(BF16).reshape(NX, count, 128)
    out[:, count:, :] = jnp.zeros((NX, rows - count, vocab + 128), BF16)


def head(own, other, w_own, w_other, rows):
    vocab = w_own.shape[1]
    total = own.shape[0] * own.shape[1] * own.shape[2]
    return pl.pallas_call(
        head_kernel,
        out_shape=jax.ShapeDtypeStruct((NX, rows, vocab + 128), BF16),
        compiler_params=pltpu.CompilerParams(vmem_limit_bytes=32 << 20),
        cost_estimate=pl.CostEstimate(
            flops=4 * total * own.shape[3] * vocab, bytes_accessed=4 << 20, transcendentals=0
        ),
        name="head",
    )(own, other, w_own, w_other)


def finish_kernel(place, parts, token, stats):
    count = token.shape[0]
    vocab = parts.shape[2] - 128
    total = jnp.sum(parts[:, :count, :].astype(F32), axis=0)
    square = jnp.sum(total[:, vocab:], axis=1, keepdims=True)
    logits = total[:, :vocab] * lax.rsqrt(square / place[1] + EPS)
    top = jnp.max(logits, axis=1, keepdims=True)
    summed = jnp.sum(jnp.exp(logits - top), axis=1, keepdims=True)
    slice_width = vocab // NX
    local = token[...] - place[0] * slice_width
    block = NZ * NY * NC * slice_width
    lanes = lax.broadcasted_iota(jnp.int32, logits.shape, 1)
    entry = (lanes // slice_width) * block + lanes % slice_width
    chosen = jnp.sum(jnp.where(entry == local, logits, 0.0), axis=1, keepdims=True)
    lane = lax.broadcasted_iota(jnp.int32, stats.shape, 1)
    stats[...] = jnp.where(lane == 0, top, jnp.where(lane == 1, summed, chosen))


def finish(place, parts, token):
    return pl.pallas_call(
        finish_kernel,
        out_shape=jax.ShapeDtypeStruct((token.shape[0], 128), F32),
        in_specs=[
            pl.BlockSpec(memory_space=pltpu.SMEM),
            pl.BlockSpec(memory_space=pltpu.VMEM),
            pl.BlockSpec(memory_space=pltpu.VMEM),
        ],
        compiler_params=pltpu.CompilerParams(vmem_limit_bytes=32 << 20),
        name="finish",
    )(place, parts, token)


def shards(
    queries,
    new_keys,
    new_values,
    k_cache,
    v_cache,
    lengths,
    residual,
    w_out,
    router,
    gain_moe,
    w_gate,
    w_up,
    w_down,
    expert_ids,
    gain_final,
    w_vocab,
    tokens,
    mu,
):
    x, z, y, core = (lax.axis_index(name) for name in ("x", "z", "y", "c"))
    expert = y * NC + core
    place = jnp.stack([expert, core]).astype(jnp.int32)
    width_all = gain_moe.shape[0]
    unit = w_out.shape[1]
    total_rows = residual.shape[0]
    part_rows = total_rows // (NX * NY * NC)

    packs = []
    for shift in range(NX):
        target = (x + shift) % NX
        rows = lax.dynamic_slice_in_dim(
            residual, (target * NY * NC + expert) * part_rows, part_rows
        )
        pack = jnp.concatenate([w_out, rows], axis=0)
        if shift:
            pack = lax.ppermute(pack, "x", [(i, (i + shift) % NX) for i in range(NX)])
        packs.append(pack)
    depth = w_out.shape[0]
    w_wide = jnp.concatenate([pack[:depth] for pack in packs], axis=1)
    residual_wide = jnp.concatenate([pack[depth:] for pack in packs], axis=1)

    half = width_all // NC
    slab = half // NX
    vocab_rows = w_vocab.reshape(NC, NX, slab, -1)
    vocab_parts = []
    for shift in range(NX):
        part = lax.dynamic_index_in_dim(vocab_rows, (x + shift) % NX, 1, keepdims=False)
        if shift:
            part = lax.ppermute(part, "x", [(i, (i + shift) % NX) for i in range(NX)])
        vocab_parts.append(part)
    gain_slab = gain_final.reshape(NC, NX, slab)
    gain_slab = lax.dynamic_index_in_dim(gain_slab, x, 1, keepdims=False)[:, :, None]
    columns = []
    for i in range(NX):
        away = (x - i) % NX
        part = vocab_parts[NX - 1]
        for shift in range(NX - 1):
            part = jnp.where(away == shift, vocab_parts[shift], part)
        columns.append((part.astype(F32) * gain_slab).astype(BF16))
    head_w = jnp.concatenate(columns, axis=2)
    head_own = lax.dynamic_index_in_dim(head_w, core, 0, keepdims=False)
    head_other = lax.dynamic_index_in_dim(head_w, 1 - core, 0, keepdims=False)

    down_sent = lax.dynamic_slice_in_dim(w_down[0], (1 - core) * half, half, axis=1)
    down_other = swap_cores(down_sent)

    attended = attend(queries, new_keys, new_values, k_cache, v_cache, lengths)
    attended_x = spread(attended, "z", NZ).reshape(-1, depth)
    partial_heads = jnp.dot(attended_x, w_wide, preferred_element_type=F32).astype(BF16)
    pieces = exchange(partial_heads.reshape(NY * NC, part_rows, NX * unit), EX)
    summed = jnp.sum(pieces.astype(F32), axis=0) + residual_wide.astype(F32)
    turned = summed.astype(BF16).reshape(part_rows, NX, unit)
    hidden = jnp.concatenate(
        [lax.dynamic_index_in_dim(turned, (x - i) % NX, 1, keepdims=False) for i in range(NX)],
        axis=1,
    )

    hidden_z = spread(hidden, "z", NZ)
    own = spread(hidden_z, XY, NXY)
    other = swap_cores(own)

    order = expert_ids.reshape(NXY, NC, part_rows, 2).transpose(1, 0, 2, 3)
    order = order.reshape(NC, -1, 2)
    order_own = lax.dynamic_index_in_dim(order, core, 0, keepdims=False)
    order_other = lax.dynamic_index_in_dim(order, 1 - core, 0, keepdims=False)
    gain_col = gain_moe[:, None]
    router_g = (router.astype(F32) * gain_col).astype(BF16)
    router_z = router_g.T.reshape(-1, NX, NZ, unit).transpose(2, 0, 1, 3)
    router_z = router_z.reshape(NZ, -1, NX * unit)
    gate_g = (w_gate[0].astype(F32) * gain_col).astype(BF16)
    up_g = (w_up[0].astype(F32) * gain_col).astype(BF16)
    act_own = experts(place, own, gate_g, up_g, router_z, order_own)
    act_other = experts(place, other, gate_g, up_g, router_z, order_other)
    acts = (act_own, act_other, swap_cores(act_other), swap_cores(act_own))
    sent = down(place, acts, w_down[0], down_other)
    sent = sent.reshape(NXY, NZ, part_rows, slab)
    sums = jnp.sum(exchange(sent, XY).astype(F32), axis=0).astype(BF16)
    sums = jnp.sum(exchange(sums, "z").astype(F32), axis=0)

    units = slab // unit
    first_unit = core * (half // unit) + x * units
    start = (y * NX + z // 2, first_unit % NZ, 0, 0)
    size = (1, units, part_rows, NX * unit)
    rows_here = jnp.where(
        z % 2 == core, lax.dynamic_slice(own, start, size), lax.dynamic_slice(other, start, size)
    )[0].reshape(units, part_rows, NX, unit)
    cut = lax.dynamic_index_in_dim(rows_here, first_unit // NZ, 2, keepdims=False)
    hidden_here = cut.transpose(1, 0, 2).reshape(part_rows, slab).astype(F32)
    moved = (hidden_here + sums).astype(BF16)

    final_own = spread(spread(moved, "z", NZ), "y", NY).reshape(NY, NZ, part_rows, slab)
    final_other = swap_cores(final_own)
    count = total_rows // NX
    partial = head(final_own, final_other, head_own, head_other, count + 16)

    own_rows = total_rows // (NX * NZ * NY * NC)
    size = (NX, 1, own_rows, slab)
    start = (0, z, expert * own_rows, 0)
    near = lax.dynamic_slice(final_own, start, size)
    far = lax.dynamic_slice(final_other, start, size)
    low = jnp.where(core == 0, near, far)
    high = jnp.where(core == 0, far, near)
    vocab = head_own.shape[1]
    rows_out = jnp.concatenate([low, high], axis=1).reshape(NX, -1, vocab)
    partial = lax.dynamic_update_slice(partial, rows_out, (0, count, 0))
    parts = exchange(partial, "x")
    hidden_out = parts[:, count : count + rows_out.shape[1], :vocab]
    hidden_out = hidden_out.reshape(NX, NC, own_rows, slab).transpose(2, 1, 0, 3)
    hidden_out = hidden_out.reshape(own_rows, width_all)

    token = lax.dynamic_slice_in_dim(tokens, x * count, count)[:, None]
    where = jnp.stack([z * (NY * NC) + expert, jnp.int32(width_all)]).astype(jnp.int32)
    stats = finish(where, parts, token)
    flat = stats[:, :4].reshape(-1, own_rows * 4)
    flat = jnp.pad(flat, ((0, 0), (0, 128 - own_rows * 4)))
    got = exchange(flat, ("z", "y", "c"))[:, : own_rows * 4].reshape(-1, own_rows, 4)
    top = jnp.max(got[:, :, 0], axis=0)
    summed_all = jnp.sum(got[:, :, 1] * jnp.exp(got[:, :, 0] - top[None]), axis=0)
    chosen = jnp.sum(got[:, :, 2], axis=0)
    surprise = (top + jnp.log(summed_all) - chosen) / LOG_TWO
    mu_next = mu - RATE * (surprise - TARGET)
    return (hidden_out, surprise, mu_next)


def solution(mesh):
    fine = Mesh(mesh.devices.reshape(NX, NZ, NY, NC), ALL)
    dp = ("x", "z")
    return jax.shard_map(
        shards,
        mesh=fine,
        in_specs=(
            P(dp, EX),
            P(dp, EX),
            P(dp, EX),
            P(dp, EX, None, None),
            P(dp, EX, None, None),
            P(dp),
            P(None, dp),
            P(EX, dp),
            P(),
            P(),
            P(EX, None, dp),
            P(EX, None, dp),
            P(EX, dp, None),
            P(),
            P(),
            P(None, ALL),
            P(),
            P(ALL),
        ),
        out_specs=(P(ALL, None), P(ALL), P(ALL)),
        check_vma=False,
    )
```

time: 293 us -> 282 us (0.962)
  blocking collectives: 109 us -> 61.2 us
  starting transfers between devices: 45.1 us -> 63.2 us
  waiting for transfers between devices: 80.9 us -> 94.8 us
  other arithmetic: 5.4 us -> 12.6 us
  Pallas kernels: 30.6 us -> 24.2 us
  local copies, waits for them, and re-layouts: 14.6 us -> 18.2 us
    all_to_all x4 -> x3, blocking collectives: 109 us -> 61.2 us  [exchange(): return lax.all_to_all(value, axes, split_axis=0, concat_axis=0, tiled=True)]
    all_to_all x5 -> x7, starting transfers between devices: 28.8 us -> 40.8 us  [exchange(): return lax.all_to_all(value, axes, split_axis=0, concat_axis=0, tiled=True)]
    all_to_all x5 -> x7, waiting for transfers between devices: 68.6 us -> 80.2 us  [exchange(): return lax.all_to_all(value, axes, split_axis=0, concat_axis=0, tiled=True)]
    pallas_call x2 -> x3, Pallas kernels: 19 us -> 7.88 us  [the longest x1 4.89 us: down(): pl.pallas_call(down_kernel, out_shape=jax.ShapeDtypeStruct((NX, NXY, NC,...]
    ppermute x0 -> x3, waiting for transfers between devices: none -> 10.5 us  [shards(): part = lax.ppermute(part, 'x', [(i, (i + shift) % NX) for i in range(NX)])]
    ppermute x0 -> x3, starting transfers between devices: none -> 6.45 us  [shards(): part = lax.ppermute(part, 'x', [(i, (i + shift) % NX) for i in range(NX)])]
    ppermute x4 -> x5, waiting for transfers between devices: 7.56 us -> 1.3 us  [swap_cores(): return lax.ppermute(value, 'c', [(0, 1), (1, 0)])]
    convert_element_type x0 -> x3, other arithmetic: none -> 5.29 us  [the longest x1 3.57 us: shards(): up_g = (w_up[0].astype(F32) * gain_col).astype(BF16)]
  transfers between devices with their start and end apart: 12 -> 18, of which waited for: 9 -> 10; matrix products, arithmetic and copies ran while one was open for 4% -> 7% of each run, Pallas kernels for 4% -> 6%
where the time goes in v2:
time: 282 us; the launch traced here: 280 us
  waiting for transfers between devices  94.8 us (34%)
  starting transfers between devices  63.2 us (22%)
  blocking collectives  61.2 us (22%)
  Pallas kernels  24.2 us (9%)
  local copies, waits for them, and re-layouts  18.2 us (6%)
  other arithmetic  12.6 us (4%)
  matrix products  4.82 us (2%)
    all_to_all x7, waiting for transfers between devices, exchange(): return lax.all_to_all(value, axes, split_axis=0, concat_axis=0, tiled=True)  80.2 us
    all_to_all x3, blocking collectives, exchange(): return lax.all_to_all(value, axes, split_axis=0, concat_axis=0, tiled=True)  61.2 us
    all_to_all x7, starting transfers between devices, exchange(): return lax.all_to_all(value, axes, split_axis=0, concat_axis=0, tiled=True)  40.8 us
    pallas_call x2, Pallas kernels, experts(): pl.pallas_call(expert_kernel, out_shape=jax.ShapeDtypeStruct((total, hidd...  16.3 us
    ppermute x3, waiting for transfers between devices, shards(): part = lax.ppermute(part, 'x', [(i, (i + shift) % NX) for i in range(NX)])  10.5 us
    ppermute x5, starting transfers between devices, swap_cores(): return lax.ppermute(value, 'c', [(0, 1), (1, 0)])  10.2 us
    ppermute x3, starting transfers between devices, shards(): part = lax.ppermute(part, 'x', [(i, (i + shift) % NX) for i in range(NX)])  6.45 us
    ppermute x3, starting transfers between devices, shards(): pack = lax.ppermute(pack, 'x', [(i, (i + shift) % NX) for i in range(NX)])  5.72 us
  transfers between devices with their start and end apart: 18, of which 10 were waited for; matrix products, arithmetic and copies ran while one was open for 7% of the time, Pallas kernels for 6%

profile of v2, /device:TPU:1, one launch (start us, length us, event | category | flops | bytes accessed | tf_op | source)
XLA Modules:
  0.0 280.3 jit_solution(9502837291846956443)
XLA Ops:
  0.7 1.1 constant_dynamic-slice_fusion.6
  2.0 1.2 copy.131
  3.3 2.1 collective-permute-start
  5.4 2.5 collective-permute-start.1
  7.8 1.2 collective-permute-start.2
  12.0 1.4 fusion.14
  14.1 8.2 %all-to-all-start = ((bf16[8,16,768]{2,1,0:T(8,128)(2,1)}), bf16[8,16,768]{2,1,0:T(8,128)(2,1)}, u32[]{:S(2)}, u32[]{:S(2)}) async-start(bf16[8,16,768]{2,1,0:T(8,128)(2,1)} %broadcast_in_dim.26), calls=%async_computation | async-start | bytes 393216 | tf_op jit(solution)/shard_map/all_to_all | solution.py:27
  22.5 2.7 collective-permute-done.1
  25.3 5.8 %all-to-all-done = bf16[8,16,768]{2,1,0:T(8,128)(2,1)} async-done(((bf16[8,16,768]{2,1,0:T(8,128)(2,1)}), bf16[8,16,768]{2,1,0:T(8,128)(2,1)}, u32[]{:S(2)}, u32[]{:S(2)}) %all-to-all-start) | async-done | bytes 196640 | tf_op jit(solution)/shard_map/all_to_all | solution.py:27
  31.1 2.2 fusion.10
  33.3 7.4 %all-to-all-start.1 = ((bf16[8,16,768]{2,1,0:T(8,128)(2,1)}), bf16[8,16,768]{2,1,0:T(8,128)(2,1)S(1)}, u32[]{:S(2)}, u32[]{:S(2)}) async-start(bf16[8,16,768]{2,1,0:T(8,128)(2,1)} %bitcast.6), calls=%async_computation.1 | async-start | bytes 393216 | tf_op jit(solution)/shard_map/all_to_all | solution.py:27
  40.6 5.9 %all-to-all-done.1 = bf16[8,16,768]{2,1,0:T(8,128)(2,1)S(1)} async-done(((bf16[8,16,768]{2,1,0:T(8,128)(2,1)}), bf16[8,16,768]{2,1,0:T(8,128)(2,1)S(1)}, u32[]{:S(2)}, u32[]{:S(2)}) %all-to-all-start.1) | async-done | bytes 196640 | tf_op jit(solution)/shard_map/all_to_all | solution.py:27
  47.0 11.0 %all_to_all.57 = bf16[8,16,768]{2,1,0:T(8,128)(2,1)S(1)} all-to-all(bf16[8,16,768]{2,1,0:T(8,128)(2,1)S(1)} %broadcast_in_dim.27), channel_id=1, replica_groups=mesh['x'=4,'z'=8,'y'=4,'c'=2] {'z'}, dimensions={0} | all-to-all | bytes 393216 | tf_op jit(solution)/shard_map/all_to_all | solution.py:27
  58.3 39.2 %all_to_all.58.state = bf16[16,8,16,768]{3,2,1,0:T(8,128)(2,1)} all-to-all(bf16[16,8,16,768]{3,2,1,0:T(8,128)(2,1)S(1)} %broadcast_in_dim.28), channel_id=1, replica_groups=mesh['x'=4,'z'=8,'y'=4,'c'=2] {'x','y'}, dimensions={0} | all-to-all | bytes 6291456 | tf_op jit(solution)/shard_map/all_to_all | solution.py:27
  97.5 4.7 %collective-permute-start.3 = (bf16[16,8,16,768]{3,2,1,0:T(8,128)(2,1)}, bf16[16,8,16,768]{3,2,1,0:T(8,128)(2,1)}, u32[]{:S(2)}, u32[]{:S(2)}) collective-permute-start(bf16[16,8,16,768]{3,2,1,0:T(8,128)(2,1)} %all_to_all.58.state), channel_id=1, source_target_pairs={{0,1},{1,0},{2,3},{3,2},{4,5},{5,4},{6,7},{7,6},{8,9},{9,8},{10,11... | collective-permute-start | bytes 9437192 | tf_op jit(solution)/shard_map/ppermute | solution.py:23
  102.2 2.7 dynamic-slice_bitcast_fusion
  105.9 3.6 %fusion = (bf16[4,8,192,256]{3,2,1,0:T(8,128)(2,1)S(1)}, bf16[4,8,192,256]{3,2,1,0:T(8,128)(2,1)S(1)}) fusion(bf16[4,8,192,256]{3,2,1,0:T(8,128)(2,1)} %bitcast.125, f32[4,8,192]{2,1,0:T(8,128)S(1)} %mul.159, bf16[4,8,192,256]{3,2,1,0:T(8,128)(2,1)} %bitcast.126), kind=kLoop, calls=%fused_computation.1 | loop fusion | flops 9437184 | bytes 12607488 | tf_op jit(solution)/shard_map/convert_element_type | solution.py:361
  109.5 8.0 %experts.2.mine_own = bf16[256,256]{1,0:T(8,128)(2,1)S(1)} custom-call(s32[2]{0:T(128)S(1)} %pad_add_fusion.place, bf16[16,8,16,768]{3,2,1,0:T(8,128)(2,1)} %all_to_all.58.state, bf16[4,8,192,256]{3,2,1,0:T(8,128)(2,1)S(1)} %get-tuple-element.28.gate_w, bf16[4,8,192,256]{3,2,1,0:T(8,128)(2,1)S(1)} %get-tuple-element.27.up_w, ...), custom_call_target="tpu_custom_call" | custom-call | flops 1610612736 | bytes 10485760 | tf_op jit(solution)/shard_map/experts/pallas_call | solution.py:116
  118.0 8.3 %experts.3.mine_other = bf16[256,256]{1,0:T(8,128)(2,1)S(1)} custom-call(s32[2]{0:T(128)S(1)} %pad_add_fusion.place, bf16[16,8,16,768]{3,2,1,0:T(8,128)(2,1)} %collective-permute-done.3.state, bf16[4,8,192,256]{3,2,1,0:T(8,128)(2,1)S(1)} %get-tuple-element.28.gate_w, bf16[4,8,192,256]{3,2,1,0:T(8,128)(2,1)S(1)} %get-tuple-element.27.up_w, ...), custom_call_target="tpu_custom_call" | custom-call | flops 1610612736 | bytes 10485760 | tf_op jit(solution)/shard_map/experts/pallas_call | solution.py:116
  126.5 1.3 collective-permute-done.4.theirs_own
  127.8 4.9 %down.1 = bf16[4,16,2,16,768]{4,3,2,1,0:T(8,128)(2,1)S(1)} custom-call(s32[2]{0:T(128)S(1)} %pad_add_fusion.place, bf16[256,256]{1,0:T(8,128)(2,1)S(1)} %experts.2.mine_own, bf16[256,256]{1,0:T(8,128)(2,1)S(1)} %experts.3.mine_other, bf16[256,256]{1,0:T(8,128)(2,1)S(1)} %collective-permute-done.4.theirs_own, ...), custom_call_target="tpu_custom_call" | custom-call | flops 1610612736 | bytes 7340032 | tf_op jit(solution)/shard_map/down/pallas_call | solution.py:176
  132.7 1.6 copy-done.1
  134.3 4.5 %all-to-all-start.4 = ((bf16[16,8,16,768]{3,2,1,0:T(8,128)(2,1)}), bf16[16,8,16,768]{3,2,1,0:T(8,128)(2,1)}, u32[]{:S(2)}, u32[]{:S(2)}) async-start(bf16[16,8,16,768]{3,2,1,0:T(8,128)(2,1)} %bitcast.122), calls=%async_computation.4 | async-start | bytes 6291456 | tf_op jit(solution)/shard_map/all_to_all | solution.py:27
  138.9 42.2 %all-to-all-done.4 = bf16[16,8,16,768]{3,2,1,0:T(8,128)(2,1)} async-done(((bf16[16,8,16,768]{3,2,1,0:T(8,128)(2,1)}), bf16[16,8,16,768]{3,2,1,0:T(8,128)(2,1)}, u32[]{:S(2)}, u32[]{:S(2)}) %all-to-all-start.4) | async-done | bytes 3145760 | tf_op jit(solution)/shard_map/all_to_all | solution.py:27
  181.1 3.0 %reduce_sum.62 = bf16[8,16,768]{2,1,0:T(8,128)(2,1)} reduce(bf16[16,8,16,768]{3,2,1,0:T(8,128)(2,1)} %all-to-all-done.4, bf16[]{:T(256)} %constant.190.clone.1), dimensions={0}, to_apply=%region_3.4 | reduce | flops 1474560 | bytes 3342338 | tf_op jit(solution)/shard_map/reduce_sum | solution.py:367
  184.2 3.7 %all-to-all-start.5 = ((bf16[8,16,768]{2,1,0:T(8,128)(2,1)}), bf16[8,16,768]{2,1,0:T(8,128)(2,1)S(1)}, u32[]{:S(2)}, u32[]{:S(2)}) async-start(bf16[8,16,768]{2,1,0:T(8,128)(2,1)} %reduce_sum.62), calls=%async_computation.5 | async-start | bytes 393216 | tf_op jit(solution)/shard_map/all_to_all | solution.py:27
  187.9 1.0 dynamic-slice_select_fusion
  189.2 7.1 %all-to-all-done.5 = bf16[8,16,768]{2,1,0:T(8,128)(2,1)S(1)} async-done(((bf16[8,16,768]{2,1,0:T(8,128)(2,1)}), bf16[8,16,768]{2,1,0:T(8,128)(2,1)S(1)}, u32[]{:S(2)}, u32[]{:S(2)}) %all-to-all-start.5) | async-done | bytes 196640 | tf_op jit(solution)/shard_map/all_to_all | solution.py:27
  196.4 11.0 %all_to_all.59 = bf16[8,16,768]{2,1,0:T(8,128)(2,1)S(1)} all-to-all(bf16[8,16,768]{2,1,0:T(8,128)(2,1)S(1)} %broadcast_in_dim.29), channel_id=1, replica_groups=mesh['x'=4,'z'=8,'y'=4,'c'=2] {'z'}, dimensions={0} | all-to-all | bytes 393216 | tf_op jit(solution)/shard_map/all_to_all | solution.py:27
  207.5 0.9 broadcast_in_dim.30
  208.4 5.6 %all-to-all-start.7 = ((bf16[4,8,16,768]{3,2,1,0:T(8,128)(2,1)}), bf16[4,8,16,768]{3,2,1,0:T(8,128)(2,1)S(1)}, u32[]{:S(2)}, u32[]{:S(2)}) async-start(bf16[4,8,16,768]{3,2,1,0:T(8,128)(2,1)} %broadcast_in_dim.30), calls=%async_computation.7 | async-start | bytes 1572864 | tf_op jit(solution)/shard_map/all_to_all | solution.py:27
  214.0 1.0 dynamic-slice_bitcast_fusion.3
  215.0 2.9 %collective-permute-start.10 = (bf16[2,768,128]{2,1,0:T(8,128)(2,1)}, bf16[2,768,128]{2,1,0:T(8,128)(2,1)}, u32[]{:S(2)}, u32[]{:S(2)}) collective-permute-start(bf16[2,768,128]{2,1,0:T(8,128)(2,1)} %get-tuple-element.15), channel_id=1, source_target_pairs={{0,192},{64,0},{128,64},{192,128},{1,193},{65,1},{129,65},{193,129... | collective-permute-start | bytes 1179656 | tf_op jit(solution)/shard_map/ppermute | solution.py:319
  217.9 2.7 collective-permute-start.8
  220.6 0.9 collective-permute-start.9
  221.5 1.0 all-to-all-done.7.own
  222.5 4.7 %collective-permute-start.7 = (bf16[4,8,16,768]{3,2,1,0:T(8,128)(2,1)S(1)}, bf16[4,8,16,768]{3,2,1,0:T(8,128)(2,1)}, u32[]{:S(2)}, u32[]{:S(2)}) collective-permute-start(bf16[4,8,16,768]{3,2,1,0:T(8,128)(2,1)S(1)} %all-to-all-done.7.own), channel_id=1, source_target_pairs={{0,1},{1,0},{2,3},{3,2},{4,5},{5,4},{6,7},{7,6},{8,9},{9,8},{10,11... | collective-permute-start | bytes 2359304 | tf_op jit(solution)/shard_map/ppermute | solution.py:23
  227.3 10.5 %collective-permute-done.9 = bf16[2,768,128]{2,1,0:T(8,128)(2,1)} collective-permute-done((bf16[2,768,128]{2,1,0:T(8,128)(2,1)S(1)}, bf16[2,768,128]{2,1,0:T(8,128)(2,1)}, u32[]{:S(2)}, u32[]{:S(2)}) %collective-permute-start.9) | collective-permute-done | bytes 393248 | tf_op jit(solution)/shard_map/ppermute | solution.py:319
  237.8 1.7 multiply_convert_fusion.3
  239.8 0.8 broadcast_select_fusion.1
  240.8 2.1 head.1
  242.9 0.9 copy-done.3
  243.8 2.8 dynamic_update_slice.3
  246.5 4.2 %all-to-all-start.8 = ((bf16[4,144,640]{2,1,0:T(8,128)(2,1)}), bf16[4,144,640]{2,1,0:T(8,128)(2,1)S(1)}, u32[]{:S(2)}, u32[]{:S(2)}) async-start(bf16[4,144,640]{2,1,0:T(8,128)(2,1)} %dynamic_update_slice.3), calls=%async_computation.8 | async-start | bytes 1474560 | tf_op jit(solution)/shard_map/all_to_all | solution.py:27
  251.7 9.5 %all-to-all-done.8.parts = bf16[4,144,640]{2,1,0:T(8,128)(2,1)S(1)} async-done(((bf16[4,144,640]{2,1,0:T(8,128)(2,1)}), bf16[4,144,640]{2,1,0:T(8,128)(2,1)S(1)}, u32[]{:S(2)}, u32[]{:S(2)}) %all-to-all-start.8) | async-done | bytes 737312 | tf_op jit(solution)/shard_map/all_to_all | solution.py:27
  261.1 0.9 finish.1
  262.7 7.3 %all-to-all-start.9 = ((f32[64,1,128]{2,1,0:T(1,128)}), f32[64,1,128]{2,1,0:T(1,128)S(1)}, u32[]{:S(2)}, u32[]{:S(2)}) async-start(f32[64,1,128]{2,1,0:T(1,128)} %bitcast.37), calls=%async_computation.9 | async-start | bytes 65536 | tf_op jit(solution)/shard_map/all_to_all | solution.py:27
  270.7 8.7 %all-to-all-done.9 = f32[64,1,128]{2,1,0:T(1,128)S(1)} async-done(((f32[64,1,128]{2,1,0:T(1,128)}), f32[64,1,128]{2,1,0:T(1,128)S(1)}, u32[]{:S(2)}, u32[]{:S(2)}) %all-to-all-start.9) | async-done | bytes 32800 | tf_op jit(solution)/shard_map/all_to_all | solution.py:27
  (102 shorter events, 10.7 us)
Async XLA Ops:
  0.6 10.7 %copy-start = (bf16[16,1,128,128]{3,2,1,0:T(8,128)(2,1)S(1)}, bf16[16,1,128,128]{3,2,1,0:T(8,128)(2,1)}, u32[]{:S(2)}) copy-start(bf16[16,1,128,128]{3,2,1,0:T(8,128)(2,1)} %param.21) | copy-start | bytes 1572868
  0.6 11.4 %copy-start.8 = (bf16[16,128]{1,0:T(8,128)(2,1)S(1)}, bf16[16,128]{1,0:T(8,128)(2,1)}, u32[]{:S(2)}) copy-start(bf16[16,128]{1,0:T(8,128)(2,1)} %param.20) | copy-start | bytes 12292
  3.3 19.1 %collective-permute-start = (bf16[784,192]{1,0:T(8,128)(2,1)S(1)}, bf16[784,192]{1,0:T(8,128)(2,1)S(1)}, u32[]{:S(2)}, u32[]{:S(2)}) collective-permute-start(bf16[784,192]{1,0:T(8,128)(2,1)S(1)} %get-tuple-element.18), channel_id=1, source_target_pairs={{0,64},{64,128},{128,192},{192,0},{1,65},{65,129},{129,193},{193,1... | collective-permute-start | bytes 903176 | tf_op jit(solution)/shard_map/ppermute | solution.py:306
  5.4 19.7 %collective-permute-start.1 = (bf16[784,192]{1,0:T(8,128)(2,1)S(1)}, bf16[784,192]{1,0:T(8,128)(2,1)S(1)}, u32[]{:S(2)}, u32[]{:S(2)}) collective-permute-start(bf16[784,192]{1,0:T(8,128)(2,1)S(1)} %get-tuple-element.19), channel_id=1, source_target_pairs={{0,128},{64,192},{128,0},{192,64},{1,129},{65,193},{129,1},{193,65... | collective-permute-start | bytes 903176 | tf_op jit(solution)/shard_map/ppermute | solution.py:306
  7.8 17.4 %collective-permute-start.2 = (bf16[784,192]{1,0:T(8,128)(2,1)S(1)}, bf16[784,192]{1,0:T(8,128)(2,1)S(1)}, u32[]{:S(2)}, u32[]{:S(2)}) collective-permute-start(bf16[784,192]{1,0:T(8,128)(2,1)S(1)} %get-tuple-element.20), channel_id=1, source_target_pairs={{0,192},{64,0},{128,64},{192,128},{1,193},{65,1},{129,65},{193,129... | collective-permute-start | bytes 903176 | tf_op jit(solution)/shard_map/ppermute | solution.py:306
  14.1 17.0 %all-to-all-start = ((bf16[8,16,768]{2,1,0:T(8,128)(2,1)}), bf16[8,16,768]{2,1,0:T(8,128)(2,1)}, u32[]{:S(2)}, u32[]{:S(2)}) async-start(bf16[8,16,768]{2,1,0:T(8,128)(2,1)} %broadcast_in_dim.26), calls=%async_computation | async-start | bytes 393216 | tf_op jit(solution)/shard_map/all_to_all | solution.py:27
  33.3 13.2 %all-to-all-start.1 = ((bf16[8,16,768]{2,1,0:T(8,128)(2,1)}), bf16[8,16,768]{2,1,0:T(8,128)(2,1)S(1)}, u32[]{:S(2)}, u32[]{:S(2)}) async-start(bf16[8,16,768]{2,1,0:T(8,128)(2,1)} %bitcast.6), calls=%async_computation.1 | async-start | bytes 393216 | tf_op jit(solution)/shard_map/all_to_all | solution.py:27
  97.5 7.4 %copy-start.5 = (bf16[6144,8]{0,1:T(8,128)(2,1)S(1)}, bf16[6144,8]{0,1:T(8,128)(2,1)}, u32[]{:S(2)}) copy-start(bf16[6144,8]{0,1:T(8,128)(2,1)} %param.26) | copy-start | bytes 294916
  97.5 7.4 %copy-start.6 = (f32[6144]{0:T(1024)S(1)}, f32[6144]{0:T(1024)}, u32[]{:S(2)}) copy-start(f32[6144]{0:T(1024)} %param.27) | copy-start | bytes 73732
  97.5 7.5 %copy-start.9 = (s32[512,2]{0,1:T(2,128)S(1)}, s32[512,2]{0,1:T(2,128)}, u32[]{:S(2)}) copy-start(s32[512,2]{0,1:T(2,128)} %param.31) | copy-start | bytes 12292
  97.5 20.5 %collective-permute-start.3 = (bf16[16,8,16,768]{3,2,1,0:T(8,128)(2,1)}, bf16[16,8,16,768]{3,2,1,0:T(8,128)(2,1)}, u32[]{:S(2)}, u32[]{:S(2)}) collective-permute-start(bf16[16,8,16,768]{3,2,1,0:T(8,128)(2,1)} %all_to_all.58.state), channel_id=1, source_target_pairs={{0,1},{1,0},{2,3},{3,2},{4,5},{5,4},{6,7},{7,6},{8,9},{9,8},{10,11... | collective-permute-start | bytes 9437192 | tf_op jit(solution)/shard_map/ppermute | solution.py:23
  104.8 21.6 %collective-permute-start.6 = (bf16[256,3072]{1,0:T(8,128)(2,1)}, bf16[256,3072]{1,0:T(8,128)(2,1)S(1)}, u32[]{:S(2)}, u32[]{:S(2)}) collective-permute-start(bf16[256,3072]{1,0:T(8,128)(2,1)} %dynamic-slice_bitcast_fusion), channel_id=1, source_target_pairs={{0,1},{1,0},{2,3},{3,2},{4,5},{5,4},{6,7},{7,6},{8,9},{9,8},{10,11... | collective-permute-start | bytes 4718600 | tf_op jit(solution)/shard_map/ppermute | solution.py:23
  117.5 9.0 %collective-permute-start.5 = (bf16[256,256]{1,0:T(8,128)(2,1)S(1)}, bf16[256,256]{1,0:T(8,128)(2,1)S(1)}, u32[]{:S(2)}, u32[]{:S(2)}) collective-permute-start(bf16[256,256]{1,0:T(8,128)(2,1)S(1)} %experts.2.mine_own), channel_id=1, source_target_pairs={{0,1},{1,0},{2,3},{3,2},{4,5},{5,4},{6,7},{7,6},{8,9},{9,8},{10,11... | collective-permute-start | bytes 393224 | tf_op jit(solution)/shard_map/ppermute | solution.py:23
  118.0 9.7 %copy-start.2 = (bf16[1,256,6144]{2,1,0:T(8,128)(2,1)S(1)}, bf16[1,256,6144]{2,1,0:T(8,128)(2,1)}, u32[]{:S(2)}) copy-start(bf16[1,256,6144]{2,1,0:T(8,128)(2,1)} %param.30) | copy-start | bytes 9437188
  126.3 1.4 collective-permute-start.4
  132.7 1.7 copy-start.1
  134.3 46.8 %all-to-all-start.4 = ((bf16[16,8,16,768]{3,2,1,0:T(8,128)(2,1)}), bf16[16,8,16,768]{3,2,1,0:T(8,128)(2,1)}, u32[]{:S(2)}, u32[]{:S(2)}) async-start(bf16[16,8,16,768]{3,2,1,0:T(8,128)(2,1)} %bitcast.122), calls=%async_computation.4 | async-start | bytes 6291456 | tf_op jit(solution)/shard_map/all_to_all | solution.py:27
  184.2 29.8 %copy-start.4 = (bf16[6144,128]{1,0:T(8,128)(2,1)S(1)}, bf16[6144,128]{1,0:T(8,128)(2,1)}, u32[]{:S(2)}) copy-start(bf16[6144,128]{1,0:T(8,128)(2,1)} %param.33) | copy-start | bytes 4718596
  184.2 12.2 %all-to-all-start.5 = ((bf16[8,16,768]{2,1,0:T(8,128)(2,1)}), bf16[8,16,768]{2,1,0:T(8,128)(2,1)S(1)}, u32[]{:S(2)}, u32[]{:S(2)}) async-start(bf16[8,16,768]{2,1,0:T(8,128)(2,1)} %reduce_sum.62), calls=%async_computation.5 | async-start | bytes 393216 | tf_op jit(solution)/shard_map/all_to_all | solution.py:27
  189.0 38.2 %copy-start.7 = (f32[6144]{0:T(1024)S(1)}, f32[6144]{0:T(1024)}, u32[]{:S(2)}) copy-start(f32[6144]{0:T(1024)} %param.32) | copy-start | bytes 73732
  208.4 14.1 %all-to-all-start.7 = ((bf16[4,8,16,768]{3,2,1,0:T(8,128)(2,1)}), bf16[4,8,16,768]{3,2,1,0:T(8,128)(2,1)S(1)}, u32[]{:S(2)}, u32[]{:S(2)}) async-start(bf16[4,8,16,768]{3,2,1,0:T(8,128)(2,1)} %broadcast_in_dim.30), calls=%async_computation.7 | async-start | bytes 1572864 | tf_op jit(solution)/shard_map/all_to_all | solution.py:27
  215.0 12.3 %collective-permute-start.10 = (bf16[2,768,128]{2,1,0:T(8,128)(2,1)}, bf16[2,768,128]{2,1,0:T(8,128)(2,1)}, u32[]{:S(2)}, u32[]{:S(2)}) collective-permute-start(bf16[2,768,128]{2,1,0:T(8,128)(2,1)} %get-tuple-element.15), channel_id=1, source_target_pairs={{0,192},{64,0},{128,64},{192,128},{1,193},{65,1},{129,65},{193,129... | collective-permute-start | bytes 1179656 | tf_op jit(solution)/shard_map/ppermute | solution.py:319
  217.9 9.4 %collective-permute-start.8 = (bf16[2,768,128]{2,1,0:T(8,128)(2,1)}, bf16[2,768,128]{2,1,0:T(8,128)(2,1)}, u32[]{:S(2)}, u32[]{:S(2)}) collective-permute-start(bf16[2,768,128]{2,1,0:T(8,128)(2,1)} %get-tuple-element.17), channel_id=1, source_target_pairs={{0,128},{64,192},{128,0},{192,64},{1,129},{65,193},{129,1},{193,65... | collective-permute-start | bytes 1179656 | tf_op jit(solution)/shard_map/ppermute | solution.py:319
  220.6 17.2 %collective-permute-start.9 = (bf16[2,768,128]{2,1,0:T(8,128)(2,1)S(1)}, bf16[2,768,128]{2,1,0:T(8,128)(2,1)}, u32[]{:S(2)}, u32[]{:S(2)}) collective-permute-start(bf16[2,768,128]{2,1,0:T(8,128)(2,1)S(1)} %get-tuple-element.16), channel_id=1, source_target_pairs={{0,64},{64,128},{128,192},{192,0},{1,65},{65,129},{129,193},{193,1... | collective-permute-start | bytes 1179656 | tf_op jit(solution)/shard_map/ppermute | solution.py:319
  222.5 17.3 %collective-permute-start.7 = (bf16[4,8,16,768]{3,2,1,0:T(8,128)(2,1)S(1)}, bf16[4,8,16,768]{3,2,1,0:T(8,128)(2,1)}, u32[]{:S(2)}, u32[]{:S(2)}) collective-permute-start(bf16[4,8,16,768]{3,2,1,0:T(8,128)(2,1)S(1)} %all-to-all-done.7.own), channel_id=1, source_target_pairs={{0,1},{1,0},{2,3},{3,2},{4,5},{5,4},{6,7},{7,6},{8,9},{9,8},{10,11... | collective-permute-start | bytes 2359304 | tf_op jit(solution)/shard_map/ppermute | solution.py:23
  240.7 39.1 %copy-start.10 = (f32[2]{0:T(128)S(1)}, f32[2]{0:T(128)}, u32[]{:S(2)}) copy-start(f32[2]{0:T(128)} %param.35) | copy-start | bytes 28
  242.9 0.9 copy-start.3
  246.5 14.6 %all-to-all-start.8 = ((bf16[4,144,640]{2,1,0:T(8,128)(2,1)}), bf16[4,144,640]{2,1,0:T(8,128)(2,1)S(1)}, u32[]{:S(2)}, u32[]{:S(2)}) async-start(bf16[4,144,640]{2,1,0:T(8,128)(2,1)} %dynamic_update_slice.3), calls=%async_computation.8 | async-start | bytes 1474560 | tf_op jit(solution)/shard_map/all_to_all | solution.py:27
  262.7 16.7 %all-to-all-start.9 = ((f32[64,1,128]{2,1,0:T(1,128)}), f32[64,1,128]{2,1,0:T(1,128)S(1)}, u32[]{:S(2)}, u32[]{:S(2)}) async-start(f32[64,1,128]{2,1,0:T(1,128)} %bitcast.37), calls=%async_computation.9 | async-start | bytes 65536 | tf_op jit(solution)/shard_map/all_to_all | solution.py:27

commit v3 on v2

--- a/solution.py
+++ b/solution.py
@@ -60,17 +60,20 @@
 ):
     step = pl.program_id(0)
     width = state.shape[-1]
-    hidden = state[...].reshape(-1, width)
-    gate = jnp.dot(hidden, gate_w[...].reshape(width, -1), preferred_element_type=F32)
-    up = jnp.dot(hidden, up_w[...].reshape(width, -1), preferred_element_type=F32)
-    route = lax.dot_general(
-        hidden, router_w[0], (((1,), (1,)), ((), ())), preferred_element_type=F32
-    )
-    wide = hidden.astype(F32)
-    square = jnp.zeros(squares.shape, F32)
-    for start in range(0, width, 128):
-        piece = wide[:, start : start + 128]
-        square += piece * piece
+    gate = up = route = square = 0.0
+    for block in range(state.shape[1]):
+        hidden = state[:, block].reshape(-1, width)
+        gate += jnp.dot(
+            hidden, gate_w[:, block].reshape(width, -1), preferred_element_type=F32
+        )
+        up += jnp.dot(hidden, up_w[:, block].reshape(width, -1), preferred_element_type=F32)
+        route += lax.dot_general(
+            hidden, router_w[block], (((1,), (1,)), ((), ())), preferred_element_type=F32
+        )
+        wide = hidden.astype(F32)
+        for start in range(0, width, 128):
+            piece = wide[:, start : start + 128]
+            square += piece * piece
 
     @pl.when(step == 0)
     def _():
@@ -111,19 +114,20 @@
     total = NXY * rows
     hidden_units = gate_w.shape[-1]
     unit = width // NX
-    weights = pl.BlockSpec((NX, 1, unit, hidden_units), lambda z, p: (0, z, 0, 0))
+    step = 4
+    weights = pl.BlockSpec((NX, step, unit, hidden_units), lambda z, p: (0, z, 0, 0))
     count = router_w.shape[1]
     return pl.pallas_call(
         expert_kernel,
         out_shape=jax.ShapeDtypeStruct((total, hidden_units), BF16),
         grid_spec=pltpu.PrefetchScalarGridSpec(
             num_scalar_prefetch=1,
-            grid=(NZ,),
+            grid=(NZ // step,),
             in_specs=[
-                pl.BlockSpec((NXY, 1, rows, width), lambda z, p: (0, z, 0, 0)),
+                pl.BlockSpec((NXY, step, rows, width), lambda z, p: (0, z, 0, 0)),
                 weights,
                 weights,
-                pl.BlockSpec((1, count, width), lambda z, p: (z, 0, 0)),
+                pl.BlockSpec((step, count, width), lambda z, p: (z, 0, 0)),
                 pl.BlockSpec((total, 2), lambda z, p: (0, 0)),
             ],
             out_specs=pl.BlockSpec((total, hidden_units), lambda z, p: (0, 0)),
@@ -175,7 +179,7 @@
     block = width // steps
     return pl.pallas_call(
         down_kernel,
-        out_shape=jax.ShapeDtypeStruct((NX, NXY, NC, rows, width), BF16),
+        out_shape=pltpu.HBM((NX, NXY, NC, rows, width), BF16),
         grid_spec=pltpu.PrefetchScalarGridSpec(
             num_scalar_prefetch=1,
             grid=(NX, steps),
@@ -198,10 +202,9 @@
     )(place, *acts, w_mine, w_theirs)
 
 
-def head_kernel(own, other, w_own, w_other, out):
+def head_kernel(own, other, w_own, w_other, below, out):
     width = own.shape[-1]
     vocab = w_own.shape[1]
-    rows = out.shape[1]
     near = own[...].reshape(-1, width)
     far = other[...].reshape(-1, width)
     logits = jnp.dot(near, w_own[...], preferred_element_type=F32)
@@ -218,21 +221,22 @@
     count = near.shape[0] // NX
     out[:, :count, :vocab] = logits.astype(BF16).reshape(NX, count, vocab)
     out[:, :count, vocab:] = extra.astype(BF16).reshape(NX, count, 128)
-    out[:, count:, :] = jnp.zeros((NX, rows - count, vocab + 128), BF16)
-
-
-def head(own, other, w_own, w_other, rows):
+    out[:, count:, :] = below[...]
+
+
+def head(own, other, w_own, w_other, below):
     vocab = w_own.shape[1]
     total = own.shape[0] * own.shape[1] * own.shape[2]
+    rows = total // NX + below.shape[1]
     return pl.pallas_call(
         head_kernel,
-        out_shape=jax.ShapeDtypeStruct((NX, rows, vocab + 128), BF16),
+        out_shape=pltpu.HBM((NX, rows, vocab + 128), BF16),
         compiler_params=pltpu.CompilerParams(vmem_limit_bytes=32 << 20),
         cost_estimate=pl.CostEstimate(
             flops=4 * total * own.shape[3] * vocab, bytes_accessed=4 << 20, transcendentals=0
         ),
         name="head",
-    )(own, other, w_own, w_other)
+    )(own, other, w_own, w_other, below)
 
 
 def finish_kernel(place, parts, token, stats):
@@ -346,9 +350,6 @@
     )
 
     hidden_z = spread(hidden, "z", NZ)
-    own = spread(hidden_z, XY, NXY)
-    other = swap_cores(own)
-
     order = expert_ids.reshape(NXY, NC, part_rows, 2).transpose(1, 0, 2, 3)
     order = order.reshape(NC, -1, 2)
     order_own = lax.dynamic_index_in_dim(order, core, 0, keepdims=False)
@@ -359,6 +360,13 @@
     router_z = router_z.reshape(NZ, -1, NX * unit)
     gate_g = (w_gate[0].astype(F32) * gain_col).astype(BF16)
     up_g = (w_up[0].astype(F32) * gain_col).astype(BF16)
+    ready = (hidden_z, gate_g, up_g, router_z, order_own, order_other)
+    ready = lax.optimization_barrier(ready + (head_own, head_other, down_other))
+    hidden_z, gate_g, up_g, router_z, order_own, order_other = ready[:6]
+    head_own, head_other, down_other = ready[6:]
+    own = spread(hidden_z, XY, NXY)
+    other = swap_cores(own)
+
     act_own = experts(place, own, gate_g, up_g, router_z, order_own)
     act_other = experts(place, other, gate_g, up_g, router_z, order_other)
     acts = (act_own, act_other, swap_cores(act_other), swap_cores(act_own))
@@ -381,7 +389,6 @@
     final_own = spread(spread(moved, "z", NZ), "y", NY).reshape(NY, NZ, part_rows, slab)
     final_other = swap_cores(final_own)
     count = total_rows // NX
-    partial = head(final_own, final_other, head_own, head_other, count + 16)
 
     own_rows = total_rows // (NX * NZ * NY * NC)
     size = (NX, 1, own_rows, slab)
@@ -392,7 +399,8 @@
     high = jnp.where(core == 0, far, near)
     vocab = head_own.shape[1]
     rows_out = jnp.concatenate([low, high], axis=1).reshape(NX, -1, vocab)
-    partial = lax.dynamic_update_slice(partial, rows_out, (0, count, 0))
+    below = jnp.pad(rows_out, ((0, 0), (0, 16 - rows_out.shape[1]), (0, 128)))
+    partial = head(final_own, final_other, head_own, head_other, below)
     parts = exchange(partial, "x")
     hidden_out = parts[:, count : count + rows_out.shape[1], :vocab]
     hidden_out = hidden_out.reshape(NX, NC, own_rows, slab).transpose(2, 1, 0, 3)

time: 282 us -> 286 us (1.014)
  starting transfers between devices: 63.2 us -> 76.4 us
  waiting for transfers between devices: 94.8 us -> 83.6 us
  other arithmetic: 12.6 us -> 16 us
  Pallas kernels: 24.2 us -> 21 us
    ppermute x5, starting transfers between devices: 10.2 us -> 26.6 us  [swap_cores(): return lax.ppermute(value, 'c', [(0, 1), (1, 0)])]
    ppermute x3, waiting for transfers between devices: 10.5 us -> 0.01 us  [shards(): part = lax.ppermute(part, 'x', [(i, (i + shift) % NX) for i in range(NX)])]
    pallas_call x2, Pallas kernels: 16.3 us -> 9.1 us  [experts(): pl.pallas_call(expert_kernel, out_shape=jax.ShapeDtypeStruct((total, hidd...]
    slice x3, local copies, waits for them, and re-layouts: 0.08 us -> 4.34 us  [shards(): w_wide = jnp.concatenate([pack[:depth] for pack in packs], axis=1)]
    pallas_call x2, Pallas kernels: 7.03 us -> 11 us  [the longest x1 7.97 us: down(): pl.pallas_call(down_kernel, out_shape=pltpu.HBM((NX, NXY, NC, rows, width...]
  transfers between devices with their start and end apart: 18 -> 18, of which waited for: 10 -> 9; matrix products, arithmetic and copies ran while one was open for 7% -> 10% of each run, Pallas kernels for 6% -> 3%
where the time goes in v3:
time: 286 us; the launch traced here: 285 us
  waiting for transfers between devices  83.6 us (29%)
  starting transfers between devices  76.4 us (27%)
  blocking collectives  62.8 us (22%)
  Pallas kernels  21 us (7%)
  local copies, waits for them, and re-layouts  18.6 us (7%)
  other arithmetic  16 us (6%)
  matrix products  5.22 us (2%)
    all_to_all x7, waiting for transfers between devices, exchange(): return lax.all_to_all(value, axes, split_axis=0, concat_axis=0, tiled=True)  80 us
    all_to_all x3, blocking collectives, exchange(): return lax.all_to_all(value, axes, split_axis=0, concat_axis=0, tiled=True)  62.8 us
    all_to_all x7, starting transfers between devices, exchange(): return lax.all_to_all(value, axes, split_axis=0, concat_axis=0, tiled=True)  41.6 us
    ppermute x5, starting transfers between devices, swap_cores(): return lax.ppermute(value, 'c', [(0, 1), (1, 0)])  26.6 us
    pallas_call x2, Pallas kernels, experts(): pl.pallas_call(expert_kernel, out_shape=jax.ShapeDtypeStruct((total, hidd...  9.1 us
    pallas_call x1, Pallas kernels, down(): pl.pallas_call(down_kernel, out_shape=pltpu.HBM((NX, NXY, NC, rows, width...  7.97 us
  transfers between devices with their start and end apart: 18, of which 9 were waited for; matrix products, arithmetic and copies ran while one was open for 10% of the time, Pallas kernels for 3%

profile of v3, /device:TPU:1, one launch (start us, length us, event | category | flops | bytes accessed | tf_op | source)
XLA Modules:
  0.0 284.8 jit_solution(17046159594017236131)
XLA Ops:
  0.7 0.9 reshape.177
  3.0 0.8 fusion.29
  4.5 1.4 fusion.14
  6.6 9.0 %all-to-all-start = ((bf16[8,16,768]{2,1,0:T(8,128)(2,1)}), bf16[8,16,768]{2,1,0:T(8,128)(2,1)}, u32[]{:S(2)}, u32[]{:S(2)}) async-start(bf16[8,16,768]{2,1,0:T(8,128)(2,1)} %broadcast_in_dim.26), calls=%async_computation | async-start | bytes 393216 | tf_op jit(solution)/shard_map/all_to_all | solution.py:27
  15.6 1.0 constant_dynamic-slice_fusion.6
  16.7 1.2 copy.131
  17.9 1.2 pad_maximum_fusion.1
  19.1 2.5 collective-permute-start.2
  22.7 1.1 dynamic-slice_bitcast_fusion.3
  23.8 1.8 collective-permute-start.3
  25.7 0.8 collective-permute-start.4
  26.5 5.2 %fusion = (bf16[6144,256]{1,0:T(8,128)(2,1)}, bf16[6144,256]{1,0:T(8,128)(2,1)}) fusion(bf16[1,6144,256]{2,1,0:T(8,128)(2,1)} %param.29, f32[6144]{0:T(1024)S(1)} %copy-done.8, bf16[1,6144,256]{2,1,0:T(8,128)(2,1)} %param.28), kind=kLoop, calls=%fused_computation.1 | loop fusion | flops 9437184 | bytes 12607488 | tf_op jit(solution)/shard_map/convert_element_type | solution.py:362
  31.7 2.8 dynamic-slice_bitcast_fusion
  35.5 2.0 collective-permute-start.5
  38.1 15.9 %collective-permute-start.6 = (bf16[256,3072]{1,0:T(8,128)(2,1)}, bf16[256,3072]{1,0:T(8,128)(2,1)}, u32[]{:S(2)}, u32[]{:S(2)}) collective-permute-start(bf16[256,3072]{1,0:T(8,128)(2,1)} %dynamic-slice_bitcast_fusion), channel_id=1, source_target_pairs={{0,1},{1,0},{2,3},{3,2},{4,5},{5,4},{6,7},{7,6},{8,9},{9,8},{10,11... | collective-permute-start | bytes 4718600 | tf_op jit(solution)/shard_map/ppermute | solution.py:23
  54.8 1.8 slice.51
  56.6 1.8 slice.50
  58.4 0.8 slice.49
  59.1 2.6 fusion.10
  61.7 4.6 %all-to-all-start.1 = ((bf16[8,16,768]{2,1,0:T(8,128)(2,1)}), bf16[8,16,768]{2,1,0:T(8,128)(2,1)S(1)}, u32[]{:S(2)}, u32[]{:S(2)}) async-start(bf16[8,16,768]{2,1,0:T(8,128)(2,1)} %bitcast.6), calls=%async_computation.1 | async-start | bytes 393216 | tf_op jit(solution)/shard_map/all_to_all | solution.py:27
  66.3 5.9 %all-to-all-done.1 = bf16[8,16,768]{2,1,0:T(8,128)(2,1)S(1)} async-done(((bf16[8,16,768]{2,1,0:T(8,128)(2,1)}), bf16[8,16,768]{2,1,0:T(8,128)(2,1)S(1)}, u32[]{:S(2)}, u32[]{:S(2)}) %all-to-all-start.1) | async-done | bytes 196640 | tf_op jit(solution)/shard_map/all_to_all | solution.py:27
  73.3 6.6 %all-to-all-start.2 = ((bf16[8,16,768]{2,1,0:T(8,128)(2,1)}), bf16[8,16,768]{2,1,0:T(8,128)(2,1)S(1)}, u32[]{:S(2)}, u32[]{:S(2)}) async-start(bf16[8,16,768]{2,1,0:T(8,128)(2,1)} %broadcast_in_dim.27), calls=%async_computation.2 | async-start | bytes 393216 | tf_op jit(solution)/shard_map/all_to_all | solution.py:27
  80.0 1.7 multiply_convert_fusion.3
  82.0 6.5 %all-to-all-done.2 = bf16[8,16,768]{2,1,0:T(8,128)(2,1)S(1)} async-done(((bf16[8,16,768]{2,1,0:T(8,128)(2,1)}), bf16[8,16,768]{2,1,0:T(8,128)(2,1)S(1)}, u32[]{:S(2)}, u32[]{:S(2)}) %all-to-all-start.2) | async-done | bytes 196640 | tf_op jit(solution)/shard_map/all_to_all | solution.py:27
  88.8 38.5 %all_to_all.57.state = bf16[16,8,16,768]{3,2,1,0:T(8,128)(2,1)S(1)} all-to-all(bf16[16,8,16,768]{3,2,1,0:T(8,128)(2,1)S(1)} %broadcast_in_dim.28), channel_id=1, replica_groups=mesh['x'=4,'z'=8,'y'=4,'c'=2] {'x','y'}, dimensions={0} | all-to-all | bytes 6291456 | tf_op jit(solution)/shard_map/all_to_all | solution.py:27
  127.3 5.1 %collective-permute-start.7 = (bf16[16,8,16,768]{3,2,1,0:T(8,128)(2,1)S(1)}, bf16[16,8,16,768]{3,2,1,0:T(8,128)(2,1)S(1)}, u32[]{:S(2)}, u32[]{:S(2)}) collective-permute-start(bf16[16,8,16,768]{3,2,1,0:T(8,128)(2,1)S(1)} %all_to_all.57.state), channel_id=1, source_target_pairs={{0,1},{1,0},{2,3},{3,2},{4,5},{5,4},{6,7},{7,6},{8,9},{9,8},{10,11... | collective-permute-start | bytes 9437192 | tf_op jit(solution)/shard_map/ppermute | solution.py:23
  132.5 4.6 %experts.2.mine_own = bf16[256,256]{1,0:T(8,128)(2,1)S(1)} custom-call(s32[2]{0:T(128)S(1)} %pad_add_fusion.place, bf16[16,8,16,768]{3,2,1,0:T(8,128)(2,1)S(1)} %all_to_all.57.state, bf16[4,8,192,256]{3,2,1,0:T(8,128)(2,1)S(1)} %bitcast.128, bf16[4,8,192,256]{3,2,1,0:T(8,128)(2,1)S(1)} %bitcast.126, bf16[8,8,768]{2,1,0:T(8,128)(2,1)S(1)} %reshape.183.router_w, ...), custom_call_target="tpu_custom_call" | custom-call | flops 1610612736 | bytes 10485760 | tf_op jit(solution)/shard_map/experts/pallas_call | solution.py:120
  137.7 4.5 %experts.3.mine_other = bf16[256,256]{1,0:T(8,128)(2,1)S(1)} custom-call(s32[2]{0:T(128)S(1)} %pad_add_fusion.place, bf16[16,8,16,768]{3,2,1,0:T(8,128)(2,1)S(1)} %collective-permute-done.7.state, bf16[4,8,192,256]{3,2,1,0:T(8,128)(2,1)S(1)} %bitcast.129, bf16[4,8,192,256]{3,2,1,0:T(8,128)(2,1)S(1)} %bitcast.127, bf16[8,8,768]{2,1,0:T(8,128)(2,1)S(1)} %reshape.183.router_w, ...), custom_call_target="tpu_custom_call" | custom-call | flops 1610612736 | bytes 10485760 | tf_op jit(solution)/shard_map/experts/pallas_call | solution.py:120
  142.7 1.0 collective-permute-done.8.theirs_own
  143.7 8.0 %down.1 = bf16[4,16,2,16,768]{4,3,2,1,0:T(8,128)(2,1)} custom-call(s32[2]{0:T(128)S(1)} %pad_add_fusion.place, bf16[256,256]{1,0:T(8,128)(2,1)S(1)} %experts.2.mine_own, bf16[256,256]{1,0:T(8,128)(2,1)S(1)} %experts.3.mine_other, bf16[256,256]{1,0:T(8,128)(2,1)S(1)} %collective-permute-done.8.theirs_own, ...), custom_call_target="tpu_custom_call" | custom-call | flops 1610612736 | bytes 7340032 | tf_op jit(solution)/shard_map/down/pallas_call | solution.py:180
  151.7 4.5 %all-to-all-start.4 = ((bf16[16,8,16,768]{3,2,1,0:T(8,128)(2,1)}), bf16[16,8,16,768]{3,2,1,0:T(8,128)(2,1)}, u32[]{:S(2)}, u32[]{:S(2)}) async-start(bf16[16,8,16,768]{3,2,1,0:T(8,128)(2,1)} %bitcast.132), calls=%async_computation.4 | async-start | bytes 6291456 | tf_op jit(solution)/shard_map/all_to_all | solution.py:27
  156.2 41.4 %all-to-all-done.4 = bf16[16,8,16,768]{3,2,1,0:T(8,128)(2,1)} async-done(((bf16[16,8,16,768]{3,2,1,0:T(8,128)(2,1)}), bf16[16,8,16,768]{3,2,1,0:T(8,128)(2,1)}, u32[]{:S(2)}, u32[]{:S(2)}) %all-to-all-start.4) | async-done | bytes 3145760 | tf_op jit(solution)/shard_map/all_to_all | solution.py:27
  197.6 3.0 %reduce_sum.62 = bf16[8,16,768]{2,1,0:T(8,128)(2,1)} reduce(bf16[16,8,16,768]{3,2,1,0:T(8,128)(2,1)} %all-to-all-done.4, bf16[]{:T(256)} %constant.191.clone.1), dimensions={0}, to_apply=%region_3.4 | reduce | flops 1474560 | bytes 3342338 | tf_op jit(solution)/shard_map/reduce_sum | solution.py:375
  200.6 3.4 %all-to-all-start.5 = ((bf16[8,16,768]{2,1,0:T(8,128)(2,1)}), bf16[8,16,768]{2,1,0:T(8,128)(2,1)S(1)}, u32[]{:S(2)}, u32[]{:S(2)}) async-start(bf16[8,16,768]{2,1,0:T(8,128)(2,1)} %reduce_sum.62), calls=%async_computation.5 | async-start | bytes 393216 | tf_op jit(solution)/shard_map/all_to_all | solution.py:27
  204.0 1.0 dynamic-slice_select_fusion
  205.4 7.2 %all-to-all-done.5 = bf16[8,16,768]{2,1,0:T(8,128)(2,1)S(1)} async-done(((bf16[8,16,768]{2,1,0:T(8,128)(2,1)}), bf16[8,16,768]{2,1,0:T(8,128)(2,1)S(1)}, u32[]{:S(2)}, u32[]{:S(2)}) %all-to-all-start.5) | async-done | bytes 196640 | tf_op jit(solution)/shard_map/all_to_all | solution.py:27
  212.7 11.1 %all_to_all.58 = bf16[8,16,768]{2,1,0:T(8,128)(2,1)S(1)} all-to-all(bf16[8,16,768]{2,1,0:T(8,128)(2,1)S(1)} %broadcast_in_dim.29), channel_id=1, replica_groups=mesh['x'=4,'z'=8,'y'=4,'c'=2] {'z'}, dimensions={0} | all-to-all | bytes 393216 | tf_op jit(solution)/shard_map/all_to_all | solution.py:27
  223.9 13.2 %all_to_all.59.own = bf16[4,8,16,768]{3,2,1,0:T(8,128)(2,1)S(1)} all-to-all(bf16[4,8,16,768]{3,2,1,0:T(8,128)(2,1)S(1)} %broadcast_in_dim.30), channel_id=1, replica_groups=mesh['x'=4,'z'=8,'y'=4,'c'=2] {'y'}, dimensions={0} | all-to-all | bytes 1572864 | tf_op jit(solution)/shard_map/all_to_all | solution.py:27
  237.1 5.1 %collective-permute-start.10 = (bf16[4,8,16,768]{3,2,1,0:T(8,128)(2,1)S(1)}, bf16[4,8,16,768]{3,2,1,0:T(8,128)(2,1)}, u32[]{:S(2)}, u32[]{:S(2)}) collective-permute-start(bf16[4,8,16,768]{3,2,1,0:T(8,128)(2,1)S(1)} %all_to_all.59.own), channel_id=1, source_target_pairs={{0,1},{1,0},{2,3},{3,2},{4,5},{5,4},{6,7},{7,6},{8,9},{9,8},{10,11... | collective-permute-start | bytes 2359304 | tf_op jit(solution)/shard_map/ppermute | solution.py:23
  242.1 2.0 collective-permute-done.10.other
  244.2 0.8 broadcast_select_fusion.1
  245.1 3.0 %head.1 = bf16[4,144,640]{2,1,0:T(8,128)(2,1)} custom-call(bf16[4,8,16,768]{3,2,1,0:T(8,128)(2,1)S(1)} %all_to_all.59.own, bf16[4,8,16,768]{3,2,1,0:T(8,128)(2,1)} %collective-permute-done.10.other, bf16[768,512]{1,0:T(8,128)(2,1)S(1)} %get-tuple-element.19.w_own, bf16[768,512]{1,0:T(8,128)(2,1)S(1)} %get-tuple-element.20.w_other, ...), custom_call_target="tpu_custom_call" | custom-call | flops 805306368 | bytes 4194304 | tf_op jit(solution)/shard_map/head/pallas_call | solution.py:231
  248.2 7.9 %all-to-all-start.8 = ((bf16[4,144,640]{2,1,0:T(8,128)(2,1)}), bf16[4,144,640]{2,1,0:T(8,128)(2,1)S(1)}, u32[]{:S(2)}, u32[]{:S(2)}) async-start(bf16[4,144,640]{2,1,0:T(8,128)(2,1)} %head.1), calls=%async_computation.8 | async-start | bytes 1474560 | tf_op jit(solution)/shard_map/all_to_all | solution.py:27
  256.1 0.8 dynamic-slice_bitcast_fusion.8
  257.0 10.2 %all-to-all-done.8.parts = bf16[4,144,640]{2,1,0:T(8,128)(2,1)S(1)} async-done(((bf16[4,144,640]{2,1,0:T(8,128)(2,1)}), bf16[4,144,640]{2,1,0:T(8,128)(2,1)S(1)}, u32[]{:S(2)}, u32[]{:S(2)}) %all-to-all-start.8) | async-done | bytes 737312 | tf_op jit(solution)/shard_map/all_to_all | solution.py:27
  267.3 0.9 finish.1
  268.8 5.6 %all-to-all-start.9 = ((f32[64,1,128]{2,1,0:T(1,128)}), f32[64,1,128]{2,1,0:T(1,128)S(1)}, u32[]{:S(2)}, u32[]{:S(2)}) async-start(f32[64,1,128]{2,1,0:T(1,128)} %bitcast.39), calls=%async_computation.9 | async-start | bytes 65536 | tf_op jit(solution)/shard_map/all_to_all | solution.py:27
  275.1 8.8 %all-to-all-done.9 = f32[64,1,128]{2,1,0:T(1,128)S(1)} async-done(((f32[64,1,128]{2,1,0:T(1,128)}), f32[64,1,128]{2,1,0:T(1,128)S(1)}, u32[]{:S(2)}, u32[]{:S(2)}) %all-to-all-start.9) | async-done | bytes 32800 | tf_op jit(solution)/shard_map/all_to_all | solution.py:27
  (103 shorter events, 12.4 us)
Async XLA Ops:
  0.6 3.2 %copy-start = (bf16[16,1,128,128]{3,2,1,0:T(8,128)(2,1)S(1)}, bf16[16,1,128,128]{3,2,1,0:T(8,128)(2,1)}, u32[]{:S(2)}) copy-start(bf16[16,1,128,128]{3,2,1,0:T(8,128)(2,1)} %param.21) | copy-start | bytes 1572868
  0.6 22.1 %copy-start.6 = (bf16[6144,128]{1,0:T(8,128)(2,1)S(1)}, bf16[6144,128]{1,0:T(8,128)(2,1)}, u32[]{:S(2)}) copy-start(bf16[6144,128]{1,0:T(8,128)(2,1)} %param.33) | copy-start | bytes 4718596
  5.9 20.6 %copy-start.7 = (bf16[6144,8]{0,1:T(8,128)(2,1)S(1)}, bf16[6144,8]{0,1:T(8,128)(2,1)}, u32[]{:S(2)}) copy-start(bf16[6144,8]{0,1:T(8,128)(2,1)} %param.26) | copy-start | bytes 294916
  5.9 20.6 %copy-start.8 = (f32[6144]{0:T(1024)S(1)}, f32[6144]{0:T(1024)}, u32[]{:S(2)}) copy-start(f32[6144]{0:T(1024)} %param.27) | copy-start | bytes 73732
  6.6 52.6 %all-to-all-start = ((bf16[8,16,768]{2,1,0:T(8,128)(2,1)}), bf16[8,16,768]{2,1,0:T(8,128)(2,1)}, u32[]{:S(2)}, u32[]{:S(2)}) async-start(bf16[8,16,768]{2,1,0:T(8,128)(2,1)} %broadcast_in_dim.26), calls=%async_computation | async-start | bytes 393216 | tf_op jit(solution)/shard_map/all_to_all | solution.py:27
  19.1 16.3 %collective-permute-start.2 = (bf16[784,192]{1,0:T(8,128)(2,1)}, bf16[784,192]{1,0:T(8,128)(2,1)}, u32[]{:S(2)}, u32[]{:S(2)}) collective-permute-start(bf16[784,192]{1,0:T(8,128)(2,1)} %get-tuple-element.38), channel_id=1, source_target_pairs={{0,192},{64,0},{128,64},{192,128},{1,193},{65,1},{129,65},{193,129... | collective-permute-start | bytes 903176 | tf_op jit(solution)/shard_map/ppermute | solution.py:310
  21.6 16.5 %collective-permute-start.1 = (bf16[784,192]{1,0:T(8,128)(2,1)}, bf16[784,192]{1,0:T(8,128)(2,1)}, u32[]{:S(2)}, u32[]{:S(2)}) collective-permute-start(bf16[784,192]{1,0:T(8,128)(2,1)} %get-tuple-element.37), channel_id=1, source_target_pairs={{0,128},{64,192},{128,0},{192,64},{1,129},{65,193},{129,1},{193,65... | collective-permute-start | bytes 903176 | tf_op jit(solution)/shard_map/ppermute | solution.py:310
  22.1 36.2 %collective-permute-start = (bf16[784,192]{1,0:T(8,128)(2,1)}, bf16[784,192]{1,0:T(8,128)(2,1)S(1)}, u32[]{:S(2)}, u32[]{:S(2)}) collective-permute-start(bf16[784,192]{1,0:T(8,128)(2,1)} %get-tuple-element.36), channel_id=1, source_target_pairs={{0,64},{64,128},{128,192},{192,0},{1,65},{65,129},{129,193},{193,1... | collective-permute-start | bytes 903176 | tf_op jit(solution)/shard_map/ppermute | solution.py:310
  23.8 56.2 %collective-permute-start.3 = (bf16[2,768,128]{2,1,0:T(8,128)(2,1)}, bf16[2,768,128]{2,1,0:T(8,128)(2,1)}, u32[]{:S(2)}, u32[]{:S(2)}) collective-permute-start(bf16[2,768,128]{2,1,0:T(8,128)(2,1)} %get-tuple-element.35), channel_id=1, source_target_pairs={{0,128},{64,192},{128,0},{192,64},{1,129},{65,193},{129,1},{193,65... | collective-permute-start | bytes 1179656 | tf_op jit(solution)/shard_map/ppermute | solution.py:323
  25.7 54.3 %collective-permute-start.4 = (bf16[2,768,128]{2,1,0:T(8,128)(2,1)}, bf16[2,768,128]{2,1,0:T(8,128)(2,1)}, u32[]{:S(2)}, u32[]{:S(2)}) collective-permute-start(bf16[2,768,128]{2,1,0:T(8,128)(2,1)} %get-tuple-element.34), channel_id=1, source_target_pairs={{0,64},{64,128},{128,192},{192,0},{1,65},{65,129},{129,193},{193,1... | collective-permute-start | bytes 1179656 | tf_op jit(solution)/shard_map/ppermute | solution.py:323
  31.7 3.3 %copy-start.10 = (s32[512,2]{0,1:T(2,128)S(1)}, s32[512,2]{0,1:T(2,128)}, u32[]{:S(2)}) copy-start(s32[512,2]{0,1:T(2,128)} %param.31) | copy-start | bytes 12292
  31.7 3.7 %copy-start.9 = (f32[6144]{0:T(1024)S(1)}, f32[6144]{0:T(1024)}, u32[]{:S(2)}) copy-start(f32[6144]{0:T(1024)} %param.32) | copy-start | bytes 73732
  35.5 44.5 %collective-permute-start.5 = (bf16[2,768,128]{2,1,0:T(8,128)(2,1)}, bf16[2,768,128]{2,1,0:T(8,128)(2,1)}, u32[]{:S(2)}, u32[]{:S(2)}) collective-permute-start(bf16[2,768,128]{2,1,0:T(8,128)(2,1)} %get-tuple-element.33), channel_id=1, source_target_pairs={{0,192},{64,0},{128,64},{192,128},{1,193},{65,1},{129,65},{193,129... | collective-permute-start | bytes 1179656 | tf_op jit(solution)/shard_map/ppermute | solution.py:323
  38.1 50.4 %collective-permute-start.6 = (bf16[256,3072]{1,0:T(8,128)(2,1)}, bf16[256,3072]{1,0:T(8,128)(2,1)}, u32[]{:S(2)}, u32[]{:S(2)}) collective-permute-start(bf16[256,3072]{1,0:T(8,128)(2,1)} %dynamic-slice_bitcast_fusion), channel_id=1, source_target_pairs={{0,1},{1,0},{2,3},{3,2},{4,5},{5,4},{6,7},{7,6},{8,9},{9,8},{10,11... | collective-permute-start | bytes 4718600 | tf_op jit(solution)/shard_map/ppermute | solution.py:23
  61.7 10.5 %all-to-all-start.1 = ((bf16[8,16,768]{2,1,0:T(8,128)(2,1)}), bf16[8,16,768]{2,1,0:T(8,128)(2,1)S(1)}, u32[]{:S(2)}, u32[]{:S(2)}) async-start(bf16[8,16,768]{2,1,0:T(8,128)(2,1)} %bitcast.6), calls=%async_computation.1 | async-start | bytes 393216 | tf_op jit(solution)/shard_map/all_to_all | solution.py:27
  73.3 15.2 %all-to-all-start.2 = ((bf16[8,16,768]{2,1,0:T(8,128)(2,1)}), bf16[8,16,768]{2,1,0:T(8,128)(2,1)S(1)}, u32[]{:S(2)}, u32[]{:S(2)}) async-start(bf16[8,16,768]{2,1,0:T(8,128)(2,1)} %broadcast_in_dim.27), calls=%async_computation.2 | async-start | bytes 393216 | tf_op jit(solution)/shard_map/all_to_all | solution.py:27
  88.8 43.7 %copy-start.1 = (bf16[6144,256]{1,0:T(8,128)(2,1)S(1)}, bf16[6144,256]{1,0:T(8,128)(2,1)}, u32[]{:S(2)}) copy-start(bf16[6144,256]{1,0:T(8,128)(2,1)} %get-tuple-element.14) | copy-start | bytes 9437188
  88.8 43.7 %copy-start.2 = (bf16[6144,256]{1,0:T(8,128)(2,1)S(1)}, bf16[6144,256]{1,0:T(8,128)(2,1)}, u32[]{:S(2)}) copy-start(bf16[6144,256]{1,0:T(8,128)(2,1)} %get-tuple-element.13) | copy-start | bytes 9437188
  127.3 9.7 %copy-start.3 = (bf16[16,8,16,768]{3,2,1,0:T(8,128)(2,1)}, bf16[16,8,16,768]{3,2,1,0:T(8,128)(2,1)S(1)}, u32[]{:S(2)}) copy-start(bf16[16,8,16,768]{3,2,1,0:T(8,128)(2,1)S(1)} %all_to_all.57.state) | copy-start | bytes 9437188
  127.3 10.4 %collective-permute-start.7 = (bf16[16,8,16,768]{3,2,1,0:T(8,128)(2,1)S(1)}, bf16[16,8,16,768]{3,2,1,0:T(8,128)(2,1)S(1)}, u32[]{:S(2)}, u32[]{:S(2)}) collective-permute-start(bf16[16,8,16,768]{3,2,1,0:T(8,128)(2,1)S(1)} %all_to_all.57.state), channel_id=1, source_target_pairs={{0,1},{1,0},{2,3},{3,2},{4,5},{5,4},{6,7},{7,6},{8,9},{9,8},{10,11... | collective-permute-start | bytes 9437192 | tf_op jit(solution)/shard_map/ppermute | solution.py:23
  137.1 6.6 %copy-start.4 = (bf16[1,256,6144]{2,1,0:T(8,128)(2,1)S(1)}, bf16[1,256,6144]{2,1,0:T(8,128)(2,1)}, u32[]{:S(2)}) copy-start(bf16[1,256,6144]{2,1,0:T(8,128)(2,1)} %param.30) | copy-start | bytes 9437188
  137.1 5.7 %collective-permute-start.9 = (bf16[256,256]{1,0:T(8,128)(2,1)S(1)}, bf16[256,256]{1,0:T(8,128)(2,1)S(1)}, u32[]{:S(2)}, u32[]{:S(2)}) collective-permute-start(bf16[256,256]{1,0:T(8,128)(2,1)S(1)} %experts.2.mine_own), channel_id=1, source_target_pairs={{0,1},{1,0},{2,3},{3,2},{4,5},{5,4},{6,7},{7,6},{8,9},{9,8},{10,11... | collective-permute-start | bytes 393224 | tf_op jit(solution)/shard_map/ppermute | solution.py:23
  137.7 4.6 %copy-start.5 = (bf16[16,8,16,768]{3,2,1,0:T(8,128)(2,1)}, bf16[16,8,16,768]{3,2,1,0:T(8,128)(2,1)S(1)}, u32[]{:S(2)}) copy-start(bf16[16,8,16,768]{3,2,1,0:T(8,128)(2,1)S(1)} %collective-permute-done.7.state) | copy-start | bytes 9437188
  142.3 1.4 collective-permute-start.8
  151.7 45.9 %all-to-all-start.4 = ((bf16[16,8,16,768]{3,2,1,0:T(8,128)(2,1)}), bf16[16,8,16,768]{3,2,1,0:T(8,128)(2,1)}, u32[]{:S(2)}, u32[]{:S(2)}) async-start(bf16[16,8,16,768]{3,2,1,0:T(8,128)(2,1)} %bitcast.132), calls=%async_computation.4 | async-start | bytes 6291456 | tf_op jit(solution)/shard_map/all_to_all | solution.py:27
  200.6 12.0 %all-to-all-start.5 = ((bf16[8,16,768]{2,1,0:T(8,128)(2,1)}), bf16[8,16,768]{2,1,0:T(8,128)(2,1)S(1)}, u32[]{:S(2)}, u32[]{:S(2)}) async-start(bf16[8,16,768]{2,1,0:T(8,128)(2,1)} %reduce_sum.62), calls=%async_computation.5 | async-start | bytes 393216 | tf_op jit(solution)/shard_map/all_to_all | solution.py:27
  237.1 7.1 %collective-permute-start.10 = (bf16[4,8,16,768]{3,2,1,0:T(8,128)(2,1)S(1)}, bf16[4,8,16,768]{3,2,1,0:T(8,128)(2,1)}, u32[]{:S(2)}, u32[]{:S(2)}) collective-permute-start(bf16[4,8,16,768]{3,2,1,0:T(8,128)(2,1)S(1)} %all_to_all.59.own), channel_id=1, source_target_pairs={{0,1},{1,0},{2,3},{3,2},{4,5},{5,4},{6,7},{7,6},{8,9},{9,8},{10,11... | collective-permute-start | bytes 2359304 | tf_op jit(solution)/shard_map/ppermute | solution.py:23
  245.1 39.2 %copy-start.11 = (f32[2]{0:T(128)S(1)}, f32[2]{0:T(128)}, u32[]{:S(2)}) copy-start(f32[2]{0:T(128)} %param.35) | copy-start | bytes 28
  248.2 19.1 %all-to-all-start.8 = ((bf16[4,144,640]{2,1,0:T(8,128)(2,1)}), bf16[4,144,640]{2,1,0:T(8,128)(2,1)S(1)}, u32[]{:S(2)}, u32[]{:S(2)}) async-start(bf16[4,144,640]{2,1,0:T(8,128)(2,1)} %head.1), calls=%async_computation.8 | async-start | bytes 1474560 | tf_op jit(solution)/shard_map/all_to_all | solution.py:27
  268.8 15.1 %all-to-all-start.9 = ((f32[64,1,128]{2,1,0:T(1,128)}), f32[64,1,128]{2,1,0:T(1,128)S(1)}, u32[]{:S(2)}, u32[]{:S(2)}) async-start(f32[64,1,128]{2,1,0:T(1,128)} %bitcast.39), calls=%async_computation.9 | async-start | bytes 65536 | tf_op jit(solution)/shard_map/all_to_all | solution.py:27

commit v4 on v3

--- a/solution.py
+++ b/solution.py
@@ -53,6 +53,50 @@
     out = jnp.einsum("rkgl,rkld->rkgd", weight_cached, v_cache, preferred_element_type=F32)
     out = out + weight_fresh.astype(F32)[..., None] * fresh_value
     return out.reshape(rows, group * heads_kv * width).astype(BF16)
+
+
+def project_kernel(place, attended, *refs):
+    packs, (partial, residual) = refs[:NX], refs[NX:]
+    depth = attended.shape[-1]
+    value = attended[...].reshape(-1, depth)
+    products = [
+        jnp.dot(value, pack[:depth, :], preferred_element_type=F32) for pack in packs
+    ]
+    rows = [pack[depth:, :].astype(F32) for pack in packs]
+    x = place[2]
+
+    def order(parts):
+        blocks = []
+        for i in range(NX):
+            away = lax.rem(x - i + NX, NX)
+            block = parts[NX - 1]
+            for shift in range(NX - 1):
+                block = jnp.where(away == shift, parts[shift], block)
+            blocks.append(block)
+        return jnp.concatenate(blocks, axis=1).astype(BF16)
+
+    partial[...] = order(products).reshape(partial.shape)
+    residual[...] = order(rows)
+
+
+def project(place, attended, packs):
+    depth, unit = attended.shape[-1], packs[0].shape[1]
+    rows = packs[0].shape[0] - depth
+    vmem = pl.BlockSpec(memory_space=pltpu.VMEM)
+    return pl.pallas_call(
+        project_kernel,
+        out_shape=(
+            jax.ShapeDtypeStruct((NY * NC, rows, NX * unit), BF16),
+            jax.ShapeDtypeStruct((rows, NX * unit), BF16),
+        ),
+        in_specs=[pl.BlockSpec(memory_space=pltpu.SMEM)] + [vmem] * (1 + NX),
+        out_specs=(vmem, vmem),
+        compiler_params=pltpu.CompilerParams(vmem_limit_bytes=32 << 20),
+        cost_estimate=pl.CostEstimate(
+            flops=2 * NZ * rows * depth * NX * unit, bytes_accessed=2 << 20, transcendentals=0
+        ),
+        name="project",
+    )(place, attended, *packs)
 
 
 def expert_kernel(
@@ -175,25 +219,21 @@
     total, units = acts[0].shape
     rows = total // NXY
     width = w_theirs.shape[1] // NX
-    steps = 2
-    block = width // steps
     return pl.pallas_call(
         down_kernel,
         out_shape=pltpu.HBM((NX, NXY, NC, rows, width), BF16),
         grid_spec=pltpu.PrefetchScalarGridSpec(
             num_scalar_prefetch=1,
-            grid=(NX, steps),
-            in_specs=[pl.BlockSpec((total, units), lambda x, s, p: (0, 0))] * 4
+            grid=(NX,),
+            in_specs=[pl.BlockSpec((total, units), lambda x, p: (0, 0))] * 4
             + [
-                pl.BlockSpec((units, block), lambda x, s, p: (0, (p[1] * NX + x) * steps + s)),
-                pl.BlockSpec((units, block), lambda x, s, p: (0, x * steps + s)),
+                pl.BlockSpec((units, width), lambda x, p: (0, p[1] * NX + x)),
+                pl.BlockSpec((units, width), lambda x, p: (0, x)),
             ],
-            out_specs=pl.BlockSpec(
-                (1, NXY, NC, rows, block), lambda x, s, p: (x, 0, 0, 0, s)
-            ),
+            out_specs=pl.BlockSpec((1, NXY, NC, rows, width), lambda x, p: (x, 0, 0, 0, 0)),
         ),
         compiler_params=pltpu.CompilerParams(
-            dimension_semantics=("arbitrary", "arbitrary"), vmem_limit_bytes=32 << 20
+            dimension_semantics=("arbitrary",), vmem_limit_bytes=32 << 20
         ),
         cost_estimate=pl.CostEstimate(
             flops=8 * total * units * width * NX, bytes_accessed=7 << 20, transcendentals=0
@@ -293,26 +333,31 @@
 ):
     x, z, y, core = (lax.axis_index(name) for name in ("x", "z", "y", "c"))
     expert = y * NC + core
-    place = jnp.stack([expert, core]).astype(jnp.int32)
+    place = jnp.stack([expert, core, x]).astype(jnp.int32)
     width_all = gain_moe.shape[0]
     unit = w_out.shape[1]
     total_rows = residual.shape[0]
     part_rows = total_rows // (NX * NY * NC)
 
-    packs = []
+    sends = []
     for shift in range(NX):
         target = (x + shift) % NX
         rows = lax.dynamic_slice_in_dim(
             residual, (target * NY * NC + expert) * part_rows, part_rows
         )
-        pack = jnp.concatenate([w_out, rows], axis=0)
-        if shift:
-            pack = lax.ppermute(pack, "x", [(i, (i + shift) % NX) for i in range(NX)])
-        packs.append(pack)
+        sends.append(jnp.concatenate([w_out, rows], axis=0))
+    packs = [sends[0]]
+    for shift in range(1, NX):
+        pairs = [(i, (i + shift) % NX) for i in range(NX)]
+        packs.append(lax.ppermute(sends[shift], "x", pairs))
     depth = w_out.shape[0]
-    w_wide = jnp.concatenate([pack[:depth] for pack in packs], axis=1)
-    residual_wide = jnp.concatenate([pack[depth:] for pack in packs], axis=1)
-
+
+    attended = attend(queries, new_keys, new_values, k_cache, v_cache, lengths)
+    attended_x = spread(attended, "z", NZ)
+    partial_heads, residual_here = project(place, attended_x, packs)
+    late = (partial_heads, expert_ids, w_vocab, w_gate, w_up, w_down, router)
+    late = lax.optimization_barrier(late)
+    partial_heads, expert_ids, w_vocab, w_gate, w_up, w_down, router = late
     half = width_all // NC
     slab = half // NX
     vocab_rows = w_vocab.reshape(NC, NX, slab, -1)
@@ -338,16 +383,9 @@
     down_sent = lax.dynamic_slice_in_dim(w_down[0], (1 - core) * half, half, axis=1)
     down_other = swap_cores(down_sent)
 
-    attended = attend(queries, new_keys, new_values, k_cache, v_cache, lengths)
-    attended_x = spread(attended, "z", NZ).reshape(-1, depth)
-    partial_heads = jnp.dot(attended_x, w_wide, preferred_element_type=F32).astype(BF16)
-    pieces = exchange(partial_heads.reshape(NY * NC, part_rows, NX * unit), EX)
-    summed = jnp.sum(pieces.astype(F32), axis=0) + residual_wide.astype(F32)
-    turned = summed.astype(BF16).reshape(part_rows, NX, unit)
-    hidden = jnp.concatenate(
-        [lax.dynamic_index_in_dim(turned, (x - i) % NX, 1, keepdims=False) for i in range(NX)],
-        axis=1,
-    )
+    pieces = exchange(partial_heads, EX)
+    hidden = jnp.sum(pieces.astype(F32), axis=0) + residual_here.astype(F32)
+    hidden = hidden.astype(BF16)
 
     hidden_z = spread(hidden, "z", NZ)
     order = expert_ids.reshape(NXY, NC, part_rows, 2).transpose(1, 0, 2, 3)

time: 286 us -> 276 us (0.965)
  starting transfers between devices: 76.4 us -> 64.3 us
  waiting for transfers between devices: 83.6 us -> 91.6 us
  local copies, waits for them, and re-layouts: 18.6 us -> 14.9 us
    ppermute x5, starting transfers between devices: 26.6 us -> 10.7 us  [swap_cores(): return lax.ppermute(value, 'c', [(0, 1), (1, 0)])]
    ppermute x3, waiting for transfers between devices: 0.01 us -> 13.6 us  [shards(): packs.append(lax.ppermute(sends[shift], 'x', pairs))]
    all_to_all x7, waiting for transfers between devices: 80 us -> 73 us  [exchange(): return lax.all_to_all(value, axes, split_axis=0, concat_axis=0, tiled=True)]
    slice x3 -> x0, local copies, waits for them, and re-layouts: 4.34 us -> none  [shards(): w_wide = jnp.concatenate([pack[:depth] for pack in packs], axis=1)]
  transfers between devices with their start and end apart: 18 -> 18, of which waited for: 9 -> 11; matrix products, arithmetic and copies ran while one was open for 10% -> 7% of each run, Pallas kernels for 3% -> 3%
where the time goes in v4:
time: 276 us; the launch traced here: 274 us
  waiting for transfers between devices  91.6 us (33%)
  blocking collectives  65.1 us (24%)
  starting transfers between devices  64.3 us (23%)
  Pallas kernels  20.3 us (7%)
  local copies, waits for them, and re-layouts  14.9 us (5%)
  other arithmetic  14.3 us (5%)
    all_to_all x7, waiting for transfers between devices, exchange(): return lax.all_to_all(value, axes, split_axis=0, concat_axis=0, tiled=True)  73 us
    all_to_all x3, blocking collectives, exchange(): return lax.all_to_all(value, axes, split_axis=0, concat_axis=0, tiled=True)  65.1 us
    all_to_all x7, starting transfers between devices, exchange(): return lax.all_to_all(value, axes, split_axis=0, concat_axis=0, tiled=True)  43.5 us
    ppermute x3, waiting for transfers between devices, shards(): packs.append(lax.ppermute(sends[shift], 'x', pairs))  13.6 us
    ppermute x5, starting transfers between devices, swap_cores(): return lax.ppermute(value, 'c', [(0, 1), (1, 0)])  10.7 us
    pallas_call x2, Pallas kernels, experts(): pl.pallas_call(expert_kernel, out_shape=jax.ShapeDtypeStruct((total, hidd...  9.1 us
    pallas_call x1, Pallas kernels, down(): pl.pallas_call(down_kernel, out_shape=pltpu.HBM((NX, NXY, NC, rows, width...  5.56 us
  transfers between devices with their start and end apart: 18, of which 11 were waited for; matrix products, arithmetic and copies ran while one was open for 7% of the time, Pallas kernels for 3%

profile of v4, /device:TPU:1, one launch (start us, length us, event | category | flops | bytes accessed | tf_op | source)
XLA Modules:
  0.0 274.1 jit_solution(11546525674042370833)
XLA Ops:
  0.6 0.8 reshape.165
  2.9 0.8 fusion.18
  4.4 1.4 fusion.3
  6.5 9.0 %all-to-all-start = ((bf16[8,16,768]{2,1,0:T(8,128)(2,1)}), bf16[8,16,768]{2,1,0:T(8,128)(2,1)S(1)}, u32[]{:S(2)}, u32[]{:S(2)}) async-start(bf16[8,16,768]{2,1,0:T(8,128)(2,1)} %broadcast_in_dim.26), calls=%async_computation | async-start | bytes 393216 | tf_op jit(solution)/shard_map/all_to_all | solution.py:27
  15.5 1.0 constant_dynamic-slice_fusion.2
  16.6 1.2 copy.76
  18.1 1.3 collective-permute-start
  19.4 2.5 collective-permute-start.1
  21.8 1.2 collective-permute-start.2
  23.0 1.4 reshape.173
  24.3 0.7 constant_dynamic-slice_fusion.1
  25.2 4.0 %collective-permute-done.refs_1_ = bf16[784,192]{1,0:T(8,128)(2,1)S(1)} collective-permute-done((bf16[784,192]{1,0:T(8,128)(2,1)S(1)}, bf16[784,192]{1,0:T(8,128)(2,1)S(1)}, u32[]{:S(2)}, u32[]{:S(2)}) %collective-permute-start) | collective-permute-done | bytes 301088 | tf_op jit(solution)/shard_map/ppermute | solution.py:352
  29.2 9.6 %collective-permute-done.1.refs_2_ = bf16[784,192]{1,0:T(8,128)(2,1)S(1)} collective-permute-done((bf16[784,192]{1,0:T(8,128)(2,1)S(1)}, bf16[784,192]{1,0:T(8,128)(2,1)S(1)}, u32[]{:S(2)}, u32[]{:S(2)}) %collective-permute-start.1) | collective-permute-done | bytes 301088 | tf_op jit(solution)/shard_map/ppermute | solution.py:352
  38.8 1.7 project.1
  40.5 6.5 %all-to-all-start.1 = ((bf16[8,16,768]{2,1,0:T(8,128)(2,1)}), bf16[8,16,768]{2,1,0:T(8,128)(2,1)S(1)}, u32[]{:S(2)}, u32[]{:S(2)}) async-start(bf16[8,16,768]{2,1,0:T(8,128)(2,1)} %get-tuple-element.22), calls=%async_computation.1 | async-start | bytes 393216 | tf_op jit(solution)/shard_map/all_to_all | solution.py:27
  47.0 1.5 dynamic-slice_bitcast_fusion.3
  48.4 2.5 collective-permute-start.3
  50.9 2.7 dynamic-slice_bitcast_fusion
  53.9 4.7 %fusion = (bf16[6144,256]{1,0:T(8,128)(2,1)}, bf16[6144,256]{1,0:T(8,128)(2,1)}) fusion(bf16[1,6144,256]{2,1,0:T(8,128)(2,1)S(1)} %copy-done.6, f32[6144]{0:T(1024)S(1)} %copy-done.8, bf16[1,6144,256]{2,1,0:T(8,128)(2,1)} %param.28), kind=kLoop, calls=%fused_computation.1 | loop fusion | flops 9437184 | bytes 12607488 | tf_op jit(solution)/shard_map/convert_element_type | solution.py:400
  59.2 2.5 collective-permute-start.5
  62.9 6.6 %all-to-all-start.2 = ((bf16[8,16,768]{2,1,0:T(8,128)(2,1)}), bf16[8,16,768]{2,1,0:T(8,128)(2,1)S(1)}, u32[]{:S(2)}, u32[]{:S(2)}) async-start(bf16[8,16,768]{2,1,0:T(8,128)(2,1)} %broadcast_in_dim.27), calls=%async_computation.2 | async-start | bytes 393216 | tf_op jit(solution)/shard_map/all_to_all | solution.py:27
  69.5 1.3 collective-permute-done.4
  70.9 1.7 multiply_convert_fusion.3
  72.9 5.4 %all-to-all-done.2 = bf16[8,16,768]{2,1,0:T(8,128)(2,1)S(1)} async-done(((bf16[8,16,768]{2,1,0:T(8,128)(2,1)}), bf16[8,16,768]{2,1,0:T(8,128)(2,1)S(1)}, u32[]{:S(2)}, u32[]{:S(2)}) %all-to-all-start.2) | async-done | bytes 196640 | tf_op jit(solution)/shard_map/all_to_all | solution.py:27
  78.6 40.9 %all_to_all.57.state = bf16[16,8,16,768]{3,2,1,0:T(8,128)(2,1)S(1)} all-to-all(bf16[16,8,16,768]{3,2,1,0:T(8,128)(2,1)S(1)} %broadcast_in_dim.28), channel_id=1, replica_groups=mesh['x'=4,'z'=8,'y'=4,'c'=2] {'x','y'}, dimensions={0} | all-to-all | bytes 6291456 | tf_op jit(solution)/shard_map/all_to_all | solution.py:27
  119.5 4.6 %collective-permute-start.7 = (bf16[16,8,16,768]{3,2,1,0:T(8,128)(2,1)S(1)}, bf16[16,8,16,768]{3,2,1,0:T(8,128)(2,1)S(1)}, u32[]{:S(2)}, u32[]{:S(2)}) collective-permute-start(bf16[16,8,16,768]{3,2,1,0:T(8,128)(2,1)S(1)} %all_to_all.57.state), channel_id=1, source_target_pairs={{0,1},{1,0},{2,3},{3,2},{4,5},{5,4},{6,7},{7,6},{8,9},{9,8},{10,11... | collective-permute-start | bytes 9437192 | tf_op jit(solution)/shard_map/ppermute | solution.py:23
  124.1 4.6 %experts.2.mine_own = bf16[256,256]{1,0:T(8,128)(2,1)S(1)} custom-call(s32[3]{0:T(128)S(1)} %pad_add_fusion.place, bf16[16,8,16,768]{3,2,1,0:T(8,128)(2,1)S(1)} %all_to_all.57.state, bf16[4,8,192,256]{3,2,1,0:T(8,128)(2,1)S(1)} %bitcast.111, bf16[4,8,192,256]{3,2,1,0:T(8,128)(2,1)S(1)} %bitcast.109, bf16[8,8,768]{2,1,0:T(8,128)(2,1)S(1)} %reshape.169.router_w, ...), custom_call_target="tpu_custom_call" | custom-call | flops 1610612736 | bytes 10485760 | tf_op jit(solution)/shard_map/experts/pallas_call | solution.py:164
  129.4 4.5 %experts.3.mine_other = bf16[256,256]{1,0:T(8,128)(2,1)S(1)} custom-call(s32[3]{0:T(128)S(1)} %pad_add_fusion.place, bf16[16,8,16,768]{3,2,1,0:T(8,128)(2,1)S(1)} %collective-permute-done.7.state, bf16[4,8,192,256]{3,2,1,0:T(8,128)(2,1)S(1)} %bitcast.112, bf16[4,8,192,256]{3,2,1,0:T(8,128)(2,1)S(1)} %bitcast.110, bf16[8,8,768]{2,1,0:T(8,128)(2,1)S(1)} %reshape.169.router_w, ...), custom_call_target="tpu_custom_call" | custom-call | flops 1610612736 | bytes 10485760 | tf_op jit(solution)/shard_map/experts/pallas_call | solution.py:164
  134.4 1.0 collective-permute-done.8.theirs_own
  135.4 5.6 %down.1 = bf16[4,16,2,16,768]{4,3,2,1,0:T(8,128)(2,1)} custom-call(s32[3]{0:T(128)S(1)} %pad_add_fusion.place, bf16[256,256]{1,0:T(8,128)(2,1)S(1)} %experts.2.mine_own, bf16[256,256]{1,0:T(8,128)(2,1)S(1)} %experts.3.mine_other, bf16[256,256]{1,0:T(8,128)(2,1)S(1)} %collective-permute-done.8.theirs_own, ...), custom_call_target="tpu_custom_call" | custom-call | flops 1610612736 | bytes 7340032 | tf_op jit(solution)/shard_map/down/pallas_call | solution.py:222
  141.0 4.5 %all-to-all-start.4 = ((bf16[16,8,16,768]{3,2,1,0:T(8,128)(2,1)}), bf16[16,8,16,768]{3,2,1,0:T(8,128)(2,1)}, u32[]{:S(2)}, u32[]{:S(2)}) async-start(bf16[16,8,16,768]{3,2,1,0:T(8,128)(2,1)} %bitcast.115), calls=%async_computation.4 | async-start | bytes 6291456 | tf_op jit(solution)/shard_map/all_to_all | solution.py:27
  145.5 41.4 %all-to-all-done.4 = bf16[16,8,16,768]{3,2,1,0:T(8,128)(2,1)} async-done(((bf16[16,8,16,768]{3,2,1,0:T(8,128)(2,1)}), bf16[16,8,16,768]{3,2,1,0:T(8,128)(2,1)}, u32[]{:S(2)}, u32[]{:S(2)}) %all-to-all-start.4) | async-done | bytes 3145760 | tf_op jit(solution)/shard_map/all_to_all | solution.py:27
  186.9 3.1 %reduce_sum.59 = bf16[8,16,768]{2,1,0:T(8,128)(2,1)} reduce(bf16[16,8,16,768]{3,2,1,0:T(8,128)(2,1)} %all-to-all-done.4, bf16[]{:T(256)} %constant.173.clone.1), dimensions={0}, to_apply=%region_3.4 | reduce | flops 1474560 | bytes 3342338 | tf_op jit(solution)/shard_map/reduce_sum | solution.py:413
  189.9 3.4 %all-to-all-start.5 = ((bf16[8,16,768]{2,1,0:T(8,128)(2,1)}), bf16[8,16,768]{2,1,0:T(8,128)(2,1)S(1)}, u32[]{:S(2)}, u32[]{:S(2)}) async-start(bf16[8,16,768]{2,1,0:T(8,128)(2,1)} %reduce_sum.59), calls=%async_computation.5 | async-start | bytes 393216 | tf_op jit(solution)/shard_map/all_to_all | solution.py:27
  193.3 1.0 dynamic-slice_select_fusion
  194.7 7.2 %all-to-all-done.5 = bf16[8,16,768]{2,1,0:T(8,128)(2,1)S(1)} async-done(((bf16[8,16,768]{2,1,0:T(8,128)(2,1)}), bf16[8,16,768]{2,1,0:T(8,128)(2,1)S(1)}, u32[]{:S(2)}, u32[]{:S(2)}) %all-to-all-start.5) | async-done | bytes 196640 | tf_op jit(solution)/shard_map/all_to_all | solution.py:27
  202.0 11.1 %all_to_all.58 = bf16[8,16,768]{2,1,0:T(8,128)(2,1)S(1)} all-to-all(bf16[8,16,768]{2,1,0:T(8,128)(2,1)S(1)} %broadcast_in_dim.29), channel_id=1, replica_groups=mesh['x'=4,'z'=8,'y'=4,'c'=2] {'z'}, dimensions={0} | all-to-all | bytes 393216 | tf_op jit(solution)/shard_map/all_to_all | solution.py:27
  213.1 13.1 %all_to_all.59.own = bf16[4,8,16,768]{3,2,1,0:T(8,128)(2,1)S(1)} all-to-all(bf16[4,8,16,768]{3,2,1,0:T(8,128)(2,1)S(1)} %broadcast_in_dim.30), channel_id=1, replica_groups=mesh['x'=4,'z'=8,'y'=4,'c'=2] {'y'}, dimensions={0} | all-to-all | bytes 1572864 | tf_op jit(solution)/shard_map/all_to_all | solution.py:27
  226.2 5.2 %collective-permute-start.10 = (bf16[4,8,16,768]{3,2,1,0:T(8,128)(2,1)S(1)}, bf16[4,8,16,768]{3,2,1,0:T(8,128)(2,1)}, u32[]{:S(2)}, u32[]{:S(2)}) collective-permute-start(bf16[4,8,16,768]{3,2,1,0:T(8,128)(2,1)S(1)} %all_to_all.59.own), channel_id=1, source_target_pairs={{0,1},{1,0},{2,3},{3,2},{4,5},{5,4},{6,7},{7,6},{8,9},{9,8},{10,11... | collective-permute-start | bytes 2359304 | tf_op jit(solution)/shard_map/ppermute | solution.py:23
  231.4 2.0 collective-permute-done.10.other
  233.5 0.8 broadcast_select_fusion.1
  234.4 3.0 %head.1 = bf16[4,144,640]{2,1,0:T(8,128)(2,1)} custom-call(bf16[4,8,16,768]{3,2,1,0:T(8,128)(2,1)S(1)} %all_to_all.59.own, bf16[4,8,16,768]{3,2,1,0:T(8,128)(2,1)} %collective-permute-done.10.other, bf16[768,512]{1,0:T(8,128)(2,1)S(1)} %get-tuple-element.37.w_own, bf16[768,512]{1,0:T(8,128)(2,1)S(1)} %get-tuple-element.38.w_other, ...), custom_call_target="tpu_custom_call" | custom-call | flops 805306368 | bytes 4194304 | tf_op jit(solution)/shard_map/head/pallas_call | solution.py:271
  237.4 7.9 %all-to-all-start.8 = ((bf16[4,144,640]{2,1,0:T(8,128)(2,1)}), bf16[4,144,640]{2,1,0:T(8,128)(2,1)S(1)}, u32[]{:S(2)}, u32[]{:S(2)}) async-start(bf16[4,144,640]{2,1,0:T(8,128)(2,1)} %head.1), calls=%async_computation.8 | async-start | bytes 1474560 | tf_op jit(solution)/shard_map/all_to_all | solution.py:27
  245.3 0.8 dynamic-slice_bitcast_fusion.8
  246.3 10.2 %all-to-all-done.8.parts = bf16[4,144,640]{2,1,0:T(8,128)(2,1)S(1)} async-done(((bf16[4,144,640]{2,1,0:T(8,128)(2,1)}), bf16[4,144,640]{2,1,0:T(8,128)(2,1)S(1)}, u32[]{:S(2)}, u32[]{:S(2)}) %all-to-all-start.8) | async-done | bytes 737312 | tf_op jit(solution)/shard_map/all_to_all | solution.py:27
  256.5 0.9 finish.1
  258.1 5.6 %all-to-all-start.9 = ((f32[64,1,128]{2,1,0:T(1,128)}), f32[64,1,128]{2,1,0:T(1,128)S(1)}, u32[]{:S(2)}, u32[]{:S(2)}) async-start(f32[64,1,128]{2,1,0:T(1,128)} %bitcast.34), calls=%async_computation.9 | async-start | bytes 65536 | tf_op jit(solution)/shard_map/all_to_all | solution.py:27
  264.4 8.8 %all-to-all-done.9 = f32[64,1,128]{2,1,0:T(1,128)S(1)} async-done(((f32[64,1,128]{2,1,0:T(1,128)}), f32[64,1,128]{2,1,0:T(1,128)S(1)}, u32[]{:S(2)}, u32[]{:S(2)}) %all-to-all-start.9) | async-done | bytes 32800 | tf_op jit(solution)/shard_map/all_to_all | solution.py:27
  (86 shorter events, 10.2 us)
Async XLA Ops:
  0.6 3.1 %copy-start = (bf16[16,1,128,128]{3,2,1,0:T(8,128)(2,1)S(1)}, bf16[16,1,128,128]{3,2,1,0:T(8,128)(2,1)}, u32[]{:S(2)}) copy-start(bf16[16,1,128,128]{3,2,1,0:T(8,128)(2,1)} %param.21) | copy-start | bytes 1572868
  6.5 32.3 %all-to-all-start = ((bf16[8,16,768]{2,1,0:T(8,128)(2,1)}), bf16[8,16,768]{2,1,0:T(8,128)(2,1)S(1)}, u32[]{:S(2)}, u32[]{:S(2)}) async-start(bf16[8,16,768]{2,1,0:T(8,128)(2,1)} %broadcast_in_dim.26), calls=%async_computation | async-start | bytes 393216 | tf_op jit(solution)/shard_map/all_to_all | solution.py:27
  18.1 11.1 %collective-permute-start = (bf16[784,192]{1,0:T(8,128)(2,1)S(1)}, bf16[784,192]{1,0:T(8,128)(2,1)S(1)}, u32[]{:S(2)}, u32[]{:S(2)}) collective-permute-start(bf16[784,192]{1,0:T(8,128)(2,1)S(1)} %get-tuple-element.55), channel_id=1, source_target_pairs={{0,64},{64,128},{128,192},{192,0},{1,65},{65,129},{129,193},{193,1... | collective-permute-start | bytes 903176 | tf_op jit(solution)/shard_map/ppermute | solution.py:352
  19.4 19.4 %collective-permute-start.1 = (bf16[784,192]{1,0:T(8,128)(2,1)S(1)}, bf16[784,192]{1,0:T(8,128)(2,1)S(1)}, u32[]{:S(2)}, u32[]{:S(2)}) collective-permute-start(bf16[784,192]{1,0:T(8,128)(2,1)S(1)} %get-tuple-element.56), channel_id=1, source_target_pairs={{0,128},{64,192},{128,0},{192,64},{1,129},{65,193},{129,1},{193,65... | collective-permute-start | bytes 903176 | tf_op jit(solution)/shard_map/ppermute | solution.py:352
  21.8 17.0 %collective-permute-start.2 = (bf16[784,192]{1,0:T(8,128)(2,1)S(1)}, bf16[784,192]{1,0:T(8,128)(2,1)S(1)}, u32[]{:S(2)}, u32[]{:S(2)}) collective-permute-start(bf16[784,192]{1,0:T(8,128)(2,1)S(1)} %get-tuple-element.54), channel_id=1, source_target_pairs={{0,192},{64,0},{128,64},{192,128},{1,193},{65,1},{129,65},{193,129... | collective-permute-start | bytes 903176 | tf_op jit(solution)/shard_map/ppermute | solution.py:352
  40.5 13.4 %copy-start.8 = (f32[6144]{0:T(1024)S(1)}, f32[6144]{0:T(1024)}, u32[]{:S(2)}) copy-start(f32[6144]{0:T(1024)} %param.27) | copy-start | bytes 73732
  40.5 21.6 %all-to-all-start.1 = ((bf16[8,16,768]{2,1,0:T(8,128)(2,1)}), bf16[8,16,768]{2,1,0:T(8,128)(2,1)S(1)}, u32[]{:S(2)}, u32[]{:S(2)}) async-start(bf16[8,16,768]{2,1,0:T(8,128)(2,1)} %get-tuple-element.22), calls=%async_computation.1 | async-start | bytes 393216 | tf_op jit(solution)/shard_map/all_to_all | solution.py:27
  47.0 6.9 %copy-start.6 = (bf16[1,6144,256]{2,1,0:T(8,128)(2,1)S(1)}, bf16[1,6144,256]{2,1,0:T(8,128)(2,1)}, u32[]{:S(2)}) copy-start(bf16[1,6144,256]{2,1,0:T(8,128)(2,1)} %param.29) | copy-start | bytes 9437188
  48.4 21.1 %collective-permute-start.3 = (bf16[2,768,128]{2,1,0:T(8,128)(2,1)S(1)}, bf16[2,768,128]{2,1,0:T(8,128)(2,1)S(1)}, u32[]{:S(2)}, u32[]{:S(2)}) collective-permute-start(bf16[2,768,128]{2,1,0:T(8,128)(2,1)S(1)} %get-tuple-element.53), channel_id=1, source_target_pairs={{0,128},{64,192},{128,0},{192,64},{1,129},{65,193},{129,1},{193,65... | collective-permute-start | bytes 1179656 | tf_op jit(solution)/shard_map/ppermute | solution.py:368
  53.6 5.0 %copy-start.7 = (bf16[6144,8]{0,1:T(8,128)(2,1)S(1)}, bf16[6144,8]{0,1:T(8,128)(2,1)}, u32[]{:S(2)}) copy-start(bf16[6144,8]{0,1:T(8,128)(2,1)} %param.26) | copy-start | bytes 294916
  53.6 5.0 %copy-start.9 = (s32[512,2]{0,1:T(2,128)S(1)}, s32[512,2]{0,1:T(2,128)}, u32[]{:S(2)}) copy-start(s32[512,2]{0,1:T(2,128)} %param.31) | copy-start | bytes 12292
  53.6 24.7 %collective-permute-start.6 = (bf16[256,3072]{1,0:T(8,128)(2,1)}, bf16[256,3072]{1,0:T(8,128)(2,1)}, u32[]{:S(2)}, u32[]{:S(2)}) collective-permute-start(bf16[256,3072]{1,0:T(8,128)(2,1)} %dynamic-slice_bitcast_fusion), channel_id=1, source_target_pairs={{0,1},{1,0},{2,3},{3,2},{4,5},{5,4},{6,7},{7,6},{8,9},{9,8},{10,11... | collective-permute-start | bytes 4718600 | tf_op jit(solution)/shard_map/ppermute | solution.py:23
  59.0 11.9 %collective-permute-start.4 = (bf16[2,768,128]{2,1,0:T(8,128)(2,1)S(1)}, bf16[2,768,128]{2,1,0:T(8,128)(2,1)}, u32[]{:S(2)}, u32[]{:S(2)}) collective-permute-start(bf16[2,768,128]{2,1,0:T(8,128)(2,1)S(1)} %get-tuple-element.52), channel_id=1, source_target_pairs={{0,64},{64,128},{128,192},{192,0},{1,65},{65,129},{129,193},{193,1... | collective-permute-start | bytes 1179656 | tf_op jit(solution)/shard_map/ppermute | solution.py:368
  59.2 11.7 %collective-permute-start.5 = (bf16[2,768,128]{2,1,0:T(8,128)(2,1)S(1)}, bf16[2,768,128]{2,1,0:T(8,128)(2,1)}, u32[]{:S(2)}, u32[]{:S(2)}) collective-permute-start(bf16[2,768,128]{2,1,0:T(8,128)(2,1)S(1)} %get-tuple-element.51), channel_id=1, source_target_pairs={{0,192},{64,0},{128,64},{192,128},{1,193},{65,1},{129,65},{193,129... | collective-permute-start | bytes 1179656 | tf_op jit(solution)/shard_map/ppermute | solution.py:368
  62.9 15.4 %all-to-all-start.2 = ((bf16[8,16,768]{2,1,0:T(8,128)(2,1)}), bf16[8,16,768]{2,1,0:T(8,128)(2,1)S(1)}, u32[]{:S(2)}, u32[]{:S(2)}) async-start(bf16[8,16,768]{2,1,0:T(8,128)(2,1)} %broadcast_in_dim.27), calls=%async_computation.2 | async-start | bytes 393216 | tf_op jit(solution)/shard_map/all_to_all | solution.py:27
  78.6 45.5 %copy-start.1 = (bf16[6144,256]{1,0:T(8,128)(2,1)S(1)}, bf16[6144,256]{1,0:T(8,128)(2,1)}, u32[]{:S(2)}) copy-start(bf16[6144,256]{1,0:T(8,128)(2,1)} %get-tuple-element.32) | copy-start | bytes 9437188
  78.6 45.5 %copy-start.2 = (bf16[6144,256]{1,0:T(8,128)(2,1)S(1)}, bf16[6144,256]{1,0:T(8,128)(2,1)}, u32[]{:S(2)}) copy-start(bf16[6144,256]{1,0:T(8,128)(2,1)} %get-tuple-element.31) | copy-start | bytes 9437188
  119.5 9.2 %copy-start.3 = (bf16[16,8,16,768]{3,2,1,0:T(8,128)(2,1)}, bf16[16,8,16,768]{3,2,1,0:T(8,128)(2,1)S(1)}, u32[]{:S(2)}) copy-start(bf16[16,8,16,768]{3,2,1,0:T(8,128)(2,1)S(1)} %all_to_all.57.state) | copy-start | bytes 9437188
  119.5 9.9 %collective-permute-start.7 = (bf16[16,8,16,768]{3,2,1,0:T(8,128)(2,1)S(1)}, bf16[16,8,16,768]{3,2,1,0:T(8,128)(2,1)S(1)}, u32[]{:S(2)}, u32[]{:S(2)}) collective-permute-start(bf16[16,8,16,768]{3,2,1,0:T(8,128)(2,1)S(1)} %all_to_all.57.state), channel_id=1, source_target_pairs={{0,1},{1,0},{2,3},{3,2},{4,5},{5,4},{6,7},{7,6},{8,9},{9,8},{10,11... | collective-permute-start | bytes 9437192 | tf_op jit(solution)/shard_map/ppermute | solution.py:23
  128.7 6.7 %copy-start.4 = (bf16[1,256,6144]{2,1,0:T(8,128)(2,1)S(1)}, bf16[1,256,6144]{2,1,0:T(8,128)(2,1)}, u32[]{:S(2)}) copy-start(bf16[1,256,6144]{2,1,0:T(8,128)(2,1)} %param.30) | copy-start | bytes 9437188
  128.7 5.7 %collective-permute-start.9 = (bf16[256,256]{1,0:T(8,128)(2,1)S(1)}, bf16[256,256]{1,0:T(8,128)(2,1)S(1)}, u32[]{:S(2)}, u32[]{:S(2)}) collective-permute-start(bf16[256,256]{1,0:T(8,128)(2,1)S(1)} %experts.2.mine_own), channel_id=1, source_target_pairs={{0,1},{1,0},{2,3},{3,2},{4,5},{5,4},{6,7},{7,6},{8,9},{9,8},{10,11... | collective-permute-start | bytes 393224 | tf_op jit(solution)/shard_map/ppermute | solution.py:23
  129.4 4.6 %copy-start.5 = (bf16[16,8,16,768]{3,2,1,0:T(8,128)(2,1)}, bf16[16,8,16,768]{3,2,1,0:T(8,128)(2,1)S(1)}, u32[]{:S(2)}) copy-start(bf16[16,8,16,768]{3,2,1,0:T(8,128)(2,1)S(1)} %collective-permute-done.7.state) | copy-start | bytes 9437188
  133.9 1.4 collective-permute-start.8
  141.0 45.9 %all-to-all-start.4 = ((bf16[16,8,16,768]{3,2,1,0:T(8,128)(2,1)}), bf16[16,8,16,768]{3,2,1,0:T(8,128)(2,1)}, u32[]{:S(2)}, u32[]{:S(2)}) async-start(bf16[16,8,16,768]{3,2,1,0:T(8,128)(2,1)} %bitcast.115), calls=%async_computation.4 | async-start | bytes 6291456 | tf_op jit(solution)/shard_map/all_to_all | solution.py:27
  189.9 12.0 %all-to-all-start.5 = ((bf16[8,16,768]{2,1,0:T(8,128)(2,1)}), bf16[8,16,768]{2,1,0:T(8,128)(2,1)S(1)}, u32[]{:S(2)}, u32[]{:S(2)}) async-start(bf16[8,16,768]{2,1,0:T(8,128)(2,1)} %reduce_sum.59), calls=%async_computation.5 | async-start | bytes 393216 | tf_op jit(solution)/shard_map/all_to_all | solution.py:27
  226.2 7.3 %collective-permute-start.10 = (bf16[4,8,16,768]{3,2,1,0:T(8,128)(2,1)S(1)}, bf16[4,8,16,768]{3,2,1,0:T(8,128)(2,1)}, u32[]{:S(2)}, u32[]{:S(2)}) collective-permute-start(bf16[4,8,16,768]{3,2,1,0:T(8,128)(2,1)S(1)} %all_to_all.59.own), channel_id=1, source_target_pairs={{0,1},{1,0},{2,3},{3,2},{4,5},{5,4},{6,7},{7,6},{8,9},{9,8},{10,11... | collective-permute-start | bytes 2359304 | tf_op jit(solution)/shard_map/ppermute | solution.py:23
  234.4 39.2 %copy-start.10 = (f32[2]{0:T(128)S(1)}, f32[2]{0:T(128)}, u32[]{:S(2)}) copy-start(f32[2]{0:T(128)} %param.35) | copy-start | bytes 28
  237.4 19.1 %all-to-all-start.8 = ((bf16[4,144,640]{2,1,0:T(8,128)(2,1)}), bf16[4,144,640]{2,1,0:T(8,128)(2,1)S(1)}, u32[]{:S(2)}, u32[]{:S(2)}) async-start(bf16[4,144,640]{2,1,0:T(8,128)(2,1)} %head.1), calls=%async_computation.8 | async-start | bytes 1474560 | tf_op jit(solution)/shard_map/all_to_all | solution.py:27
  258.1 15.1 %all-to-all-start.9 = ((f32[64,1,128]{2,1,0:T(1,128)}), f32[64,1,128]{2,1,0:T(1,128)S(1)}, u32[]{:S(2)}, u32[]{:S(2)}) async-start(f32[64,1,128]{2,1,0:T(1,128)} %bitcast.34), calls=%async_computation.9 | async-start | bytes 65536 | tf_op jit(solution)/shard_map/all_to_all | solution.py:27

commit v5 on v4

--- a/solution.py
+++ b/solution.py
@@ -31,38 +31,103 @@
     return exchange(jnp.broadcast_to(value[None], (count,) + value.shape), axes)
 
 
+def attend_kernel(lengths, queries, new_keys, new_values, k_cache, v_cache, out):
+    rows, _, span, width = k_cache.shape
+    group = queries.shape[1] // width
+    total = group * rows
+    query = jnp.concatenate(
+        [queries[:, h * width : (h + 1) * width] for h in range(group)], axis=0
+    )
+    scale = width ** (-0.5)
+    keys = k_cache[...].reshape(rows * span, width)
+    scores = (
+        lax.dot_general(query, keys, (((1,), (1,)), ((), ())), preferred_element_type=F32) * scale
+    )
+    fresh_key = jnp.concatenate([new_keys[...].astype(F32)] * group, axis=0)
+    fresh = jnp.sum(query.astype(F32) * fresh_key, axis=1, keepdims=True) * scale
+    request = lax.broadcasted_iota(jnp.int32, (total, 1), 0) % rows
+    first = request * span
+    last = first
+    for r in range(rows):
+        last = jnp.where(request == r, r * span + lengths[r], last)
+    column = lax.broadcasted_iota(jnp.int32, scores.shape, 1)
+    scores = jnp.where((column >= first) & (column < last), scores, -1e30)
+    top = jnp.maximum(jnp.max(scores, axis=1, keepdims=True), fresh)
+    part = jnp.exp(scores - top)
+    part_fresh = jnp.exp(fresh - top)
+    sums = jnp.sum(part, axis=1, keepdims=True) + part_fresh
+    weight = (part / sums).astype(BF16)
+    weight_fresh = (part_fresh / sums).astype(BF16).astype(F32)
+    values = v_cache[...].reshape(rows * span, width)
+    result = jnp.dot(weight, values, preferred_element_type=F32)
+    fresh_value = jnp.concatenate([new_values[...].astype(F32)] * group, axis=0)
+    result = (result + weight_fresh * fresh_value).astype(BF16)
+    wide = jnp.concatenate([result[h * rows : (h + 1) * rows] for h in range(group)], axis=1)
+    for z in range(out.shape[0]):
+        out[z] = wide
+
+
 def attend(queries, new_keys, new_values, k_cache, v_cache, lengths):
-    rows, heads_kv, span, width = k_cache.shape
-    group = queries.shape[1] // (heads_kv * width)
-    query = queries.reshape(rows, heads_kv, group, width)
-    scale = width ** (-0.5)
-    cached = (
-        jnp.einsum("rkgd,rkld->rkgl", query, k_cache, preferred_element_type=F32) * scale
+    rows, width = queries.shape
+    vmem = pl.BlockSpec(memory_space=pltpu.VMEM)
+    return pl.pallas_call(
+        attend_kernel,
+        out_shape=pltpu.HBM((NZ, rows, width), BF16),
+        in_specs=[pl.BlockSpec(memory_space=pltpu.SMEM)] + [vmem] * 5,
+        out_specs=vmem,
+        compiler_params=pltpu.CompilerParams(vmem_limit_bytes=32 << 20),
+        cost_estimate=pl.CostEstimate(flops=2 << 34, bytes_accessed=2 << 20, transcendentals=0),
+        name="attend",
+    )(lengths, queries, new_keys, new_values, k_cache, v_cache)
+
+
+def pack_kernel(place, w_out, residual, *packs):
+    unit, depth = w_out.shape
+    rows = packs[0].shape[0] - unit
+    line = lax.broadcasted_iota(jnp.int32, (NX * rows, residual.shape[1]), 0)
+    target = lax.rem(place[2] + line // rows, NX)
+    wanted = (target * NY * NC + place[0]) * rows + line % rows
+    pick = lax.broadcasted_iota(jnp.int32, line.shape, 1) == wanted
+    parts = lax.dot_general(
+        pick.astype(F32).astype(BF16),
+        residual[...],
+        (((1,), (1,)), ((), ())),
+        preferred_element_type=F32,
     )
-    fresh_key = new_keys.reshape(rows, heads_kv, width)
-    fresh = jnp.einsum("rkgd,rkd->rkg", query, fresh_key, preferred_element_type=F32) * scale
-    live = jnp.arange(span, dtype=jnp.int32)[None, :] < lengths[:, None]
-    cached = jnp.where(live[:, None, None, :], cached, -1e30)
-    top = jnp.maximum(jnp.max(cached, axis=-1), fresh)
-    part_cached = jnp.exp(cached - top[..., None])
-    part_fresh = jnp.exp(fresh - top)
-    total = jnp.sum(part_cached, axis=-1) + part_fresh
-    weight_cached = (part_cached / total[..., None]).astype(BF16)
-    weight_fresh = (part_fresh / total).astype(BF16)
-    fresh_value = new_values.reshape(rows, heads_kv, 1, width).astype(F32)
-    out = jnp.einsum("rkgl,rkld->rkgd", weight_cached, v_cache, preferred_element_type=F32)
-    out = out + weight_fresh.astype(F32)[..., None] * fresh_value
-    return out.reshape(rows, group * heads_kv * width).astype(BF16)
+    for shift, pack in enumerate(packs):
+        part = parts[shift * rows : (shift + 1) * rows, :]
+        pack[:unit, :] = w_out[...]
+        pack[unit:, :] = jnp.concatenate(
+            [part, jnp.zeros((rows, depth - unit), F32)], axis=1
+        ).astype(BF16)
+
+
+def pack(place, w_out, residual, rows):
+    unit, depth = w_out.shape
+    shape = (unit + rows, depth)
+    vmem = pl.BlockSpec(memory_space=pltpu.VMEM)
+    return pl.pallas_call(
+        pack_kernel,
+        out_shape=[jax.ShapeDtypeStruct(shape, BF16)] + [pltpu.HBM(shape, BF16)] * (NX - 1),
+        in_specs=[pl.BlockSpec(memory_space=pltpu.SMEM), vmem, vmem],
+        out_specs=[vmem] * NX,
+        compiler_params=pltpu.CompilerParams(vmem_limit_bytes=32 << 20),
+        name="pack",
+    )(place, w_out, residual)
 
 
 def project_kernel(place, attended, *refs):
     packs, (partial, residual) = refs[:NX], refs[NX:]
     depth = attended.shape[-1]
     value = attended[...].reshape(-1, depth)
+    unit = residual.shape[1] // NX
     products = [
-        jnp.dot(value, pack[:depth, :], preferred_element_type=F32) for pack in packs
+        lax.dot_general(
+            value, pack[:unit, :], (((1,), (1,)), ((), ())), preferred_element_type=F32
+        )
+        for pack in packs
     ]
-    rows = [pack[depth:, :].astype(F32) for pack in packs]
+    rows = [pack[unit:, :].astype(F32)[:, :unit] for pack in packs]
     x = place[2]
 
     def order(parts):
@@ -80,8 +145,8 @@
 
 
 def project(place, attended, packs):
-    depth, unit = attended.shape[-1], packs[0].shape[1]
-    rows = packs[0].shape[0] - depth
+    _, rows, depth = attended.shape
+    unit = packs[0].shape[0] - rows
     vmem = pl.BlockSpec(memory_space=pltpu.VMEM)
     return pl.pallas_call(
         project_kernel,
@@ -339,25 +404,17 @@
     total_rows = residual.shape[0]
     part_rows = total_rows // (NX * NY * NC)
 
-    sends = []
-    for shift in range(NX):
-        target = (x + shift) % NX
-        rows = lax.dynamic_slice_in_dim(
-            residual, (target * NY * NC + expert) * part_rows, part_rows
-        )
-        sends.append(jnp.concatenate([w_out, rows], axis=0))
+    sends = pack(place, w_out.T, residual.T, part_rows)
+    *sends, queries = lax.optimization_barrier((*sends, queries))
     packs = [sends[0]]
     for shift in range(1, NX):
         pairs = [(i, (i + shift) % NX) for i in range(NX)]
         packs.append(lax.ppermute(sends[shift], "x", pairs))
-    depth = w_out.shape[0]
 
     attended = attend(queries, new_keys, new_values, k_cache, v_cache, lengths)
-    attended_x = spread(attended, "z", NZ)
+    attended_x = exchange(attended, "z")
     partial_heads, residual_here = project(place, attended_x, packs)
-    late = (partial_heads, expert_ids, w_vocab, w_gate, w_up, w_down, router)
-    late = lax.optimization_barrier(late)
-    partial_heads, expert_ids, w_vocab, w_gate, w_up, w_down, router = late
+    partial_heads, w_vocab = lax.optimization_barrier((partial_heads, w_vocab))
     half = width_all // NC
     slab = half // NX
     vocab_rows = w_vocab.reshape(NC, NX, slab, -1)
@@ -380,14 +437,15 @@
     head_own = lax.dynamic_index_in_dim(head_w, core, 0, keepdims=False)
     head_other = lax.dynamic_index_in_dim(head_w, 1 - core, 0, keepdims=False)
 
-    down_sent = lax.dynamic_slice_in_dim(w_down[0], (1 - core) * half, half, axis=1)
-    down_other = swap_cores(down_sent)
-
     pieces = exchange(partial_heads, EX)
     hidden = jnp.sum(pieces.astype(F32), axis=0) + residual_here.astype(F32)
     hidden = hidden.astype(BF16)
 
     hidden_z = spread(hidden, "z", NZ)
+    early = (hidden_z, head_own, head_other, expert_ids, w_gate, w_up, w_down, router)
+    early = lax.optimization_barrier(early)
+    hidden_z, head_own, head_other, expert_ids, w_gate, w_up, w_down, router = early
+    own = spread(hidden_z, XY, NXY)
     order = expert_ids.reshape(NXY, NC, part_rows, 2).transpose(1, 0, 2, 3)
     order = order.reshape(NC, -1, 2)
     order_own = lax.dynamic_index_in_dim(order, core, 0, keepdims=False)
@@ -398,11 +456,11 @@
     router_z = router_z.reshape(NZ, -1, NX * unit)
     gate_g = (w_gate[0].astype(F32) * gain_col).astype(BF16)
     up_g = (w_up[0].astype(F32) * gain_col).astype(BF16)
-    ready = (hidden_z, gate_g, up_g, router_z, order_own, order_other)
-    ready = lax.optimization_barrier(ready + (head_own, head_other, down_other))
-    hidden_z, gate_g, up_g, router_z, order_own, order_other = ready[:6]
-    head_own, head_other, down_other = ready[6:]
-    own = spread(hidden_z, XY, NXY)
+    down_sent = lax.dynamic_slice_in_dim(w_down[0], (1 - core) * half, half, axis=1)
+    down_other = swap_cores(down_sent)
+    ready = (own, gate_g, up_g, router_z, order_own, order_other, down_other)
+    ready = lax.optimization_barrier(ready)
+    own, gate_g, up_g, router_z, order_own, order_other, down_other = ready
     other = swap_cores(own)
 
     act_own = experts(place, own, gate_g, up_g, router_z, order_own)

time: 276 us -> 277 us (level)
  blocking collectives: 65.1 us -> 25.3 us
  waiting for transfers between devices: 91.6 us -> 123 us
  starting transfers between devices: 64.3 us -> 75.7 us
  other arithmetic: 14.3 us -> 9.09 us
  local copies, waits for them, and re-layouts: 14.9 us -> 18.6 us
    all_to_all x3 -> x2, blocking collectives: 65.1 us -> 25.3 us  [exchange(): return lax.all_to_all(value, axes, split_axis=0, concat_axis=0, tiled=True)]
    all_to_all x7 -> x8, waiting for transfers between devices: 73 us -> 100 us  [exchange(): return lax.all_to_all(value, axes, split_axis=0, concat_axis=0, tiled=True)]
    all_to_all x7 -> x8, starting transfers between devices: 43.5 us -> 55.8 us  [exchange(): return lax.all_to_all(value, axes, split_axis=0, concat_axis=0, tiled=True)]
    unnamed x29 -> x49, local copies, waits for them, and re-layouts: 1.5 us -> 9.83 us
    ppermute x3, waiting for transfers between devices: 1.33 us -> 7.71 us  [shards(): part = lax.ppermute(part, 'x', [(i, (i + shift) % NX) for i in range(NX)])]
    pallas_call x0 -> x2, Pallas kernels: none -> 3.82 us  [the longest x1 2.16 us: attend(): pl.pallas_call(attend_kernel, out_shape=pltpu.HBM((NZ, rows, width), BF16...]
  transfers between devices with their start and end apart: 18 -> 19, of which waited for: 11 -> 12; matrix products, arithmetic and copies ran while one was open for 7% -> 5% of each run, Pallas kernels for 3% -> 4%
where the time goes in v5:
time: 277 us; the launch traced here: 276 us
  waiting for transfers between devices  123 us (44%)
  starting transfers between devices  75.7 us (27%)
  blocking collectives  25.3 us (9%)
  Pallas kernels  22.6 us (8%)
  local copies, waits for them, and re-layouts  18.6 us (7%)
  other arithmetic  9.09 us (3%)
    all_to_all x8, waiting for transfers between devices, exchange(): return lax.all_to_all(value, axes, split_axis=0, concat_axis=0, tiled=True)  100 us
    all_to_all x8, starting transfers between devices, exchange(): return lax.all_to_all(value, axes, split_axis=0, concat_axis=0, tiled=True)  55.8 us
    all_to_all x2, blocking collectives, exchange(): return lax.all_to_all(value, axes, split_axis=0, concat_axis=0, tiled=True)  25.3 us
    ppermute x3, waiting for transfers between devices, shards(): packs.append(lax.ppermute(sends[shift], 'x', pairs))  12.5 us
    ppermute x5, starting transfers between devices, swap_cores(): return lax.ppermute(value, 'c', [(0, 1), (1, 0)])  9.95 us
    pallas_call x2, Pallas kernels, experts(): pl.pallas_call(expert_kernel, out_shape=jax.ShapeDtypeStruct((total, hidd...  9.87 us
    unnamed x49, local copies, waits for them, and re-layouts  9.83 us
    ppermute x3, waiting for transfers between devices, shards(): part = lax.ppermute(part, 'x', [(i, (i + shift) % NX) for i in range(NX)])  7.71 us
  transfers between devices with their start and end apart: 19, of which 12 were waited for; matrix products, arithmetic and copies ran while one was open for 5% of the time, Pallas kernels for 4%

profile of v5, /device:TPU:1, one launch (start us, length us, event | category | flops | bytes accessed | tf_op | source)
XLA Modules:
  0.0 275.9 jit_solution(10635086601693005539)
XLA Ops:
  0.7 1.0 copy-done.9
  1.7 0.9 copy-done.10
  2.6 1.7 pack.1
  4.3 1.0 copy-done.11
  5.3 1.0 copy-done.12
  9.1 2.2 attend.1
  11.3 9.1 %all-to-all-start = ((bf16[8,16,768]{2,1,0:T(8,128)(2,1)}), bf16[8,16,768]{2,1,0:T(8,128)(2,1)S(1)}, u32[]{:S(2)}, u32[]{:S(2)}) async-start(bf16[8,16,768]{2,1,0:T(8,128)(2,1)} %attend.1), calls=%async_computation | async-start | bytes 393216 | tf_op jit(solution)/shard_map/all_to_all | solution.py:27
  20.4 1.2 collective-permute-start
  21.7 2.4 collective-permute-start.1
  24.1 1.2 collective-permute-start.2
  25.3 4.6 %collective-permute-done.refs_1_ = bf16[208,768]{1,0:T(8,128)(2,1)S(1)} collective-permute-done((bf16[208,768]{1,0:T(8,128)(2,1)}, bf16[208,768]{1,0:T(8,128)(2,1)S(1)}, u32[]{:S(2)}, u32[]{:S(2)}) %collective-permute-start) | collective-permute-done | bytes 319520 | tf_op jit(solution)/shard_map/ppermute | solution.py:412
  29.9 7.8 %collective-permute-done.1.refs_2_ = bf16[208,768]{1,0:T(8,128)(2,1)S(1)} collective-permute-done((bf16[208,768]{1,0:T(8,128)(2,1)}, bf16[208,768]{1,0:T(8,128)(2,1)S(1)}, u32[]{:S(2)}, u32[]{:S(2)}) %collective-permute-start.1) | collective-permute-done | bytes 319520 | tf_op jit(solution)/shard_map/ppermute | solution.py:412
  37.8 1.8 project.1
  39.7 6.3 %all-to-all-start.1 = ((bf16[8,16,768]{2,1,0:T(8,128)(2,1)}), bf16[8,16,768]{2,1,0:T(8,128)(2,1)S(1)}, u32[]{:S(2)}, u32[]{:S(2)}) async-start(bf16[8,16,768]{2,1,0:T(8,128)(2,1)} %get-tuple-element.41), calls=%async_computation.1 | async-start | bytes 393216 | tf_op jit(solution)/shard_map/all_to_all | solution.py:27
  46.0 2.5 collective-permute-start.3
  48.7 2.5 collective-permute-start.5
  52.9 6.6 %all-to-all-start.2 = ((bf16[8,16,768]{2,1,0:T(8,128)(2,1)}), bf16[8,16,768]{2,1,0:T(8,128)(2,1)S(1)}, u32[]{:S(2)}, u32[]{:S(2)}) async-start(bf16[8,16,768]{2,1,0:T(8,128)(2,1)} %broadcast_in_dim.10), calls=%async_computation.2 | async-start | bytes 393216 | tf_op jit(solution)/shard_map/all_to_all | solution.py:27
  59.5 7.7 %collective-permute-done.4 = bf16[2,768,128]{2,1,0:T(8,128)(2,1)} collective-permute-done((bf16[2,768,128]{2,1,0:T(8,128)(2,1)S(1)}, bf16[2,768,128]{2,1,0:T(8,128)(2,1)}, u32[]{:S(2)}, u32[]{:S(2)}) %collective-permute-start.4) | collective-permute-done | bytes 393248 | tf_op jit(solution)/shard_map/ppermute | solution.py:425
  67.2 1.6 multiply_convert_fusion.3
  69.0 1.3 dynamic-slice_bitcast_fusion.1
  70.3 2.0 broadcast_in_dim.11
  72.4 6.3 %all-to-all-start.3 = ((bf16[16,8,16,768]{3,2,1,0:T(8,128)(2,1)}), bf16[16,8,16,768]{3,2,1,0:T(8,128)(2,1)}, u32[]{:S(2)}, u32[]{:S(2)}) async-start(bf16[16,8,16,768]{3,2,1,0:T(8,128)(2,1)} %broadcast_in_dim.11), calls=%async_computation.3 | async-start | bytes 6291456 | tf_op jit(solution)/shard_map/all_to_all | solution.py:27
  79.2 1.0 copy.44
  81.2 1.0 dynamic-slice_bitcast_fusion.6
  82.2 4.0 %fusion = (bf16[6144,256]{1,0:T(8,128)(2,1)S(1)}, bf16[6144,256]{1,0:T(8,128)(2,1)}) fusion(bf16[1,6144,256]{2,1,0:T(8,128)(2,1)S(1)} %copy-done.17, f32[6144]{0:T(1024)S(1)} %copy-done.20, bf16[1,6144,256]{2,1,0:T(8,128)(2,1)} %param.28), kind=kLoop, calls=%fused_computation.1 | loop fusion | flops 9437184 | bytes 12607488 | tf_op jit(solution)/shard_map/convert_element_type | solution.py:458
  86.2 1.1 copy-done.7
  87.3 31.8 %all-to-all-done.3.state = bf16[16,8,16,768]{3,2,1,0:T(8,128)(2,1)} async-done(((bf16[16,8,16,768]{3,2,1,0:T(8,128)(2,1)}), bf16[16,8,16,768]{3,2,1,0:T(8,128)(2,1)}, u32[]{:S(2)}, u32[]{:S(2)}) %all-to-all-start.3) | async-done | bytes 3145760 | tf_op jit(solution)/shard_map/all_to_all | solution.py:27
  119.2 2.8 %collective-permute-start.7 = (bf16[16,8,16,768]{3,2,1,0:T(8,128)(2,1)}, bf16[16,8,16,768]{3,2,1,0:T(8,128)(2,1)S(1)}, u32[]{:S(2)}, u32[]{:S(2)}) collective-permute-start(bf16[16,8,16,768]{3,2,1,0:T(8,128)(2,1)} %all-to-all-done.3.state), channel_id=1, source_target_pairs={{0,1},{1,0},{2,3},{3,2},{4,5},{5,4},{6,7},{7,6},{8,9},{9,8},{10,11... | collective-permute-start | bytes 9437192 | tf_op jit(solution)/shard_map/ppermute | solution.py:23
  121.9 1.9 copy-done.1
  123.8 5.3 %experts.2.mine_own = bf16[256,256]{1,0:T(8,128)(2,1)S(1)} custom-call(s32[3]{0:T(128)S(1)} %pad_add_fusion.place, bf16[16,8,16,768]{3,2,1,0:T(8,128)(2,1)} %all-to-all-done.3.state, bf16[4,8,192,256]{3,2,1,0:T(8,128)(2,1)S(1)} %bitcast.96, bf16[4,8,192,256]{3,2,1,0:T(8,128)(2,1)S(1)} %bitcast.94, bf16[8,8,768]{2,1,0:T(8,128)(2,1)S(1)} %reshape.81.router_w, ...), custom_call_target="tpu_custom_call" | custom-call | flops 1610612736 | bytes 10485760 | tf_op jit(solution)/shard_map/experts/pallas_call | solution.py:229
  129.5 4.6 %experts.3.mine_other = bf16[256,256]{1,0:T(8,128)(2,1)S(1)} custom-call(s32[3]{0:T(128)S(1)} %pad_add_fusion.place, bf16[16,8,16,768]{3,2,1,0:T(8,128)(2,1)S(1)} %collective-permute-done.7.state, bf16[4,8,192,256]{3,2,1,0:T(8,128)(2,1)S(1)} %bitcast.97, bf16[4,8,192,256]{3,2,1,0:T(8,128)(2,1)S(1)} %bitcast.95, bf16[8,8,768]{2,1,0:T(8,128)(2,1)S(1)} %reshape.81.router_w, ...), custom_call_target="tpu_custom_call" | custom-call | flops 1610612736 | bytes 10485760 | tf_op jit(solution)/shard_map/experts/pallas_call | solution.py:229
  134.6 1.0 collective-permute-done.8.theirs_own
  135.6 4.3 %down.1 = bf16[4,16,2,16,768]{4,3,2,1,0:T(8,128)(2,1)} custom-call(s32[3]{0:T(128)S(1)} %pad_add_fusion.place, bf16[256,256]{1,0:T(8,128)(2,1)S(1)} %experts.2.mine_own, bf16[256,256]{1,0:T(8,128)(2,1)S(1)} %experts.3.mine_other, bf16[256,256]{1,0:T(8,128)(2,1)S(1)} %collective-permute-done.8.theirs_own, ...), custom_call_target="tpu_custom_call" | custom-call | flops 1610612736 | bytes 7340032 | tf_op jit(solution)/shard_map/down/pallas_call | solution.py:287
  139.9 8.9 %all-to-all-start.4 = ((bf16[16,8,16,768]{3,2,1,0:T(8,128)(2,1)}), bf16[16,8,16,768]{3,2,1,0:T(8,128)(2,1)S(1)}, u32[]{:S(2)}, u32[]{:S(2)}) async-start(bf16[16,8,16,768]{3,2,1,0:T(8,128)(2,1)} %bitcast.102), calls=%async_computation.4 | async-start | bytes 6291456 | tf_op jit(solution)/shard_map/all_to_all | solution.py:27
  148.9 40.6 %all-to-all-done.4 = bf16[16,8,16,768]{3,2,1,0:T(8,128)(2,1)S(1)} async-done(((bf16[16,8,16,768]{3,2,1,0:T(8,128)(2,1)}), bf16[16,8,16,768]{3,2,1,0:T(8,128)(2,1)S(1)}, u32[]{:S(2)}, u32[]{:S(2)}) %all-to-all-start.4) | async-done | bytes 3145760 | tf_op jit(solution)/shard_map/all_to_all | solution.py:27
  189.4 1.1 reduce_sum.49
  190.6 6.8 %all-to-all-start.5 = ((bf16[8,16,768]{2,1,0:T(8,128)(2,1)}), bf16[8,16,768]{2,1,0:T(8,128)(2,1)S(1)}, u32[]{:S(2)}, u32[]{:S(2)}) async-start(bf16[8,16,768]{2,1,0:T(8,128)(2,1)} %reduce_sum.49), calls=%async_computation.5 | async-start | bytes 393216 | tf_op jit(solution)/shard_map/all_to_all | solution.py:27
  197.3 1.0 dynamic-slice_select_fusion
  198.7 7.4 %all-to-all-done.5 = bf16[8,16,768]{2,1,0:T(8,128)(2,1)S(1)} async-done(((bf16[8,16,768]{2,1,0:T(8,128)(2,1)}), bf16[8,16,768]{2,1,0:T(8,128)(2,1)S(1)}, u32[]{:S(2)}, u32[]{:S(2)}) %all-to-all-start.5) | async-done | bytes 196640 | tf_op jit(solution)/shard_map/all_to_all | solution.py:27
  206.1 11.1 %all_to_all.57 = bf16[8,16,768]{2,1,0:T(8,128)(2,1)S(1)} all-to-all(bf16[8,16,768]{2,1,0:T(8,128)(2,1)S(1)} %broadcast_in_dim.12), channel_id=1, replica_groups=mesh['x'=4,'z'=8,'y'=4,'c'=2] {'z'}, dimensions={0} | all-to-all | bytes 393216 | tf_op jit(solution)/shard_map/all_to_all | solution.py:27
  217.3 14.2 %all_to_all.58.own = bf16[4,8,16,768]{3,2,1,0:T(8,128)(2,1)S(1)} all-to-all(bf16[4,8,16,768]{3,2,1,0:T(8,128)(2,1)S(1)} %broadcast_in_dim.13), channel_id=1, replica_groups=mesh['x'=4,'z'=8,'y'=4,'c'=2] {'y'}, dimensions={0} | all-to-all | bytes 1572864 | tf_op jit(solution)/shard_map/all_to_all | solution.py:27
  231.5 5.5 %collective-permute-start.10 = (bf16[4,8,16,768]{3,2,1,0:T(8,128)(2,1)S(1)}, bf16[4,8,16,768]{3,2,1,0:T(8,128)(2,1)S(1)}, u32[]{:S(2)}, u32[]{:S(2)}) collective-permute-start(bf16[4,8,16,768]{3,2,1,0:T(8,128)(2,1)S(1)} %all_to_all.58.own), channel_id=1, source_target_pairs={{0,1},{1,0},{2,3},{3,2},{4,5},{5,4},{6,7},{7,6},{8,9},{9,8},{10,11... | collective-permute-start | bytes 2359304 | tf_op jit(solution)/shard_map/ppermute | solution.py:23
  237.0 1.9 collective-permute-done.10.other
  239.1 1.9 head.1
  240.9 6.3 %all-to-all-start.8 = ((bf16[4,144,640]{2,1,0:T(8,128)(2,1)}), bf16[4,144,640]{2,1,0:T(8,128)(2,1)S(1)}, u32[]{:S(2)}, u32[]{:S(2)}) async-start(bf16[4,144,640]{2,1,0:T(8,128)(2,1)} %head.1), calls=%async_computation.8 | async-start | bytes 1474560 | tf_op jit(solution)/shard_map/all_to_all | solution.py:27
  247.5 10.9 %all-to-all-done.8.parts = bf16[4,144,640]{2,1,0:T(8,128)(2,1)S(1)} async-done(((bf16[4,144,640]{2,1,0:T(8,128)(2,1)}), bf16[4,144,640]{2,1,0:T(8,128)(2,1)S(1)}, u32[]{:S(2)}, u32[]{:S(2)}) %all-to-all-start.8) | async-done | bytes 737312 | tf_op jit(solution)/shard_map/all_to_all | solution.py:27
  260.0 5.5 %all-to-all-start.9 = ((f32[64,1,128]{2,1,0:T(1,128)}), f32[64,1,128]{2,1,0:T(1,128)S(1)}, u32[]{:S(2)}, u32[]{:S(2)}) async-start(f32[64,1,128]{2,1,0:T(1,128)} %bitcast.31), calls=%async_computation.9 | async-start | bytes 65536 | tf_op jit(solution)/shard_map/all_to_all | solution.py:27
  266.2 8.8 %all-to-all-done.9 = f32[64,1,128]{2,1,0:T(1,128)S(1)} async-done(((f32[64,1,128]{2,1,0:T(1,128)}), f32[64,1,128]{2,1,0:T(1,128)S(1)}, u32[]{:S(2)}, u32[]{:S(2)}) %all-to-all-start.9) | async-done | bytes 32800 | tf_op jit(solution)/shard_map/all_to_all | solution.py:27
  (97 shorter events, 11.3 us)
Async XLA Ops:
  0.6 246.6 %copy-start = (s32[512]{0:T(512)S(1)}, s32[512]{0:T(512)}, u32[]{:S(2)}) copy-start(s32[512]{0:T(512)} %param.34) | copy-start | bytes 6148
  0.7 1.0 copy-start.9
  1.7 0.9 copy-start.10
  4.3 1.0 copy-start.11
  5.3 1.0 copy-start.12
  6.4 0.7 copy-start.13
  7.1 0.7 copy-start.14
  7.8 0.7 copy-start.15
  8.5 0.7 copy-start.16
  9.1 16.1 %copy-start.21 = (f32[6144]{0:T(1024)S(1)}, f32[6144]{0:T(1024)}, u32[]{:S(2)}) copy-start(f32[6144]{0:T(1024)} %param.32) | copy-start | bytes 73732
  11.3 34.7 %copy-start.18 = (bf16[6144,128]{1,0:T(8,128)(2,1)S(1)}, bf16[6144,128]{1,0:T(8,128)(2,1)}, u32[]{:S(2)}) copy-start(bf16[6144,128]{1,0:T(8,128)(2,1)} %param.33) | copy-start | bytes 4718596
  11.3 26.5 %all-to-all-start = ((bf16[8,16,768]{2,1,0:T(8,128)(2,1)}), bf16[8,16,768]{2,1,0:T(8,128)(2,1)S(1)}, u32[]{:S(2)}, u32[]{:S(2)}) async-start(bf16[8,16,768]{2,1,0:T(8,128)(2,1)} %attend.1), calls=%async_computation | async-start | bytes 393216 | tf_op jit(solution)/shard_map/all_to_all | solution.py:27
  20.4 9.5 %collective-permute-start = (bf16[208,768]{1,0:T(8,128)(2,1)}, bf16[208,768]{1,0:T(8,128)(2,1)S(1)}, u32[]{:S(2)}, u32[]{:S(2)}) collective-permute-start(bf16[208,768]{1,0:T(8,128)(2,1)} %get-tuple-element.37), channel_id=1, source_target_pairs={{0,64},{64,128},{128,192},{192,0},{1,65},{65,129},{129,193},{193,1... | collective-permute-start | bytes 958472 | tf_op jit(solution)/shard_map/ppermute | solution.py:412
  21.7 16.1 %collective-permute-start.1 = (bf16[208,768]{1,0:T(8,128)(2,1)}, bf16[208,768]{1,0:T(8,128)(2,1)S(1)}, u32[]{:S(2)}, u32[]{:S(2)}) collective-permute-start(bf16[208,768]{1,0:T(8,128)(2,1)} %get-tuple-element.38), channel_id=1, source_target_pairs={{0,128},{64,192},{128,0},{192,64},{1,129},{65,193},{129,1},{193,65... | collective-permute-start | bytes 958472 | tf_op jit(solution)/shard_map/ppermute | solution.py:412
  24.1 13.7 %collective-permute-start.2 = (bf16[208,768]{1,0:T(8,128)(2,1)}, bf16[208,768]{1,0:T(8,128)(2,1)S(1)}, u32[]{:S(2)}, u32[]{:S(2)}) collective-permute-start(bf16[208,768]{1,0:T(8,128)(2,1)} %get-tuple-element.39), channel_id=1, source_target_pairs={{0,192},{64,0},{128,64},{192,128},{1,193},{65,1},{129,65},{193,129... | collective-permute-start | bytes 958472 | tf_op jit(solution)/shard_map/ppermute | solution.py:412
  39.7 12.5 %all-to-all-start.1 = ((bf16[8,16,768]{2,1,0:T(8,128)(2,1)}), bf16[8,16,768]{2,1,0:T(8,128)(2,1)S(1)}, u32[]{:S(2)}, u32[]{:S(2)}) async-start(bf16[8,16,768]{2,1,0:T(8,128)(2,1)} %get-tuple-element.41), calls=%async_computation.1 | async-start | bytes 393216 | tf_op jit(solution)/shard_map/all_to_all | solution.py:27
  46.0 13.5 %collective-permute-start.3 = (bf16[2,768,128]{2,1,0:T(8,128)(2,1)S(1)}, bf16[2,768,128]{2,1,0:T(8,128)(2,1)S(1)}, u32[]{:S(2)}, u32[]{:S(2)}) collective-permute-start(bf16[2,768,128]{2,1,0:T(8,128)(2,1)S(1)} %get-tuple-element.73), channel_id=1, source_target_pairs={{0,128},{64,192},{128,0},{192,64},{1,129},{65,193},{129,1},{193,65... | collective-permute-start | bytes 1179656 | tf_op jit(solution)/shard_map/ppermute | solution.py:425
  48.5 18.7 %collective-permute-start.4 = (bf16[2,768,128]{2,1,0:T(8,128)(2,1)S(1)}, bf16[2,768,128]{2,1,0:T(8,128)(2,1)}, u32[]{:S(2)}, u32[]{:S(2)}) collective-permute-start(bf16[2,768,128]{2,1,0:T(8,128)(2,1)S(1)} %get-tuple-element.72), channel_id=1, source_target_pairs={{0,64},{64,128},{128,192},{192,0},{1,65},{65,129},{129,193},{193,1... | collective-permute-start | bytes 1179656 | tf_op jit(solution)/shard_map/ppermute | solution.py:425
  48.7 18.5 %collective-permute-start.5 = (bf16[2,768,128]{2,1,0:T(8,128)(2,1)S(1)}, bf16[2,768,128]{2,1,0:T(8,128)(2,1)}, u32[]{:S(2)}, u32[]{:S(2)}) collective-permute-start(bf16[2,768,128]{2,1,0:T(8,128)(2,1)S(1)} %get-tuple-element.71), channel_id=1, source_target_pairs={{0,192},{64,0},{128,64},{192,128},{1,193},{65,1},{129,65},{193,129... | collective-permute-start | bytes 1179656 | tf_op jit(solution)/shard_map/ppermute | solution.py:425
  52.9 17.5 %all-to-all-start.2 = ((bf16[8,16,768]{2,1,0:T(8,128)(2,1)}), bf16[8,16,768]{2,1,0:T(8,128)(2,1)S(1)}, u32[]{:S(2)}, u32[]{:S(2)}) async-start(bf16[8,16,768]{2,1,0:T(8,128)(2,1)} %broadcast_in_dim.10), calls=%async_computation.2 | async-start | bytes 393216 | tf_op jit(solution)/shard_map/all_to_all | solution.py:27
  72.3 6.3 %copy-start.19 = (bf16[6144,8]{0,1:T(8,128)(2,1)S(1)}, bf16[6144,8]{0,1:T(8,128)(2,1)}, u32[]{:S(2)}) copy-start(bf16[6144,8]{0,1:T(8,128)(2,1)} %param.26) | copy-start | bytes 294916
  72.3 6.3 %copy-start.20 = (f32[6144]{0:T(1024)S(1)}, f32[6144]{0:T(1024)}, u32[]{:S(2)}) copy-start(f32[6144]{0:T(1024)} %param.27) | copy-start | bytes 73732
  72.3 6.7 %copy-start.22 = (s32[512,2]{0,1:T(2,128)S(1)}, s32[512,2]{0,1:T(2,128)}, u32[]{:S(2)}) copy-start(s32[512,2]{0,1:T(2,128)} %param.31) | copy-start | bytes 12292
  72.3 7.8 %copy-start.2 = (bf16[1,256,6144]{2,1,0:T(8,128)(2,1)S(1)}, bf16[1,256,6144]{2,1,0:T(8,128)(2,1)}, u32[]{:S(2)}) copy-start(bf16[1,256,6144]{2,1,0:T(8,128)(2,1)} %param.30) | copy-start | bytes 9437188
  72.4 46.8 %all-to-all-start.3 = ((bf16[16,8,16,768]{3,2,1,0:T(8,128)(2,1)}), bf16[16,8,16,768]{3,2,1,0:T(8,128)(2,1)}, u32[]{:S(2)}, u32[]{:S(2)}) async-start(bf16[16,8,16,768]{3,2,1,0:T(8,128)(2,1)} %broadcast_in_dim.11), calls=%async_computation.3 | async-start | bytes 6291456 | tf_op jit(solution)/shard_map/all_to_all | solution.py:27
  80.2 2.0 copy-start.17
  80.3 5.9 %collective-permute-start.6 = (bf16[256,3072]{1,0:T(8,128)(2,1)S(1)}, bf16[256,3072]{1,0:T(8,128)(2,1)S(1)}, u32[]{:S(2)}, u32[]{:S(2)}) collective-permute-start(bf16[256,3072]{1,0:T(8,128)(2,1)S(1)} %dynamic-slice_bitcast_fusion), channel_id=1, source_target_pairs={{0,1},{1,0},{2,3},{3,2},{4,5},{5,4},{6,7},{7,6},{8,9},{9,8},{10,11... | collective-permute-start | bytes 4718600 | tf_op jit(solution)/shard_map/ppermute | solution.py:23
  86.2 1.1 copy-start.7
  119.2 10.3 %collective-permute-start.7 = (bf16[16,8,16,768]{3,2,1,0:T(8,128)(2,1)}, bf16[16,8,16,768]{3,2,1,0:T(8,128)(2,1)S(1)}, u32[]{:S(2)}, u32[]{:S(2)}) collective-permute-start(bf16[16,8,16,768]{3,2,1,0:T(8,128)(2,1)} %all-to-all-done.3.state), channel_id=1, source_target_pairs={{0,1},{1,0},{2,3},{3,2},{4,5},{5,4},{6,7},{7,6},{8,9},{9,8},{10,11... | collective-permute-start | bytes 9437192 | tf_op jit(solution)/shard_map/ppermute | solution.py:23
  121.9 1.9 copy-start.1
  129.2 6.4 %copy-start.3 = (bf16[1,256,6144]{2,1,0:T(8,128)(2,1)S(1)}, bf16[1,256,6144]{2,1,0:T(8,128)(2,1)}, u32[]{:S(2)}) copy-start(bf16[1,256,6144]{2,1,0:T(8,128)(2,1)} %param.30) | copy-start | bytes 9437188
  129.2 6.4 %copy-start.8 = (bf16[256,3072]{1,0:T(8,128)(2,1)S(1)}, bf16[256,3072]{1,0:T(8,128)(2,1)}, u32[]{:S(2)}) copy-start(bf16[256,3072]{1,0:T(8,128)(2,1)} %copy-done.7) | copy-start | bytes 4718596
  129.2 5.4 %collective-permute-start.9 = (bf16[256,256]{1,0:T(8,128)(2,1)S(1)}, bf16[256,256]{1,0:T(8,128)(2,1)S(1)}, u32[]{:S(2)}, u32[]{:S(2)}) collective-permute-start(bf16[256,256]{1,0:T(8,128)(2,1)S(1)} %experts.2.mine_own), channel_id=1, source_target_pairs={{0,1},{1,0},{2,3},{3,2},{4,5},{5,4},{6,7},{7,6},{8,9},{9,8},{10,11... | collective-permute-start | bytes 393224 | tf_op jit(solution)/shard_map/ppermute | solution.py:23
  129.5 4.6 %copy-start.4 = (bf16[16,8,16,768]{3,2,1,0:T(8,128)(2,1)}, bf16[16,8,16,768]{3,2,1,0:T(8,128)(2,1)S(1)}, u32[]{:S(2)}) copy-start(bf16[16,8,16,768]{3,2,1,0:T(8,128)(2,1)S(1)} %collective-permute-done.7.state) | copy-start | bytes 9437188
  134.0 1.6 collective-permute-start.8
  139.9 49.5 %all-to-all-start.4 = ((bf16[16,8,16,768]{3,2,1,0:T(8,128)(2,1)}), bf16[16,8,16,768]{3,2,1,0:T(8,128)(2,1)S(1)}, u32[]{:S(2)}, u32[]{:S(2)}) async-start(bf16[16,8,16,768]{3,2,1,0:T(8,128)(2,1)} %bitcast.102), calls=%async_computation.4 | async-start | bytes 6291456 | tf_op jit(solution)/shard_map/all_to_all | solution.py:27
  190.6 48.5 %copy-start.5 = (bf16[768,512]{1,0:T(8,128)(2,1)S(1)}, bf16[768,512]{1,0:T(8,128)(2,1)}, u32[]{:S(2)}) copy-start(bf16[768,512]{1,0:T(8,128)(2,1)} %get-tuple-element.58.w_other) | copy-start | bytes 2359300
  190.6 48.5 %copy-start.6 = (bf16[768,512]{1,0:T(8,128)(2,1)S(1)}, bf16[768,512]{1,0:T(8,128)(2,1)}, u32[]{:S(2)}) copy-start(bf16[768,512]{1,0:T(8,128)(2,1)} %get-tuple-element.57.w_own) | copy-start | bytes 2359300
  190.6 15.5 %all-to-all-start.5 = ((bf16[8,16,768]{2,1,0:T(8,128)(2,1)}), bf16[8,16,768]{2,1,0:T(8,128)(2,1)S(1)}, u32[]{:S(2)}, u32[]{:S(2)}) async-start(bf16[8,16,768]{2,1,0:T(8,128)(2,1)} %reduce_sum.49), calls=%async_computation.5 | async-start | bytes 393216 | tf_op jit(solution)/shard_map/all_to_all | solution.py:27
  231.5 7.4 %collective-permute-start.10 = (bf16[4,8,16,768]{3,2,1,0:T(8,128)(2,1)S(1)}, bf16[4,8,16,768]{3,2,1,0:T(8,128)(2,1)S(1)}, u32[]{:S(2)}, u32[]{:S(2)}) collective-permute-start(bf16[4,8,16,768]{3,2,1,0:T(8,128)(2,1)S(1)} %all_to_all.58.own), channel_id=1, source_target_pairs={{0,1},{1,0},{2,3},{3,2},{4,5},{5,4},{6,7},{7,6},{8,9},{9,8},{10,11... | collective-permute-start | bytes 2359304 | tf_op jit(solution)/shard_map/ppermute | solution.py:23
  239.0 36.3 %copy-start.23 = (f32[2]{0:T(128)S(1)}, f32[2]{0:T(128)}, u32[]{:S(2)}) copy-start(f32[2]{0:T(128)} %param.35) | copy-start | bytes 28
  240.9 17.5 %all-to-all-start.8 = ((bf16[4,144,640]{2,1,0:T(8,128)(2,1)}), bf16[4,144,640]{2,1,0:T(8,128)(2,1)S(1)}, u32[]{:S(2)}, u32[]{:S(2)}) async-start(bf16[4,144,640]{2,1,0:T(8,128)(2,1)} %head.1), calls=%async_computation.8 | async-start | bytes 1474560 | tf_op jit(solution)/shard_map/all_to_all | solution.py:27
  260.0 15.0 %all-to-all-start.9 = ((f32[64,1,128]{2,1,0:T(1,128)}), f32[64,1,128]{2,1,0:T(1,128)S(1)}, u32[]{:S(2)}, u32[]{:S(2)}) async-start(f32[64,1,128]{2,1,0:T(1,128)} %bitcast.31), calls=%async_computation.9 | async-start | bytes 65536 | tf_op jit(solution)/shard_map/all_to_all | solution.py:27

commit v6 on v5

--- a/solution.py
+++ b/solution.py
@@ -17,6 +17,10 @@
 XY = ("x", "y")
 EX = ("y", "c")
 ALL = ("x", "z", "y", "c")
+
+
+def whole(shape):
+    return pl.BlockSpec(shape, lambda *_: (0,) * len(shape))
 
 
 def swap_cores(value):
@@ -69,16 +73,17 @@
 
 def attend(queries, new_keys, new_values, k_cache, v_cache, lengths):
     rows, width = queries.shape
-    vmem = pl.BlockSpec(memory_space=pltpu.VMEM)
+    arrays = (queries, new_keys, new_values, k_cache, v_cache)
     return pl.pallas_call(
         attend_kernel,
         out_shape=pltpu.HBM((NZ, rows, width), BF16),
-        in_specs=[pl.BlockSpec(memory_space=pltpu.SMEM)] + [vmem] * 5,
-        out_specs=vmem,
+        grid=(1,),
+        in_specs=[pl.BlockSpec(memory_space=pltpu.SMEM)] + [whole(a.shape) for a in arrays],
+        out_specs=whole((NZ, rows, width)),
         compiler_params=pltpu.CompilerParams(vmem_limit_bytes=32 << 20),
         cost_estimate=pl.CostEstimate(flops=2 << 34, bytes_accessed=2 << 20, transcendentals=0),
         name="attend",
-    )(lengths, queries, new_keys, new_values, k_cache, v_cache)
+    )(lengths, *arrays)
 
 
 def pack_kernel(place, w_out, residual, *packs):
@@ -105,12 +110,16 @@
 def pack(place, w_out, residual, rows):
     unit, depth = w_out.shape
     shape = (unit + rows, depth)
-    vmem = pl.BlockSpec(memory_space=pltpu.VMEM)
     return pl.pallas_call(
         pack_kernel,
         out_shape=[jax.ShapeDtypeStruct(shape, BF16)] + [pltpu.HBM(shape, BF16)] * (NX - 1),
-        in_specs=[pl.BlockSpec(memory_space=pltpu.SMEM), vmem, vmem],
-        out_specs=[vmem] * NX,
+        grid=(1,),
+        in_specs=[
+            pl.BlockSpec(memory_space=pltpu.SMEM),
+            whole(w_out.shape),
+            whole(residual.shape),
+        ],
+        out_specs=[whole(shape)] * NX,
         compiler_params=pltpu.CompilerParams(vmem_limit_bytes=32 << 20),
         name="pack",
     )(place, w_out, residual)
@@ -165,81 +174,82 @@
 
 
 def expert_kernel(
-    place, state, gate_w, up_w, router_w, ids, act, gate_sum, up_sum, route_sum, squares
+    place, own, other, gate_w, up_w, router_w, ids, act, gate_sum, up_sum, route_sum, squares
 ):
     step = pl.program_id(0)
-    width = state.shape[-1]
-    gate = up = route = square = 0.0
-    for block in range(state.shape[1]):
-        hidden = state[:, block].reshape(-1, width)
-        gate += jnp.dot(
-            hidden, gate_w[:, block].reshape(width, -1), preferred_element_type=F32
-        )
-        up += jnp.dot(hidden, up_w[:, block].reshape(width, -1), preferred_element_type=F32)
-        route += lax.dot_general(
-            hidden, router_w[block], (((1,), (1,)), ((), ())), preferred_element_type=F32
-        )
-        wide = hidden.astype(F32)
-        for start in range(0, width, 128):
-            piece = wide[:, start : start + 128]
-            square += piece * piece
+    width = own.shape[-1]
+
+    def products(state):
+        gate = up = route = square = 0.0
+        for block in range(state.shape[1]):
+            hidden = state[:, block].reshape(-1, width)
+            gate += jnp.dot(
+                hidden, gate_w[:, block].reshape(width, -1), preferred_element_type=F32
+            )
+            up += jnp.dot(hidden, up_w[:, block].reshape(width, -1), preferred_element_type=F32)
+            route += lax.dot_general(
+                hidden, router_w[block], (((1,), (1,)), ((), ())), preferred_element_type=F32
+            )
+            wide = hidden.astype(F32)
+            for start in range(0, width, 128):
+                piece = wide[:, start : start + 128]
+                square += piece * piece
+        return gate, up, route, square
 
     @pl.when(step == 0)
     def _():
-        gate_sum[...] = gate
-        up_sum[...] = up
-        route_sum[...] = route
-        squares[...] = square
-
-    @pl.when(step > 0)
+        gate_sum[...], up_sum[...], route_sum[...], squares[...] = products(own)
+
+    @pl.when(step == 1)
     def _():
-        gate_sum[...] += gate
-        up_sum[...] += up
-        route_sum[...] += route
-        squares[...] += square
-
-    @pl.when(step == pl.num_programs(0) - 1)
-    def _():
-        expert = place[0]
-        mean = jnp.sum(squares[...], axis=1, keepdims=True) / (width * NZ)
+        gate, up, route, square = products(other)
+        square += squares[...]
+        mean = jnp.sum(square, axis=1, keepdims=True) / (width * NZ)
         scale = lax.rsqrt(mean + EPS)
-        logits = route_sum[...] * scale
+        logits = (route + route_sum[...]) * scale
         lanes = lax.broadcasted_iota(jnp.int32, logits.shape, 1)
         first = ids[:, 0:1]
         second = ids[:, 1:2]
         first_logit = jnp.sum(jnp.where(lanes == first, logits, 0.0), axis=1, keepdims=True)
         second_logit = jnp.sum(jnp.where(lanes == second, logits, 0.0), axis=1, keepdims=True)
+        expert = place[0]
         is_first = first == expert
         gap = second_logit - first_logit
         weight = 1.0 / (1.0 + jnp.exp(jnp.where(is_first, gap, -gap)))
         weight = jnp.where(is_first | (second == expert), weight, 0.0)
-        gated = gate_sum[...] * scale
-        value = jax.nn.silu(gated) * (up_sum[...] * scale)
+        gated = (gate + gate_sum[...]) * scale
+        value = jax.nn.silu(gated) * ((up + up_sum[...]) * scale)
         act[...] = (weight * value).astype(BF16)
 
 
-def experts(place, state, gate_w, up_w, router_w, ids):
-    _, _, rows, width = state.shape
+def experts(place, own, other, gate_w, up_w, router_w, ids):
+    _, step, rows, width = own.shape
     total = NXY * rows
     hidden_units = gate_w.shape[-1]
     unit = width // NX
-    step = 4
-    weights = pl.BlockSpec((NX, step, unit, hidden_units), lambda z, p: (0, z, 0, 0))
     count = router_w.shape[1]
+
+    def half(s, p):
+        return p[1] + s - 2 * p[1] * s
+
+    weights = pl.BlockSpec(
+        (NX, step, unit, hidden_units), lambda s, p: (0, half(s, p), 0, 0)
+    )
     return pl.pallas_call(
         expert_kernel,
         out_shape=jax.ShapeDtypeStruct((total, hidden_units), BF16),
         grid_spec=pltpu.PrefetchScalarGridSpec(
             num_scalar_prefetch=1,
-            grid=(NZ // step,),
+            grid=(NC,),
             in_specs=[
-                pl.BlockSpec((NXY, step, rows, width), lambda z, p: (0, z, 0, 0)),
+                whole(own.shape),
+                whole(other.shape),
                 weights,
                 weights,
-                pl.BlockSpec((step, count, width), lambda z, p: (z, 0, 0)),
-                pl.BlockSpec((total, 2), lambda z, p: (0, 0)),
+                pl.BlockSpec((step, count, width), lambda s, p: (half(s, p), 0, 0)),
+                whole(ids.shape),
             ],
-            out_specs=pl.BlockSpec((total, hidden_units), lambda z, p: (0, 0)),
+            out_specs=whole((total, hidden_units)),
             scratch_shapes=[
                 pltpu.VMEM((total, hidden_units), F32),
                 pltpu.VMEM((total, hidden_units), F32),
@@ -258,7 +268,8 @@
         name="experts",
     )(
         place,
-        state,
+        own,
+        other,
         gate_w.reshape(NX, NZ, unit, hidden_units),
         up_w.reshape(NX, NZ, unit, hidden_units),
         router_w,
@@ -266,45 +277,38 @@
     )
 
 
-def down_kernel(
-    place, mine_own, mine_other, theirs_own, theirs_other, w_mine, w_theirs, out
-):
-    width = out.shape[-1]
-    core = place[1]
-    for mine, theirs, which in (
-        (mine_own, theirs_own, core),
-        (mine_other, theirs_other, 1 - core),
-    ):
-        total = jnp.dot(mine[...], w_mine[...], preferred_element_type=F32)
-        total += jnp.dot(theirs[...], w_theirs[...], preferred_element_type=F32)
-        out[0, :, pl.ds(which, 1), :, :] = total.astype(BF16).reshape(NXY, 1, -1, width)
-
-
-def down(place, acts, w_mine, w_theirs):
-    total, units = acts[0].shape
+def down_kernel(place, mine, theirs, w_mine, w_theirs, out):
+    total = jnp.dot(mine[...], w_mine[...], preferred_element_type=F32)
+    total += jnp.dot(theirs[...], w_theirs[...], preferred_element_type=F32)
+    out[0] = total.astype(BF16).reshape(out.shape[1:])
+
+
+def down(place, mine, theirs, w_mine, w_theirs):
+    total, units = mine.shape
     rows = total // NXY
     width = w_theirs.shape[1] // NX
     return pl.pallas_call(
         down_kernel,
-        out_shape=pltpu.HBM((NX, NXY, NC, rows, width), BF16),
+        out_shape=pltpu.HBM((NX, NXY, rows, width), BF16),
         grid_spec=pltpu.PrefetchScalarGridSpec(
             num_scalar_prefetch=1,
             grid=(NX,),
-            in_specs=[pl.BlockSpec((total, units), lambda x, p: (0, 0))] * 4
-            + [
+            in_specs=[
+                whole(mine.shape),
+                whole(theirs.shape),
                 pl.BlockSpec((units, width), lambda x, p: (0, p[1] * NX + x)),
                 pl.BlockSpec((units, width), lambda x, p: (0, x)),
             ],
-            out_specs=pl.BlockSpec((1, NXY, NC, rows, width), lambda x, p: (x, 0, 0, 0, 0)),
+            out_specs=pl.BlockSpec((1, NXY, rows, width), lambda x, p: (x, 0, 0, 0)),
         ),
         compiler_params=pltpu.CompilerParams(
             dimension_semantics=("arbitrary",), vmem_limit_bytes=32 << 20
         ),
         cost_estimate=pl.CostEstimate(
-            flops=8 * total * units * width * NX, bytes_accessed=7 << 20, transcendentals=0
+            flops=4 * total * units * width * NX, bytes_accessed=5 << 20, transcendentals=0
         ),
         name="down",
-    )(place, *acts, w_mine, w_theirs)
+    )(place, mine, theirs, w_mine, w_theirs)
 
 
 def head_kernel(own, other, w_own, w_other, below, out):
@@ -414,9 +418,49 @@
     attended = attend(queries, new_keys, new_values, k_cache, v_cache, lengths)
     attended_x = exchange(attended, "z")
     partial_heads, residual_here = project(place, attended_x, packs)
-    partial_heads, w_vocab = lax.optimization_barrier((partial_heads, w_vocab))
     half = width_all // NC
     slab = half // NX
+    pieces = exchange(partial_heads, EX)
+    hidden = jnp.sum(pieces.astype(F32), axis=0) + residual_here.astype(F32)
+    hidden = hidden.astype(BF16)
+
+    hidden_z = spread(hidden, "z", NZ)
+    depth_z = NZ // NC
+    near = lax.dynamic_slice_in_dim(hidden_z, core * depth_z, depth_z)
+    far = swap_cores(lax.dynamic_slice_in_dim(hidden_z, (1 - core) * depth_z, depth_z))
+    chunks = [jnp.where(core == k, near, far) for k in range(NC)]
+
+    early = (*chunks, expert_ids, w_gate, w_up, w_down, router)
+    early = lax.optimization_barrier(early)
+    chunks = list(early[:NC])
+    expert_ids, w_gate, w_up, w_down, router = early[NC:]
+    own = [spread(chunks[0], XY, NXY)]
+    order = expert_ids.reshape(NXY, NC, part_rows, 2).transpose(1, 0, 2, 3)
+    order = order.reshape(NC, -1, 2)
+    gain_col = gain_moe[:, None]
+    router_g = (router.astype(F32) * gain_col).astype(BF16)
+    router_z = router_g.T.reshape(-1, NX, NZ, unit).transpose(2, 0, 1, 3)
+    router_z = router_z.reshape(NZ, -1, NX * unit)
+    gate_g = (w_gate[0].astype(F32) * gain_col).astype(BF16)
+    up_g = (w_up[0].astype(F32) * gain_col).astype(BF16)
+    down_sent = lax.dynamic_slice_in_dim(w_down[0], (1 - core) * half, half, axis=1)
+    down_other = swap_cores(down_sent)
+    ready = (own[0], chunks[1], gate_g, up_g, router_z, order, down_other)
+    ready = lax.optimization_barrier(ready)
+    own[0], chunks[1], gate_g, up_g, router_z, order, down_other = ready
+    own.append(spread(chunks[1], XY, NXY))
+    other = []
+    sums = []
+    for k in range(NC):
+        other.append(swap_cores(own[k]))
+        act = experts(place, own[k], other[k], gate_g, up_g, router_z, order[k])
+        sent = down(place, act, swap_cores(act), w_down[0], down_other)
+        if k == 0:
+            own[1], sent = lax.optimization_barrier((own[1], sent))
+        sent = sent.reshape(NXY, NZ // NC, part_rows, slab)
+        sums.append(jnp.sum(exchange(sent, XY).astype(F32), axis=0).astype(BF16))
+    sums = jnp.stack(sums, axis=1).reshape(NZ, part_rows, slab)
+    sums, w_vocab = lax.optimization_barrier((sums, w_vocab))
     vocab_rows = w_vocab.reshape(NC, NX, slab, -1)
     vocab_parts = []
     for shift in range(NX):
@@ -437,52 +481,26 @@
     head_own = lax.dynamic_index_in_dim(head_w, core, 0, keepdims=False)
     head_other = lax.dynamic_index_in_dim(head_w, 1 - core, 0, keepdims=False)
 
-    pieces = exchange(partial_heads, EX)
-    hidden = jnp.sum(pieces.astype(F32), axis=0) + residual_here.astype(F32)
-    hidden = hidden.astype(BF16)
-
-    hidden_z = spread(hidden, "z", NZ)
-    early = (hidden_z, head_own, head_other, expert_ids, w_gate, w_up, w_down, router)
-    early = lax.optimization_barrier(early)
-    hidden_z, head_own, head_other, expert_ids, w_gate, w_up, w_down, router = early
-    own = spread(hidden_z, XY, NXY)
-    order = expert_ids.reshape(NXY, NC, part_rows, 2).transpose(1, 0, 2, 3)
-    order = order.reshape(NC, -1, 2)
-    order_own = lax.dynamic_index_in_dim(order, core, 0, keepdims=False)
-    order_other = lax.dynamic_index_in_dim(order, 1 - core, 0, keepdims=False)
-    gain_col = gain_moe[:, None]
-    router_g = (router.astype(F32) * gain_col).astype(BF16)
-    router_z = router_g.T.reshape(-1, NX, NZ, unit).transpose(2, 0, 1, 3)
-    router_z = router_z.reshape(NZ, -1, NX * unit)
-    gate_g = (w_gate[0].astype(F32) * gain_col).astype(BF16)
-    up_g = (w_up[0].astype(F32) * gain_col).astype(BF16)
-    down_sent = lax.dynamic_slice_in_dim(w_down[0], (1 - core) * half, half, axis=1)
-    down_other = swap_cores(down_sent)
-    ready = (own, gate_g, up_g, router_z, order_own, order_other, down_other)
-    ready = lax.optimization_barrier(ready)
-    own, gate_g, up_g, router_z, order_own, order_other, down_other = ready
-    other = swap_cores(own)
-
-    act_own = experts(place, own, gate_g, up_g, router_z, order_own)
-    act_other = experts(place, other, gate_g, up_g, router_z, order_other)
-    acts = (act_own, act_other, swap_cores(act_other), swap_cores(act_own))
-    sent = down(place, acts, w_down[0], down_other)
-    sent = sent.reshape(NXY, NZ, part_rows, slab)
-    sums = jnp.sum(exchange(sent, XY).astype(F32), axis=0).astype(BF16)
     sums = jnp.sum(exchange(sums, "z").astype(F32), axis=0)
 
     units = slab // unit
     first_unit = core * (half // unit) + x * units
-    start = (y * NX + z // 2, first_unit % NZ, 0, 0)
-    size = (1, units, part_rows, NX * unit)
+    here = [
+        lax.dynamic_index_in_dim(a, y * NX + z // 2, 0, keepdims=False) for a in (*own, *other)
+    ]
+    inner = x % 2 == core
     rows_here = jnp.where(
-        z % 2 == core, lax.dynamic_slice(own, start, size), lax.dynamic_slice(other, start, size)
-    )[0].reshape(units, part_rows, NX, unit)
+        z % 2 == 0,
+        jnp.where(inner, here[0], here[NC]),
+        jnp.where(inner, here[1], here[NC + 1]),
+    ).reshape(units, part_rows, NX, unit)
     cut = lax.dynamic_index_in_dim(rows_here, first_unit // NZ, 2, keepdims=False)
     hidden_here = cut.transpose(1, 0, 2).reshape(part_rows, slab).astype(F32)
     moved = (hidden_here + sums).astype(BF16)
 
-    final_own = spread(spread(moved, "z", NZ), "y", NY).reshape(NY, NZ, part_rows, slab)
+    moved_z = spread(moved, "z", NZ)
+    moved_z, head_own, head_other = lax.optimization_barrier((moved_z, head_own, head_other))
+    final_own = spread(moved_z, "y", NY).reshape(NY, NZ, part_rows, slab)
     final_other = swap_cores(final_own)
     count = total_rows // NX
 

time: 277 us -> 270 us (0.975)
  waiting for transfers between devices: 123 us -> 109 us
  Pallas kernels: 22.6 us -> 29.3 us
    all_to_all x8 -> x10, waiting for transfers between devices: 100 us -> 88.2 us  [exchange(): return lax.all_to_all(value, axes, split_axis=0, concat_axis=0, tiled=True)]
    ppermute x5 -> x7, starting transfers between devices: 9.95 us -> 15.9 us  [swap_cores(): return lax.ppermute(value, 'c', [(0, 1), (1, 0)])]
    pallas_call x1 -> x2, Pallas kernels: 4.34 us -> 9.78 us  [down(): pl.pallas_call(down_kernel, out_shape=pltpu.HBM((NX, NXY, rows, width), B...]
    all_to_all x8 -> x10, starting transfers between devices: 55.8 us -> 50.4 us  [exchange(): return lax.all_to_all(value, axes, split_axis=0, concat_axis=0, tiled=True)]
    ppermute x3, waiting for transfers between devices: 7.71 us -> 3.51 us  [shards(): part = lax.ppermute(part, 'x', [(i, (i + shift) % NX) for i in range(NX)])]
  transfers between devices with their start and end apart: 19 -> 23, of which waited for: 12 -> 17; matrix products, arithmetic and copies ran while one was open for 5% -> 5% of each run, Pallas kernels for 4% -> 8%
where the time goes in v6:
time: 270 us; the launch traced here: 268 us
  waiting for transfers between devices  109 us (40%)
  starting transfers between devices  73.8 us (27%)
  Pallas kernels  29.3 us (11%)
  blocking collectives  22.8 us (8%)
  local copies, waits for them, and re-layouts  21.1 us (8%)
  other arithmetic  10.8 us (4%)
    all_to_all x10, waiting for transfers between devices, exchange(): return lax.all_to_all(value, axes, split_axis=0, concat_axis=0, tiled=True)  88.2 us
    all_to_all x10, starting transfers between devices, exchange(): return lax.all_to_all(value, axes, split_axis=0, concat_axis=0, tiled=True)  50.4 us
    all_to_all x2, blocking collectives, exchange(): return lax.all_to_all(value, axes, split_axis=0, concat_axis=0, tiled=True)  22.8 us
    ppermute x7, starting transfers between devices, swap_cores(): return lax.ppermute(value, 'c', [(0, 1), (1, 0)])  15.9 us
    ppermute x3, waiting for transfers between devices, shards(): packs.append(lax.ppermute(sends[shift], 'x', pairs))  12.3 us
    pallas_call x2, Pallas kernels, experts(): pl.pallas_call(expert_kernel, out_shape=jax.ShapeDtypeStruct((total, hidd...  11.7 us
    unnamed x49, local copies, waits for them, and re-layouts  11 us
    pallas_call x2, Pallas kernels, down(): pl.pallas_call(down_kernel, out_shape=pltpu.HBM((NX, NXY, rows, width), B...  9.78 us
  transfers between devices with their start and end apart: 23, of which 17 were waited for; matrix products, arithmetic and copies ran while one was open for 5% of the time, Pallas kernels for 8%

profile of v6, /device:TPU:1, one launch (start us, length us, event | category | flops | bytes accessed | tf_op | source)
XLA Modules:
  0.0 268.4 jit_solution(3275332631483590532)
XLA Ops:
  2.6 1.7 pack.1
  9.2 2.1 attend.1
  11.3 9.0 %all-to-all-start = ((bf16[8,16,768]{2,1,0:T(8,128)(2,1)}), bf16[8,16,768]{2,1,0:T(8,128)(2,1)S(1)}, u32[]{:S(2)}, u32[]{:S(2)}) async-start(bf16[8,16,768]{2,1,0:T(8,128)(2,1)} %attend.1), calls=%async_computation | async-start | bytes 393216 | tf_op jit(solution)/shard_map/all_to_all | solution.py:31
  20.4 1.3 collective-permute-start
  21.6 2.5 collective-permute-start.1
  25.3 4.5 %collective-permute-done.refs_1_ = bf16[208,768]{1,0:T(8,128)(2,1)S(1)} collective-permute-done((bf16[208,768]{1,0:T(8,128)(2,1)S(1)}, bf16[208,768]{1,0:T(8,128)(2,1)S(1)}, u32[]{:S(2)}, u32[]{:S(2)}) %collective-permute-start) | collective-permute-done | bytes 319520 | tf_op jit(solution)/shard_map/ppermute | solution.py:416
  29.7 7.8 %collective-permute-done.1.refs_2_ = bf16[208,768]{1,0:T(8,128)(2,1)S(1)} collective-permute-done((bf16[208,768]{1,0:T(8,128)(2,1)S(1)}, bf16[208,768]{1,0:T(8,128)(2,1)S(1)}, u32[]{:S(2)}, u32[]{:S(2)}) %collective-permute-start.1) | collective-permute-done | bytes 319520 | tf_op jit(solution)/shard_map/ppermute | solution.py:416
  38.7 12.0 %all_to_all.67 = bf16[8,16,768]{2,1,0:T(8,128)(2,1)S(1)} all-to-all(bf16[8,16,768]{2,1,0:T(8,128)(2,1)S(1)} %get-tuple-element.44), channel_id=1, replica_groups=mesh['x'=4,'z'=8,'y'=4,'c'=2] {'y','c'}, dimensions={0} | all-to-all | bytes 393216 | tf_op jit(solution)/shard_map/all_to_all | solution.py:31
  51.5 6.6 %all-to-all-start.2 = ((bf16[8,16,768]{2,1,0:T(8,128)(2,1)}), bf16[8,16,768]{2,1,0:T(8,128)(2,1)S(1)}, u32[]{:S(2)}, u32[]{:S(2)}) async-start(bf16[8,16,768]{2,1,0:T(8,128)(2,1)} %broadcast_in_dim.12), calls=%async_computation.2 | async-start | bytes 393216 | tf_op jit(solution)/shard_map/all_to_all | solution.py:31
  58.1 8.5 %all-to-all-done.2 = bf16[8,16,768]{2,1,0:T(8,128)(2,1)S(1)} async-done(((bf16[8,16,768]{2,1,0:T(8,128)(2,1)}), bf16[8,16,768]{2,1,0:T(8,128)(2,1)S(1)}, u32[]{:S(2)}, u32[]{:S(2)}) %all-to-all-start.2) | async-done | bytes 196640 | tf_op jit(solution)/shard_map/all_to_all | solution.py:31
  66.6 3.0 %collective-permute-start.3 = (bf16[4,16,768]{2,1,0:T(8,128)(2,1)S(1)}, bf16[4,16,768]{2,1,0:T(8,128)(2,1)S(1)}, u32[]{:S(2)}, u32[]{:S(2)}) collective-permute-start(bf16[4,16,768]{2,1,0:T(8,128)(2,1)S(1)} %constant_dynamic-slice_fusion.2), channel_id=1, source_target_pairs={{0,1},{1,0},{2,3},{3,2},{4,5},{5,4},{6,7},{7,6},{8,9},{9,8},{10,11... | collective-permute-start | bytes 294920 | tf_op jit(solution)/shard_map/ppermute | solution.py:27
  72.1 1.3 broadcast_in_dim.13
  73.5 4.7 %all-to-all-start.3 = ((bf16[16,4,16,768]{3,2,1,0:T(8,128)(2,1)}), bf16[16,4,16,768]{3,2,1,0:T(8,128)(2,1)}, u32[]{:S(2)}, u32[]{:S(2)}) async-start(bf16[16,4,16,768]{3,2,1,0:T(8,128)(2,1)} %broadcast_in_dim.13), calls=%async_computation.3 | async-start | bytes 3145728 | tf_op jit(solution)/shard_map/all_to_all | solution.py:31
  78.2 1.4 dynamic-slice_bitcast_fusion
  80.6 4.0 %fusion = (bf16[6144,256]{1,0:T(8,128)(2,1)S(1)}, bf16[6144,256]{1,0:T(8,128)(2,1)}) fusion(bf16[1,6144,256]{2,1,0:T(8,128)(2,1)S(1)} %copy-done.14, f32[6144]{0:T(1024)S(1)} %copy-done.17, bf16[1,6144,256]{2,1,0:T(8,128)(2,1)} %param.28), kind=kLoop, calls=%fused_computation.1 | loop fusion | flops 9437184 | bytes 12607488 | tf_op jit(solution)/shard_map/convert_element_type | solution.py:445
  84.6 15.9 %all-to-all-done.3.own = bf16[16,4,16,768]{3,2,1,0:T(8,128)(2,1)} async-done(((bf16[16,4,16,768]{3,2,1,0:T(8,128)(2,1)}), bf16[16,4,16,768]{3,2,1,0:T(8,128)(2,1)}, u32[]{:S(2)}, u32[]{:S(2)}) %all-to-all-start.3) | async-done | bytes 1572896 | tf_op jit(solution)/shard_map/all_to_all | solution.py:31
  100.5 2.7 %collective-permute-start.5 = (bf16[16,4,16,768]{3,2,1,0:T(8,128)(2,1)}, bf16[16,4,16,768]{3,2,1,0:T(8,128)(2,1)}, u32[]{:S(2)}, u32[]{:S(2)}) collective-permute-start(bf16[16,4,16,768]{3,2,1,0:T(8,128)(2,1)} %all-to-all-done.3.own), channel_id=1, source_target_pairs={{0,1},{1,0},{2,3},{3,2},{4,5},{5,4},{6,7},{7,6},{8,9},{9,8},{10,11... | collective-permute-start | bytes 4718600 | tf_op jit(solution)/shard_map/ppermute | solution.py:27
  103.2 1.3 broadcast_in_dim.14
  104.6 4.4 %all-to-all-start.4 = ((bf16[16,4,16,768]{3,2,1,0:T(8,128)(2,1)}), bf16[16,4,16,768]{3,2,1,0:T(8,128)(2,1)}, u32[]{:S(2)}, u32[]{:S(2)}) async-start(bf16[16,4,16,768]{3,2,1,0:T(8,128)(2,1)} %broadcast_in_dim.14), calls=%async_computation.4 | async-start | bytes 3145728 | tf_op jit(solution)/shard_map/all_to_all | solution.py:31
  110.0 1.9 copy-done.1
  111.9 5.9 %experts.2.mine = bf16[256,256]{1,0:T(8,128)(2,1)S(1)} custom-call(s32[3]{0:T(128)S(1)} %pad_add_fusion.place, bf16[16,4,16,768]{3,2,1,0:T(8,128)(2,1)} %all-to-all-done.3.own, bf16[16,4,16,768]{3,2,1,0:T(8,128)(2,1)} %collective-permute-done.5.other, bf16[4,8,192,256]{3,2,1,0:T(8,128)(2,1)S(1)} %bitcast.101, bf16[4,8,192,256]{3,2,1,0:T(8,128)(2,1)S(1)} %bitcast.99, ...), custom_call_target="tpu_custom_call" | custom-call | flops 1610612736 | bytes 10485760 | tf_op jit(solution)/shard_map/experts/pallas_call | solution.py:238
  117.8 1.3 collective-permute-done.6.theirs
  119.2 4.9 %down.2 = bf16[4,16,16,768]{3,2,1,0:T(8,128)(2,1)} custom-call(s32[3]{0:T(128)S(1)} %pad_add_fusion.place, bf16[256,256]{1,0:T(8,128)(2,1)S(1)} %experts.2.mine, bf16[256,256]{1,0:T(8,128)(2,1)S(1)} %collective-permute-done.6.theirs, bf16[256,6144]{1,0:T(8,128)(2,1)S(1)} %bitcast.103, bf16[256,3072]{1,0:T(8,128)(2,1)} %collective-permute-done.4.w_theirs), custom_call_target="tpu_custom_call" | custom-call | flops 805306368 | bytes 5242880 | tf_op jit(solution)/shard_map/down/pallas_call | solution.py:290
  124.1 8.6 %all-to-all-done.4.own = bf16[16,4,16,768]{3,2,1,0:T(8,128)(2,1)} async-done(((bf16[16,4,16,768]{3,2,1,0:T(8,128)(2,1)}), bf16[16,4,16,768]{3,2,1,0:T(8,128)(2,1)}, u32[]{:S(2)}, u32[]{:S(2)}) %all-to-all-start.4) | async-done | bytes 1572896 | tf_op jit(solution)/shard_map/all_to_all | solution.py:31
  132.6 1.3 collective-permute-start.7
  133.9 4.4 %all-to-all-start.5 = ((bf16[16,4,16,768]{3,2,1,0:T(8,128)(2,1)}), bf16[16,4,16,768]{3,2,1,0:T(8,128)(2,1)}, u32[]{:S(2)}, u32[]{:S(2)}) async-start(bf16[16,4,16,768]{3,2,1,0:T(8,128)(2,1)} %bitcast.109), calls=%async_computation.5 | async-start | bytes 3145728 | tf_op jit(solution)/shard_map/all_to_all | solution.py:31
  138.4 1.9 copy-done.2
  140.3 5.9 %experts.3.mine = bf16[256,256]{1,0:T(8,128)(2,1)S(1)} custom-call(s32[3]{0:T(128)S(1)} %pad_add_fusion.place, bf16[16,4,16,768]{3,2,1,0:T(8,128)(2,1)} %all-to-all-done.4.own, bf16[16,4,16,768]{3,2,1,0:T(8,128)(2,1)} %collective-permute-done.7.other, bf16[4,8,192,256]{3,2,1,0:T(8,128)(2,1)S(1)} %bitcast.102, bf16[4,8,192,256]{3,2,1,0:T(8,128)(2,1)S(1)} %bitcast.100, ...), custom_call_target="tpu_custom_call" | custom-call | flops 1610612736 | bytes 10485760 | tf_op jit(solution)/shard_map/experts/pallas_call | solution.py:238
  147.6 4.9 %down.3 = bf16[4,16,16,768]{3,2,1,0:T(8,128)(2,1)} custom-call(s32[3]{0:T(128)S(1)} %pad_add_fusion.place, bf16[256,256]{1,0:T(8,128)(2,1)S(1)} %experts.3.mine, bf16[256,256]{1,0:T(8,128)(2,1)S(1)} %collective-permute-done.8.theirs, bf16[256,6144]{1,0:T(8,128)(2,1)S(1)} %bitcast.104, bf16[256,3072]{1,0:T(8,128)(2,1)} %collective-permute-done.4.w_theirs), custom_call_target="tpu_custom_call" | custom-call | flops 805306368 | bytes 5242880 | tf_op jit(solution)/shard_map/down/pallas_call | solution.py:290
  152.5 9.7 %all-to-all-done.5 = bf16[16,4,16,768]{3,2,1,0:T(8,128)(2,1)} async-done(((bf16[16,4,16,768]{3,2,1,0:T(8,128)(2,1)}), bf16[16,4,16,768]{3,2,1,0:T(8,128)(2,1)}, u32[]{:S(2)}, u32[]{:S(2)}) %all-to-all-start.5) | async-done | bytes 1572896 | tf_op jit(solution)/shard_map/all_to_all | solution.py:31
  162.1 3.9 %all-to-all-start.6 = ((bf16[16,4,16,768]{3,2,1,0:T(8,128)(2,1)}), bf16[16,4,16,768]{3,2,1,0:T(8,128)(2,1)S(1)}, u32[]{:S(2)}, u32[]{:S(2)}) async-start(bf16[16,4,16,768]{3,2,1,0:T(8,128)(2,1)} %bitcast.108), calls=%async_computation.6 | async-start | bytes 3145728 | tf_op jit(solution)/shard_map/all_to_all | solution.py:31
  166.3 1.6 reduce_sum.61
  169.4 17.0 %all-to-all-done.6 = bf16[16,4,16,768]{3,2,1,0:T(8,128)(2,1)S(1)} async-done(((bf16[16,4,16,768]{3,2,1,0:T(8,128)(2,1)}), bf16[16,4,16,768]{3,2,1,0:T(8,128)(2,1)S(1)}, u32[]{:S(2)}, u32[]{:S(2)}) %all-to-all-start.6) | async-done | bytes 1572896 | tf_op jit(solution)/shard_map/all_to_all | solution.py:31
  187.3 3.4 %all-to-all-start.7 = ((bf16[8,16,768]{2,1,0:T(8,128)(2,1)}), bf16[8,16,768]{2,1,0:T(8,128)(2,1)S(1)}, u32[]{:S(2)}, u32[]{:S(2)}) async-start(bf16[8,16,768]{2,1,0:T(8,128)(2,1)} %bitcast.23), calls=%async_computation.7 | async-start | bytes 393216 | tf_op jit(solution)/shard_map/all_to_all | solution.py:31
  190.8 1.4 collective-permute-start.11
  193.6 5.7 %all-to-all-done.7 = bf16[8,16,768]{2,1,0:T(8,128)(2,1)S(1)} async-done(((bf16[8,16,768]{2,1,0:T(8,128)(2,1)}), bf16[8,16,768]{2,1,0:T(8,128)(2,1)S(1)}, u32[]{:S(2)}, u32[]{:S(2)}) %all-to-all-start.7) | async-done | bytes 196640 | tf_op jit(solution)/shard_map/all_to_all | solution.py:31
  200.0 3.4 %all-to-all-start.8 = ((bf16[8,16,768]{2,1,0:T(8,128)(2,1)}), bf16[8,16,768]{2,1,0:T(8,128)(2,1)S(1)}, u32[]{:S(2)}, u32[]{:S(2)}) async-start(bf16[8,16,768]{2,1,0:T(8,128)(2,1)} %broadcast_in_dim.15), calls=%async_computation.8 | async-start | bytes 393216 | tf_op jit(solution)/shard_map/all_to_all | solution.py:31
  203.6 3.3 %collective-permute-done.9 = bf16[2,768,128]{2,1,0:T(8,128)(2,1)} collective-permute-done((bf16[2,768,128]{2,1,0:T(8,128)(2,1)S(1)}, bf16[2,768,128]{2,1,0:T(8,128)(2,1)}, u32[]{:S(2)}, u32[]{:S(2)}) %collective-permute-start.9) | collective-permute-done | bytes 393248 | tf_op jit(solution)/shard_map/ppermute | solution.py:469
  206.9 1.7 multiply_convert_fusion.3
  208.9 3.0 %all-to-all-done.8 = bf16[8,16,768]{2,1,0:T(8,128)(2,1)S(1)} async-done(((bf16[8,16,768]{2,1,0:T(8,128)(2,1)}), bf16[8,16,768]{2,1,0:T(8,128)(2,1)S(1)}, u32[]{:S(2)}, u32[]{:S(2)}) %all-to-all-start.8) | async-done | bytes 196640 | tf_op jit(solution)/shard_map/all_to_all | solution.py:31
  212.0 10.7 %all_to_all.68.own = bf16[4,8,16,768]{3,2,1,0:T(8,128)(2,1)S(1)} all-to-all(bf16[4,8,16,768]{3,2,1,0:T(8,128)(2,1)S(1)} %broadcast_in_dim.16), channel_id=1, replica_groups=mesh['x'=4,'z'=8,'y'=4,'c'=2] {'y'}, dimensions={0} | all-to-all | bytes 1572864 | tf_op jit(solution)/shard_map/all_to_all | solution.py:31
  222.8 7.8 %collective-permute-start.12 = (bf16[4,8,16,768]{3,2,1,0:T(8,128)(2,1)S(1)}, bf16[4,8,16,768]{3,2,1,0:T(8,128)(2,1)S(1)}, u32[]{:S(2)}, u32[]{:S(2)}) collective-permute-start(bf16[4,8,16,768]{3,2,1,0:T(8,128)(2,1)S(1)} %all_to_all.68.own), channel_id=1, source_target_pairs={{0,1},{1,0},{2,3},{3,2},{4,5},{5,4},{6,7},{7,6},{8,9},{9,8},{10,11... | collective-permute-start | bytes 2359304 | tf_op jit(solution)/shard_map/ppermute | solution.py:27
  230.5 1.9 collective-permute-done.12.other
  232.6 1.9 head.1
  234.5 3.6 %all-to-all-start.10 = ((bf16[4,144,640]{2,1,0:T(8,128)(2,1)}), bf16[4,144,640]{2,1,0:T(8,128)(2,1)S(1)}, u32[]{:S(2)}, u32[]{:S(2)}) async-start(bf16[4,144,640]{2,1,0:T(8,128)(2,1)} %head.1), calls=%async_computation.10 | async-start | bytes 1474560 | tf_op jit(solution)/shard_map/all_to_all | solution.py:31
  238.4 11.2 %all-to-all-done.10.parts = bf16[4,144,640]{2,1,0:T(8,128)(2,1)S(1)} async-done(((bf16[4,144,640]{2,1,0:T(8,128)(2,1)}), bf16[4,144,640]{2,1,0:T(8,128)(2,1)S(1)}, u32[]{:S(2)}, u32[]{:S(2)}) %all-to-all-start.10) | async-done | bytes 737312 | tf_op jit(solution)/shard_map/all_to_all | solution.py:31
  251.1 7.0 %all-to-all-start.11 = ((f32[64,1,128]{2,1,0:T(1,128)}), f32[64,1,128]{2,1,0:T(1,128)S(1)}, u32[]{:S(2)}, u32[]{:S(2)}) async-start(f32[64,1,128]{2,1,0:T(1,128)} %bitcast.35), calls=%async_computation.11 | async-start | bytes 65536 | tf_op jit(solution)/shard_map/all_to_all | solution.py:31
  258.8 8.7 %all-to-all-done.11 = f32[64,1,128]{2,1,0:T(1,128)S(1)} async-done(((f32[64,1,128]{2,1,0:T(1,128)}), f32[64,1,128]{2,1,0:T(1,128)S(1)}, u32[]{:S(2)}, u32[]{:S(2)}) %all-to-all-start.11) | async-done | bytes 32800 | tf_op jit(solution)/shard_map/all_to_all | solution.py:31
  (111 shorter events, 24.6 us)
Async XLA Ops:
  0.6 237.5 %copy-start = (s32[512]{0:T(512)S(1)}, s32[512]{0:T(512)}, u32[]{:S(2)}) copy-start(s32[512]{0:T(512)} %param.34) | copy-start | bytes 6148
  0.7 1.0 copy-start.6
  1.7 0.9 copy-start.7
  4.3 1.0 copy-start.8
  5.4 1.0 copy-start.9
  6.4 0.7 copy-start.10
  7.1 0.7 copy-start.11
  7.8 0.7 copy-start.12
  8.5 0.7 copy-start.13
  9.2 11.2 %copy-start.23 = (bf16[208,768]{1,0:T(8,128)(2,1)S(1)}, bf16[208,768]{1,0:T(8,128)(2,1)}, u32[]{:S(2)}) copy-start(bf16[208,768]{1,0:T(8,128)(2,1)} %get-tuple-element.41) | copy-start | bytes 958468
  9.2 12.5 %copy-start.22 = (bf16[208,768]{1,0:T(8,128)(2,1)S(1)}, bf16[208,768]{1,0:T(8,128)(2,1)}, u32[]{:S(2)}) copy-start(bf16[208,768]{1,0:T(8,128)(2,1)} %get-tuple-element.42) | copy-start | bytes 958468
  9.2 14.9 %copy-start.21 = (bf16[208,768]{1,0:T(8,128)(2,1)S(1)}, bf16[208,768]{1,0:T(8,128)(2,1)}, u32[]{:S(2)}) copy-start(bf16[208,768]{1,0:T(8,128)(2,1)} %get-tuple-element.43) | copy-start | bytes 958468
  11.3 26.3 %all-to-all-start = ((bf16[8,16,768]{2,1,0:T(8,128)(2,1)}), bf16[8,16,768]{2,1,0:T(8,128)(2,1)S(1)}, u32[]{:S(2)}, u32[]{:S(2)}) async-start(bf16[8,16,768]{2,1,0:T(8,128)(2,1)} %attend.1), calls=%async_computation | async-start | bytes 393216 | tf_op jit(solution)/shard_map/all_to_all | solution.py:31
  20.3 50.3 %copy-start.19 = (s32[512,2]{0,1:T(2,128)S(1)}, s32[512,2]{0,1:T(2,128)}, u32[]{:S(2)}) copy-start(s32[512,2]{0,1:T(2,128)} %param.31) | copy-start | bytes 12292
  20.3 50.4 %copy-start.16 = (bf16[6144,8]{0,1:T(8,128)(2,1)S(1)}, bf16[6144,8]{0,1:T(8,128)(2,1)}, u32[]{:S(2)}) copy-start(bf16[6144,8]{0,1:T(8,128)(2,1)} %param.26) | copy-start | bytes 294916
  20.3 50.4 %copy-start.17 = (f32[6144]{0:T(1024)S(1)}, f32[6144]{0:T(1024)}, u32[]{:S(2)}) copy-start(f32[6144]{0:T(1024)} %param.27) | copy-start | bytes 73732
  20.4 9.4 %collective-permute-start = (bf16[208,768]{1,0:T(8,128)(2,1)S(1)}, bf16[208,768]{1,0:T(8,128)(2,1)S(1)}, u32[]{:S(2)}, u32[]{:S(2)}) collective-permute-start(bf16[208,768]{1,0:T(8,128)(2,1)S(1)} %copy-done.23), channel_id=1, source_target_pairs={{0,64},{64,128},{128,192},{192,0},{1,65},{65,129},{129,193},{193,1... | collective-permute-start | bytes 958472 | tf_op jit(solution)/shard_map/ppermute | solution.py:416
  21.6 15.9 %collective-permute-start.1 = (bf16[208,768]{1,0:T(8,128)(2,1)S(1)}, bf16[208,768]{1,0:T(8,128)(2,1)S(1)}, u32[]{:S(2)}, u32[]{:S(2)}) collective-permute-start(bf16[208,768]{1,0:T(8,128)(2,1)S(1)} %copy-done.22), channel_id=1, source_target_pairs={{0,128},{64,192},{128,0},{192,64},{1,129},{65,193},{129,1},{193,65... | collective-permute-start | bytes 958472 | tf_op jit(solution)/shard_map/ppermute | solution.py:416
  24.1 13.5 %collective-permute-start.2 = (bf16[208,768]{1,0:T(8,128)(2,1)S(1)}, bf16[208,768]{1,0:T(8,128)(2,1)S(1)}, u32[]{:S(2)}, u32[]{:S(2)}) collective-permute-start(bf16[208,768]{1,0:T(8,128)(2,1)S(1)} %copy-done.21), channel_id=1, source_target_pairs={{0,192},{64,0},{128,64},{192,128},{1,193},{65,1},{129,65},{193,129... | collective-permute-start | bytes 958472 | tf_op jit(solution)/shard_map/ppermute | solution.py:416
  51.5 15.1 %all-to-all-start.2 = ((bf16[8,16,768]{2,1,0:T(8,128)(2,1)}), bf16[8,16,768]{2,1,0:T(8,128)(2,1)S(1)}, u32[]{:S(2)}, u32[]{:S(2)}) async-start(bf16[8,16,768]{2,1,0:T(8,128)(2,1)} %broadcast_in_dim.12), calls=%async_computation.2 | async-start | bytes 393216 | tf_op jit(solution)/shard_map/all_to_all | solution.py:31
  66.6 3.9 %collective-permute-start.3 = (bf16[4,16,768]{2,1,0:T(8,128)(2,1)S(1)}, bf16[4,16,768]{2,1,0:T(8,128)(2,1)S(1)}, u32[]{:S(2)}, u32[]{:S(2)}) collective-permute-start(bf16[4,16,768]{2,1,0:T(8,128)(2,1)S(1)} %constant_dynamic-slice_fusion.2), channel_id=1, source_target_pairs={{0,1},{1,0},{2,3},{3,2},{4,5},{5,4},{6,7},{7,6},{8,9},{9,8},{10,11... | collective-permute-start | bytes 294920 | tf_op jit(solution)/shard_map/ppermute | solution.py:27
  73.5 4.7 %copy-start.3 = (bf16[1,256,6144]{2,1,0:T(8,128)(2,1)S(1)}, bf16[1,256,6144]{2,1,0:T(8,128)(2,1)}, u32[]{:S(2)}) copy-start(bf16[1,256,6144]{2,1,0:T(8,128)(2,1)} %param.30) | copy-start | bytes 9437188
  73.5 27.1 %all-to-all-start.3 = ((bf16[16,4,16,768]{3,2,1,0:T(8,128)(2,1)}), bf16[16,4,16,768]{3,2,1,0:T(8,128)(2,1)}, u32[]{:S(2)}, u32[]{:S(2)}) async-start(bf16[16,4,16,768]{3,2,1,0:T(8,128)(2,1)} %broadcast_in_dim.13), calls=%async_computation.3 | async-start | bytes 3145728 | tf_op jit(solution)/shard_map/all_to_all | solution.py:31
  78.2 2.5 copy-start.14
  79.5 21.0 %collective-permute-start.4 = (bf16[256,3072]{1,0:T(8,128)(2,1)}, bf16[256,3072]{1,0:T(8,128)(2,1)}, u32[]{:S(2)}, u32[]{:S(2)}) collective-permute-start(bf16[256,3072]{1,0:T(8,128)(2,1)} %dynamic-slice_bitcast_fusion), channel_id=1, source_target_pairs={{0,1},{1,0},{2,3},{3,2},{4,5},{5,4},{6,7},{7,6},{8,9},{9,8},{10,11... | collective-permute-start | bytes 4718600 | tf_op jit(solution)/shard_map/ppermute | solution.py:27
  100.5 9.4 %collective-permute-start.5 = (bf16[16,4,16,768]{3,2,1,0:T(8,128)(2,1)}, bf16[16,4,16,768]{3,2,1,0:T(8,128)(2,1)}, u32[]{:S(2)}, u32[]{:S(2)}) collective-permute-start(bf16[16,4,16,768]{3,2,1,0:T(8,128)(2,1)} %all-to-all-done.3.own), channel_id=1, source_target_pairs={{0,1},{1,0},{2,3},{3,2},{4,5},{5,4},{6,7},{7,6},{8,9},{9,8},{10,11... | collective-permute-start | bytes 4718600 | tf_op jit(solution)/shard_map/ppermute | solution.py:27
  104.6 28.1 %all-to-all-start.4 = ((bf16[16,4,16,768]{3,2,1,0:T(8,128)(2,1)}), bf16[16,4,16,768]{3,2,1,0:T(8,128)(2,1)}, u32[]{:S(2)}, u32[]{:S(2)}) async-start(bf16[16,4,16,768]{3,2,1,0:T(8,128)(2,1)} %broadcast_in_dim.14), calls=%async_computation.4 | async-start | bytes 3145728 | tf_op jit(solution)/shard_map/all_to_all | solution.py:31
  110.0 1.9 copy-start.1
  111.9 7.3 %copy-start.4 = (bf16[1,256,6144]{2,1,0:T(8,128)(2,1)S(1)}, bf16[1,256,6144]{2,1,0:T(8,128)(2,1)}, u32[]{:S(2)}) copy-start(bf16[1,256,6144]{2,1,0:T(8,128)(2,1)} %param.30) | copy-start | bytes 9437188
  117.7 1.4 collective-permute-start.6
  132.6 5.7 %collective-permute-start.7 = (bf16[16,4,16,768]{3,2,1,0:T(8,128)(2,1)}, bf16[16,4,16,768]{3,2,1,0:T(8,128)(2,1)}, u32[]{:S(2)}, u32[]{:S(2)}) collective-permute-start(bf16[16,4,16,768]{3,2,1,0:T(8,128)(2,1)} %all-to-all-done.4.own), channel_id=1, source_target_pairs={{0,1},{1,0},{2,3},{3,2},{4,5},{5,4},{6,7},{7,6},{8,9},{9,8},{10,11... | collective-permute-start | bytes 4718600 | tf_op jit(solution)/shard_map/ppermute | solution.py:27
  133.9 28.2 %all-to-all-start.5 = ((bf16[16,4,16,768]{3,2,1,0:T(8,128)(2,1)}), bf16[16,4,16,768]{3,2,1,0:T(8,128)(2,1)}, u32[]{:S(2)}, u32[]{:S(2)}) async-start(bf16[16,4,16,768]{3,2,1,0:T(8,128)(2,1)} %bitcast.109), calls=%async_computation.5 | async-start | bytes 3145728 | tf_op jit(solution)/shard_map/all_to_all | solution.py:31
  138.4 1.9 copy-start.2
  140.3 7.3 %copy-start.5 = (bf16[1,256,6144]{2,1,0:T(8,128)(2,1)S(1)}, bf16[1,256,6144]{2,1,0:T(8,128)(2,1)}, u32[]{:S(2)}) copy-start(bf16[1,256,6144]{2,1,0:T(8,128)(2,1)} %param.30) | copy-start | bytes 9437188
  146.1 1.4 collective-permute-start.8
  162.1 4.1 %copy-start.18 = (f32[6144]{0:T(1024)S(1)}, f32[6144]{0:T(1024)}, u32[]{:S(2)}) copy-start(f32[6144]{0:T(1024)} %param.32) | copy-start | bytes 73732
  162.1 24.3 %all-to-all-start.6 = ((bf16[16,4,16,768]{3,2,1,0:T(8,128)(2,1)}), bf16[16,4,16,768]{3,2,1,0:T(8,128)(2,1)S(1)}, u32[]{:S(2)}, u32[]{:S(2)}) async-start(bf16[16,4,16,768]{3,2,1,0:T(8,128)(2,1)} %bitcast.108), calls=%async_computation.6 | async-start | bytes 3145728 | tf_op jit(solution)/shard_map/all_to_all | solution.py:31
  167.9 22.8 %copy-start.15 = (bf16[6144,128]{1,0:T(8,128)(2,1)S(1)}, bf16[6144,128]{1,0:T(8,128)(2,1)}, u32[]{:S(2)}) copy-start(bf16[6144,128]{1,0:T(8,128)(2,1)} %param.33) | copy-start | bytes 4718596
  187.3 11.9 %all-to-all-start.7 = ((bf16[8,16,768]{2,1,0:T(8,128)(2,1)}), bf16[8,16,768]{2,1,0:T(8,128)(2,1)S(1)}, u32[]{:S(2)}, u32[]{:S(2)}) async-start(bf16[8,16,768]{2,1,0:T(8,128)(2,1)} %bitcast.23), calls=%async_computation.7 | async-start | bytes 393216 | tf_op jit(solution)/shard_map/all_to_all | solution.py:31
  190.8 12.6 %collective-permute-start.11 = (bf16[2,768,128]{2,1,0:T(8,128)(2,1)S(1)}, bf16[2,768,128]{2,1,0:T(8,128)(2,1)}, u32[]{:S(2)}, u32[]{:S(2)}) collective-permute-start(bf16[2,768,128]{2,1,0:T(8,128)(2,1)S(1)} %get-tuple-element.79), channel_id=1, source_target_pairs={{0,192},{64,0},{128,64},{192,128},{1,193},{65,1},{129,65},{193,129... | collective-permute-start | bytes 1179656 | tf_op jit(solution)/shard_map/ppermute | solution.py:469
  192.2 11.4 %collective-permute-start.10 = (bf16[2,768,128]{2,1,0:T(8,128)(2,1)S(1)}, bf16[2,768,128]{2,1,0:T(8,128)(2,1)}, u32[]{:S(2)}, u32[]{:S(2)}) collective-permute-start(bf16[2,768,128]{2,1,0:T(8,128)(2,1)S(1)} %get-tuple-element.80), channel_id=1, source_target_pairs={{0,64},{64,128},{128,192},{192,0},{1,65},{65,129},{129,193},{193,1... | collective-permute-start | bytes 1179656 | tf_op jit(solution)/shard_map/ppermute | solution.py:469
  192.4 14.5 %collective-permute-start.9 = (bf16[2,768,128]{2,1,0:T(8,128)(2,1)S(1)}, bf16[2,768,128]{2,1,0:T(8,128)(2,1)}, u32[]{:S(2)}, u32[]{:S(2)}) collective-permute-start(bf16[2,768,128]{2,1,0:T(8,128)(2,1)S(1)} %get-tuple-element.81), channel_id=1, source_target_pairs={{0,128},{64,192},{128,0},{192,64},{1,129},{65,193},{129,1},{193,65... | collective-permute-start | bytes 1179656 | tf_op jit(solution)/shard_map/ppermute | solution.py:469
  200.0 11.9 %all-to-all-start.8 = ((bf16[8,16,768]{2,1,0:T(8,128)(2,1)}), bf16[8,16,768]{2,1,0:T(8,128)(2,1)S(1)}, u32[]{:S(2)}, u32[]{:S(2)}) async-start(bf16[8,16,768]{2,1,0:T(8,128)(2,1)} %broadcast_in_dim.15), calls=%async_computation.8 | async-start | bytes 393216 | tf_op jit(solution)/shard_map/all_to_all | solution.py:31
  222.8 9.7 %collective-permute-start.12 = (bf16[4,8,16,768]{3,2,1,0:T(8,128)(2,1)S(1)}, bf16[4,8,16,768]{3,2,1,0:T(8,128)(2,1)S(1)}, u32[]{:S(2)}, u32[]{:S(2)}) collective-permute-start(bf16[4,8,16,768]{3,2,1,0:T(8,128)(2,1)S(1)} %all_to_all.68.own), channel_id=1, source_target_pairs={{0,1},{1,0},{2,3},{3,2},{4,5},{5,4},{6,7},{7,6},{8,9},{9,8},{10,11... | collective-permute-start | bytes 2359304 | tf_op jit(solution)/shard_map/ppermute | solution.py:27
  234.5 33.4 %copy-start.20 = (f32[2]{0:T(128)S(1)}, f32[2]{0:T(128)}, u32[]{:S(2)}) copy-start(f32[2]{0:T(128)} %param.35) | copy-start | bytes 28
  234.5 15.1 %all-to-all-start.10 = ((bf16[4,144,640]{2,1,0:T(8,128)(2,1)}), bf16[4,144,640]{2,1,0:T(8,128)(2,1)S(1)}, u32[]{:S(2)}, u32[]{:S(2)}) async-start(bf16[4,144,640]{2,1,0:T(8,128)(2,1)} %head.1), calls=%async_computation.10 | async-start | bytes 1474560 | tf_op jit(solution)/shard_map/all_to_all | solution.py:31
  251.1 16.3 %all-to-all-start.11 = ((f32[64,1,128]{2,1,0:T(1,128)}), f32[64,1,128]{2,1,0:T(1,128)S(1)}, u32[]{:S(2)}, u32[]{:S(2)}) async-start(f32[64,1,128]{2,1,0:T(1,128)} %bitcast.35), calls=%async_computation.11 | async-start | bytes 65536 | tf_op jit(solution)/shard_map/all_to_all | solution.py:31

commit v7 on v6

--- a/solution.py
+++ b/solution.py
@@ -23,6 +23,26 @@
     return pl.BlockSpec(shape, lambda *_: (0,) * len(shape))
 
 
+HBM = pl.BlockSpec(memory_space=pltpu.HBM)
+
+
+def fetch(sources, buffers, sems):
+    copies = [
+        pltpu.make_async_copy(source, buffer, sems.at[i])
+        for i, (source, buffer) in enumerate(zip(sources, buffers))
+    ]
+    for copy in copies:
+        copy.start()
+    for copy in copies:
+        copy.wait()
+
+
+def buffers_for(arrays):
+    return [pltpu.VMEM(a.shape, a.dtype) for a in arrays] + [
+        pltpu.SemaphoreType.DMA((len(arrays),))
+    ]
+
+
 def swap_cores(value):
     return lax.ppermute(value, "c", [(0, 1), (1, 0)])
 
@@ -35,7 +55,10 @@
     return exchange(jnp.broadcast_to(value[None], (count,) + value.shape), axes)
 
 
-def attend_kernel(lengths, queries, new_keys, new_values, k_cache, v_cache, out):
+def attend_kernel(lengths, *refs):
+    out = refs[5]
+    fetch(refs[:5], refs[6:11], refs[11])
+    queries, new_keys, new_values, k_cache, v_cache = refs[6:11]
     rows, _, span, width = k_cache.shape
     group = queries.shape[1] // width
     total = group * rows
@@ -78,20 +101,24 @@
         attend_kernel,
         out_shape=pltpu.HBM((NZ, rows, width), BF16),
         grid=(1,),
-        in_specs=[pl.BlockSpec(memory_space=pltpu.SMEM)] + [whole(a.shape) for a in arrays],
+        in_specs=[pl.BlockSpec(memory_space=pltpu.SMEM)] + [HBM] * len(arrays),
         out_specs=whole((NZ, rows, width)),
-        compiler_params=pltpu.CompilerParams(vmem_limit_bytes=32 << 20),
+        scratch_shapes=buffers_for(arrays),
+        compiler_params=pltpu.CompilerParams(vmem_limit_bytes=60 << 20),
         cost_estimate=pl.CostEstimate(flops=2 << 34, bytes_accessed=2 << 20, transcendentals=0),
         name="attend",
     )(lengths, *arrays)
 
 
-def pack_kernel(place, w_out, residual, *packs):
+def pack_kernel(place, *refs):
+    packs = refs[2 : 2 + NX]
+    w_out, residual, sems = refs[2 + NX :]
+    fetch(refs[:2], (w_out, residual), sems)
     unit, depth = w_out.shape
     rows = packs[0].shape[0] - unit
     line = lax.broadcasted_iota(jnp.int32, (NX * rows, residual.shape[1]), 0)
     target = lax.rem(place[2] + line // rows, NX)
-    wanted = (target * NY * NC + place[0]) * rows + line % rows
+    wanted = (target * NY + place[0] // NC) * rows + line % rows
     pick = lax.broadcasted_iota(jnp.int32, line.shape, 1) == wanted
     parts = lax.dot_general(
         pick.astype(F32).astype(BF16),
@@ -114,13 +141,10 @@
         pack_kernel,
         out_shape=[jax.ShapeDtypeStruct(shape, BF16)] + [pltpu.HBM(shape, BF16)] * (NX - 1),
         grid=(1,),
-        in_specs=[
-            pl.BlockSpec(memory_space=pltpu.SMEM),
-            whole(w_out.shape),
-            whole(residual.shape),
-        ],
+        in_specs=[pl.BlockSpec(memory_space=pltpu.SMEM), HBM, HBM],
         out_specs=[whole(shape)] * NX,
-        compiler_params=pltpu.CompilerParams(vmem_limit_bytes=32 << 20),
+        scratch_shapes=buffers_for((w_out, residual)),
+        compiler_params=pltpu.CompilerParams(vmem_limit_bytes=60 << 20),
         name="pack",
     )(place, w_out, residual)
 
@@ -129,7 +153,7 @@
     packs, (partial, residual) = refs[:NX], refs[NX:]
     depth = attended.shape[-1]
     value = attended[...].reshape(-1, depth)
-    unit = residual.shape[1] // NX
+    unit = packs[0].shape[0] - residual.shape[0]
     products = [
         lax.dot_general(
             value, pack[:unit, :], (((1,), (1,)), ((), ())), preferred_element_type=F32
@@ -149,19 +173,27 @@
             blocks.append(block)
         return jnp.concatenate(blocks, axis=1).astype(BF16)
 
-    partial[...] = order(products).reshape(partial.shape)
-    residual[...] = order(rows)
+    wide = order(products)
+    count, part = residual.shape
+    for y in range(NY):
+        for core in range(NC):
+            partial[y * NC + core] = wide[
+                y * count : (y + 1) * count, core * part : (core + 1) * part
+            ]
+    wide = order(rows)
+    residual[...] = jnp.where(place[1] == 0, wide[:, :part], wide[:, part:])
 
 
 def project(place, attended, packs):
     _, rows, depth = attended.shape
-    unit = packs[0].shape[0] - rows
+    unit = packs[0].shape[0] - NC * rows
+    shape = (NC * rows, NX * unit // NC)
     vmem = pl.BlockSpec(memory_space=pltpu.VMEM)
     return pl.pallas_call(
         project_kernel,
         out_shape=(
-            jax.ShapeDtypeStruct((NY * NC, rows, NX * unit), BF16),
-            jax.ShapeDtypeStruct((rows, NX * unit), BF16),
+            jax.ShapeDtypeStruct((NY * NC, *shape), BF16),
+            jax.ShapeDtypeStruct(shape, BF16),
         ),
         in_specs=[pl.BlockSpec(memory_space=pltpu.SMEM)] + [vmem] * (1 + NX),
         out_specs=(vmem, vmem),
@@ -204,7 +236,7 @@
     def _():
         gate, up, route, square = products(other)
         square += squares[...]
-        mean = jnp.sum(square, axis=1, keepdims=True) / (width * NZ)
+        mean = jnp.sum(square, axis=1, keepdims=True) / (width * NZ * NC)
         scale = lax.rsqrt(mean + EPS)
         logits = (route + route_sum[...]) * scale
         lanes = lax.broadcasted_iota(jnp.int32, logits.shape, 1)
@@ -223,17 +255,18 @@
 
 
 def experts(place, own, other, gate_w, up_w, router_w, ids):
-    _, step, rows, width = own.shape
+    _, _, rows, width = own.shape
     total = NXY * rows
     hidden_units = gate_w.shape[-1]
-    unit = width // NX
+    part = NX // NC
+    unit = width // part
     count = router_w.shape[1]
 
     def half(s, p):
         return p[1] + s - 2 * p[1] * s
 
     weights = pl.BlockSpec(
-        (NX, step, unit, hidden_units), lambda s, p: (0, half(s, p), 0, 0)
+        (part, NZ, unit, hidden_units), lambda s, p: (half(s, p), 0, 0, 0)
     )
     return pl.pallas_call(
         expert_kernel,
@@ -246,7 +279,7 @@
                 whole(other.shape),
                 weights,
                 weights,
-                pl.BlockSpec((step, count, width), lambda s, p: (half(s, p), 0, 0)),
+                pl.BlockSpec((NZ, count, width), lambda s, p: (0, 0, half(s, p))),
                 whole(ids.shape),
             ],
             out_specs=whole((total, hidden_units)),
@@ -261,7 +294,7 @@
             dimension_semantics=("arbitrary",), vmem_limit_bytes=32 << 20
         ),
         cost_estimate=pl.CostEstimate(
-            flops=2 * total * width * NZ * 2 * hidden_units,
+            flops=4 * total * width * NZ * 2 * hidden_units,
             bytes_accessed=10 << 20,
             transcendentals=total * hidden_units,
         ),
@@ -408,7 +441,7 @@
     total_rows = residual.shape[0]
     part_rows = total_rows // (NX * NY * NC)
 
-    sends = pack(place, w_out.T, residual.T, part_rows)
+    sends = pack(place, w_out.T, residual.T, NC * part_rows)
     *sends, queries = lax.optimization_barrier((*sends, queries))
     packs = [sends[0]]
     for shift in range(1, NX):
@@ -425,10 +458,7 @@
     hidden = hidden.astype(BF16)
 
     hidden_z = spread(hidden, "z", NZ)
-    depth_z = NZ // NC
-    near = lax.dynamic_slice_in_dim(hidden_z, core * depth_z, depth_z)
-    far = swap_cores(lax.dynamic_slice_in_dim(hidden_z, (1 - core) * depth_z, depth_z))
-    chunks = [jnp.where(core == k, near, far) for k in range(NC)]
+    chunks = [hidden_z[:, k * part_rows : (k + 1) * part_rows] for k in range(NC)]
 
     early = (*chunks, expert_ids, w_gate, w_up, w_down, router)
     early = lax.optimization_barrier(early)
@@ -485,16 +515,11 @@
 
     units = slab // unit
     first_unit = core * (half // unit) + x * units
-    here = [
-        lax.dynamic_index_in_dim(a, y * NX + z // 2, 0, keepdims=False) for a in (*own, *other)
-    ]
-    inner = x % 2 == core
-    rows_here = jnp.where(
-        z % 2 == 0,
-        jnp.where(inner, here[0], here[NC]),
-        jnp.where(inner, here[1], here[NC + 1]),
-    ).reshape(units, part_rows, NX, unit)
-    cut = lax.dynamic_index_in_dim(rows_here, first_unit // NZ, 2, keepdims=False)
+    here = [lax.dynamic_index_in_dim(a, y * NX + z // 2, 0, keepdims=False) for a in own]
+    rows_here = jnp.where(z % 2 == 0, here[0], here[1])
+    rows_here = lax.dynamic_slice_in_dim(rows_here, first_unit % NZ, units)
+    rows_here = rows_here.reshape(units, part_rows, NX // NC, unit)
+    cut = lax.dynamic_index_in_dim(rows_here, x // NC, 2, keepdims=False)
     hidden_here = cut.transpose(1, 0, 2).reshape(part_rows, slab).astype(F32)
     moved = (hidden_here + sums).astype(BF16)
 

time: 270 us -> 264 us (0.978)
  local copies, waits for them, and re-layouts: 21.1 us -> 14 us
  waiting for transfers between devices: 109 us -> 104 us
  Pallas kernels: 29.3 us -> 33.2 us
    unnamed x49 -> x38, local copies, waits for them, and re-layouts: 11 us -> 3.86 us
    ppermute x3, waiting for transfers between devices: 12.3 us -> 9.48 us  [shards(): packs.append(lax.ppermute(sends[shift], 'x', pairs))]
    ppermute x7 -> x6, starting transfers between devices: 15.9 us -> 17.1 us  [swap_cores(): return lax.ppermute(value, 'c', [(0, 1), (1, 0)])]
  transfers between devices with their start and end apart: 23 -> 22, of which waited for: 17 -> 17; matrix products, arithmetic and copies ran while one was open for 5% -> 5% of each run, Pallas kernels for 8% -> 9%
where the time goes in v7:
time: 264 us; the launch traced here: 263 us
  waiting for transfers between devices  104 us (39%)
  starting transfers between devices  75.9 us (29%)
  Pallas kernels  33.2 us (13%)
  blocking collectives  23.3 us (9%)
  local copies, waits for them, and re-layouts  14 us (5%)
  other arithmetic  11 us (4%)
    all_to_all x10, waiting for transfers between devices, exchange(): return lax.all_to_all(value, axes, split_axis=0, concat_axis=0, tiled=True)  86 us
    all_to_all x10, starting transfers between devices, exchange(): return lax.all_to_all(value, axes, split_axis=0, concat_axis=0, tiled=True)  51.3 us
    all_to_all x2, blocking collectives, exchange(): return lax.all_to_all(value, axes, split_axis=0, concat_axis=0, tiled=True)  23.3 us
    ppermute x6, starting transfers between devices, swap_cores(): return lax.ppermute(value, 'c', [(0, 1), (1, 0)])  17.1 us
    pallas_call x2, Pallas kernels, experts(): pl.pallas_call(expert_kernel, out_shape=jax.ShapeDtypeStruct((total, hidd...  12.8 us
    pallas_call x2, Pallas kernels, down(): pl.pallas_call(down_kernel, out_shape=pltpu.HBM((NX, NXY, rows, width), B...  9.77 us
    ppermute x3, waiting for transfers between devices, shards(): packs.append(lax.ppermute(sends[shift], 'x', pairs))  9.48 us
  transfers between devices with their start and end apart: 22, of which 17 were waited for; matrix products, arithmetic and copies ran while one was open for 5% of the time, Pallas kernels for 9%

profile of v7, /device:TPU:1, one launch (start us, length us, event | category | flops | bytes accessed | tf_op | source)
XLA Modules:
  0.0 262.8 jit_solution(13977794288901616148)
XLA Ops:
  1.3 3.0 %pack.1 = (bf16[224,768]{1,0:T(8,128)(2,1)}, bf16[224,768]{1,0:T(8,128)(2,1)}, bf16[224,768]{1,0:T(8,128)(2,1)}, bf16[224,768]{1,0:T(8,128)(2,1)}) custom-call(s32[3]{0:T(128)} %pad_add_fusion.place, bf16[192,768]{1,0:T(8,128)(2,1)} %bitcast.112, bf16[192,512]{1,0:T(8,128)(2,1)} %bitcast.114), custom_call_target="tpu_custom_call" | custom-call | tf_op jit(solution)/shard_map/pack/pallas_call | solution.py:140
  4.4 3.7 %attend.1 = bf16[8,16,768]{2,1,0:T(8,128)(2,1)} custom-call(s32[16]{0:T(128)} %lengths.1, bf16[16,768]{1,0:T(8,128)(2,1)} %refs_0_, bf16[16,128]{1,0:T(8,128)(2,1)} %refs_1_.1, bf16[16,128]{1,0:T(8,128)(2,1)} %refs_2_.1, bf16[16,1,128,128]{3,2,1,0:T(8,128)(2,1)} %refs_3_.1, bf16[16,1,128,128]{3,2,1,0:T(8,128)(2,1)} %refs_4_.1), custom_call_target="tpu_custom_call" | custom-call | flops 34359738368 | bytes 2097152 | tf_op jit(solution)/shard_map/attend/pallas_call | solution.py:100
  8.1 9.0 %all-to-all-start = ((bf16[8,16,768]{2,1,0:T(8,128)(2,1)}), bf16[8,16,768]{2,1,0:T(8,128)(2,1)S(1)}, u32[]{:S(2)}, u32[]{:S(2)}) async-start(bf16[8,16,768]{2,1,0:T(8,128)(2,1)} %attend.1), calls=%async_computation | async-start | bytes 393216 | tf_op jit(solution)/shard_map/all_to_all | solution.py:51
  18.4 2.5 collective-permute-start.1
  22.0 3.9 %all-to-all-done.attended = bf16[8,16,768]{2,1,0:T(8,128)(2,1)S(1)} async-done(((bf16[8,16,768]{2,1,0:T(8,128)(2,1)}), bf16[8,16,768]{2,1,0:T(8,128)(2,1)S(1)}, u32[]{:S(2)}, u32[]{:S(2)}) %all-to-all-start) | async-done | bytes 196640 | tf_op jit(solution)/shard_map/all_to_all | solution.py:51
  27.0 8.4 %collective-permute-done.1.refs_2_ = bf16[224,768]{1,0:T(8,128)(2,1)S(1)} collective-permute-done((bf16[224,768]{1,0:T(8,128)(2,1)S(1)}, bf16[224,768]{1,0:T(8,128)(2,1)S(1)}, u32[]{:S(2)}, u32[]{:S(2)}) %collective-permute-start.1) | collective-permute-done | bytes 344096 | tf_op jit(solution)/shard_map/ppermute | solution.py:449
  36.6 12.0 %all_to_all.67 = bf16[8,32,384]{2,1,0:T(8,128)(2,1)S(1)} all-to-all(bf16[8,32,384]{2,1,0:T(8,128)(2,1)S(1)} %get-tuple-element.44), channel_id=1, replica_groups=mesh['x'=4,'z'=8,'y'=4,'c'=2] {'y','c'}, dimensions={0} | all-to-all | bytes 393216 | tf_op jit(solution)/shard_map/all_to_all | solution.py:51
  49.3 6.6 %all-to-all-start.2 = ((bf16[8,32,384]{2,1,0:T(8,128)(2,1)}), bf16[8,32,384]{2,1,0:T(8,128)(2,1)S(1)}, u32[]{:S(2)}, u32[]{:S(2)}) async-start(bf16[8,32,384]{2,1,0:T(8,128)(2,1)} %broadcast_in_dim.12), calls=%async_computation.2 | async-start | bytes 393216 | tf_op jit(solution)/shard_map/all_to_all | solution.py:51
  56.0 8.5 %all-to-all-done.2 = bf16[8,32,384]{2,1,0:T(8,128)(2,1)S(1)} async-done(((bf16[8,32,384]{2,1,0:T(8,128)(2,1)}), bf16[8,32,384]{2,1,0:T(8,128)(2,1)S(1)}, u32[]{:S(2)}, u32[]{:S(2)}) %all-to-all-start.2) | async-done | bytes 196640 | tf_op jit(solution)/shard_map/all_to_all | solution.py:51
  66.0 1.4 broadcast_in_dim.13
  67.5 4.7 %all-to-all-start.3 = ((bf16[16,8,16,384]{3,2,1,0:T(8,128)(2,1)}), bf16[16,8,16,384]{3,2,1,0:T(8,128)(2,1)}, u32[]{:S(2)}, u32[]{:S(2)}) async-start(bf16[16,8,16,384]{3,2,1,0:T(8,128)(2,1)} %broadcast_in_dim.13), calls=%async_computation.3 | async-start | bytes 3145728 | tf_op jit(solution)/shard_map/all_to_all | solution.py:51
  72.2 1.3 dynamic-slice_bitcast_fusion
  73.5 3.2 %collective-permute-start.3 = (bf16[256,3072]{1,0:T(8,128)(2,1)}, bf16[256,3072]{1,0:T(8,128)(2,1)}, u32[]{:S(2)}, u32[]{:S(2)}) collective-permute-start(bf16[256,3072]{1,0:T(8,128)(2,1)} %dynamic-slice_bitcast_fusion), channel_id=1, source_target_pairs={{0,1},{1,0},{2,3},{3,2},{4,5},{5,4},{6,7},{7,6},{8,9},{9,8},{10,11... | collective-permute-start | bytes 4718600 | tf_op jit(solution)/shard_map/ppermute | solution.py:47
  76.7 4.0 %fusion = (bf16[6144,256]{1,0:T(8,128)(2,1)S(1)}, bf16[6144,256]{1,0:T(8,128)(2,1)}) fusion(bf16[1,6144,256]{2,1,0:T(8,128)(2,1)S(1)} %copy-done.8, f32[6144]{0:T(1024)S(1)} %copy-done.11, bf16[1,6144,256]{2,1,0:T(8,128)(2,1)} %param.28), kind=kLoop, calls=%fused_computation.1 | loop fusion | flops 9437184 | bytes 12607488 | tf_op jit(solution)/shard_map/convert_element_type | solution.py:475
  80.7 11.0 %all-to-all-done.3.own = bf16[16,8,16,384]{3,2,1,0:T(8,128)(2,1)} async-done(((bf16[16,8,16,384]{3,2,1,0:T(8,128)(2,1)}), bf16[16,8,16,384]{3,2,1,0:T(8,128)(2,1)}, u32[]{:S(2)}, u32[]{:S(2)}) %all-to-all-start.3) | async-done | bytes 1572896 | tf_op jit(solution)/shard_map/all_to_all | solution.py:51
  91.7 4.6 %collective-permute-start.4 = (bf16[16,8,16,384]{3,2,1,0:T(8,128)(2,1)}, bf16[16,8,16,384]{3,2,1,0:T(8,128)(2,1)}, u32[]{:S(2)}, u32[]{:S(2)}) collective-permute-start(bf16[16,8,16,384]{3,2,1,0:T(8,128)(2,1)} %all-to-all-done.3.own), channel_id=1, source_target_pairs={{0,1},{1,0},{2,3},{3,2},{4,5},{5,4},{6,7},{7,6},{8,9},{9,8},{10,11... | collective-permute-start | bytes 4718600 | tf_op jit(solution)/shard_map/ppermute | solution.py:47
  96.3 1.4 broadcast_in_dim.14
  97.7 4.4 %all-to-all-start.4 = ((bf16[16,8,16,384]{3,2,1,0:T(8,128)(2,1)}), bf16[16,8,16,384]{3,2,1,0:T(8,128)(2,1)}, u32[]{:S(2)}, u32[]{:S(2)}) async-start(bf16[16,8,16,384]{3,2,1,0:T(8,128)(2,1)} %broadcast_in_dim.14), calls=%async_computation.4 | async-start | bytes 3145728 | tf_op jit(solution)/shard_map/all_to_all | solution.py:51
  103.1 1.9 copy-done.1
  105.0 6.4 %experts.2.mine = bf16[256,256]{1,0:T(8,128)(2,1)S(1)} custom-call(s32[3]{0:T(128)S(1)} %copy-done.7, bf16[16,8,16,384]{3,2,1,0:T(8,128)(2,1)} %all-to-all-done.3.own, bf16[16,8,16,384]{3,2,1,0:T(8,128)(2,1)} %collective-permute-done.4.other, bf16[4,8,192,256]{3,2,1,0:T(8,128)(2,1)S(1)} %bitcast.99, bf16[4,8,192,256]{3,2,1,0:T(8,128)(2,1)S(1)} %bitcast.97, ...), custom_call_target="tpu_custom_call" | custom-call | flops 1610612736 | bytes 10485760 | tf_op jit(solution)/shard_map/experts/pallas_call | solution.py:271
  111.5 1.3 collective-permute-done.5.theirs
  112.9 4.9 %down.2 = bf16[4,16,16,768]{3,2,1,0:T(8,128)(2,1)} custom-call(s32[3]{0:T(128)S(1)} %copy-done.7, bf16[256,256]{1,0:T(8,128)(2,1)S(1)} %experts.2.mine, bf16[256,256]{1,0:T(8,128)(2,1)S(1)} %collective-permute-done.5.theirs, bf16[256,6144]{1,0:T(8,128)(2,1)S(1)} %bitcast.101, bf16[256,3072]{1,0:T(8,128)(2,1)} %collective-permute-done.3.w_theirs), custom_call_target="tpu_custom_call" | custom-call | flops 805306368 | bytes 5242880 | tf_op jit(solution)/shard_map/down/pallas_call | solution.py:323
  117.8 8.0 %all-to-all-done.4.own = bf16[16,8,16,384]{3,2,1,0:T(8,128)(2,1)} async-done(((bf16[16,8,16,384]{3,2,1,0:T(8,128)(2,1)}), bf16[16,8,16,384]{3,2,1,0:T(8,128)(2,1)}, u32[]{:S(2)}, u32[]{:S(2)}) %all-to-all-start.4) | async-done | bytes 1572896 | tf_op jit(solution)/shard_map/all_to_all | solution.py:51
  125.8 1.3 collective-permute-start.6
  127.1 4.6 %all-to-all-start.5 = ((bf16[16,4,16,768]{3,2,1,0:T(8,128)(2,1)}), bf16[16,4,16,768]{3,2,1,0:T(8,128)(2,1)}, u32[]{:S(2)}, u32[]{:S(2)}) async-start(bf16[16,4,16,768]{3,2,1,0:T(8,128)(2,1)} %bitcast.105), calls=%async_computation.5 | async-start | bytes 3145728 | tf_op jit(solution)/shard_map/all_to_all | solution.py:51
  131.7 1.9 copy-done.2
  133.6 6.4 %experts.3.mine = bf16[256,256]{1,0:T(8,128)(2,1)S(1)} custom-call(s32[3]{0:T(128)S(1)} %copy-done.7, bf16[16,8,16,384]{3,2,1,0:T(8,128)(2,1)} %all-to-all-done.4.own, bf16[16,8,16,384]{3,2,1,0:T(8,128)(2,1)} %collective-permute-done.6.other, bf16[4,8,192,256]{3,2,1,0:T(8,128)(2,1)S(1)} %bitcast.100, bf16[4,8,192,256]{3,2,1,0:T(8,128)(2,1)S(1)} %bitcast.98, ...), custom_call_target="tpu_custom_call" | custom-call | flops 1610612736 | bytes 10485760 | tf_op jit(solution)/shard_map/experts/pallas_call | solution.py:271
  141.4 4.9 %down.3 = bf16[4,16,16,768]{3,2,1,0:T(8,128)(2,1)} custom-call(s32[3]{0:T(128)S(1)} %copy-done.7, bf16[256,256]{1,0:T(8,128)(2,1)S(1)} %experts.3.mine, bf16[256,256]{1,0:T(8,128)(2,1)S(1)} %collective-permute-done.7.theirs, bf16[256,6144]{1,0:T(8,128)(2,1)S(1)} %bitcast.102, bf16[256,3072]{1,0:T(8,128)(2,1)} %collective-permute-done.3.w_theirs), custom_call_target="tpu_custom_call" | custom-call | flops 805306368 | bytes 5242880 | tf_op jit(solution)/shard_map/down/pallas_call | solution.py:323
  146.3 9.1 %all-to-all-done.5 = bf16[16,4,16,768]{3,2,1,0:T(8,128)(2,1)} async-done(((bf16[16,4,16,768]{3,2,1,0:T(8,128)(2,1)}), bf16[16,4,16,768]{3,2,1,0:T(8,128)(2,1)}, u32[]{:S(2)}, u32[]{:S(2)}) %all-to-all-start.5) | async-done | bytes 1572896 | tf_op jit(solution)/shard_map/all_to_all | solution.py:51
  155.4 3.9 %all-to-all-start.6 = ((bf16[16,4,16,768]{3,2,1,0:T(8,128)(2,1)}), bf16[16,4,16,768]{3,2,1,0:T(8,128)(2,1)S(1)}, u32[]{:S(2)}, u32[]{:S(2)}) async-start(bf16[16,4,16,768]{3,2,1,0:T(8,128)(2,1)} %bitcast.104), calls=%async_computation.6 | async-start | bytes 3145728 | tf_op jit(solution)/shard_map/all_to_all | solution.py:51
  159.6 1.6 reduce_sum.61
  161.3 18.5 %all-to-all-done.6 = bf16[16,4,16,768]{3,2,1,0:T(8,128)(2,1)S(1)} async-done(((bf16[16,4,16,768]{3,2,1,0:T(8,128)(2,1)}), bf16[16,4,16,768]{3,2,1,0:T(8,128)(2,1)S(1)}, u32[]{:S(2)}, u32[]{:S(2)}) %all-to-all-start.6) | async-done | bytes 1572896 | tf_op jit(solution)/shard_map/all_to_all | solution.py:51
  180.7 3.4 %all-to-all-start.7 = ((bf16[8,16,768]{2,1,0:T(8,128)(2,1)}), bf16[8,16,768]{2,1,0:T(8,128)(2,1)S(1)}, u32[]{:S(2)}, u32[]{:S(2)}) async-start(bf16[8,16,768]{2,1,0:T(8,128)(2,1)} %bitcast.22), calls=%async_computation.7 | async-start | bytes 393216 | tf_op jit(solution)/shard_map/all_to_all | solution.py:51
  185.1 1.4 collective-permute-start.10
  188.0 4.7 %all-to-all-done.7 = bf16[8,16,768]{2,1,0:T(8,128)(2,1)S(1)} async-done(((bf16[8,16,768]{2,1,0:T(8,128)(2,1)}), bf16[8,16,768]{2,1,0:T(8,128)(2,1)S(1)}, u32[]{:S(2)}, u32[]{:S(2)}) %all-to-all-start.7) | async-done | bytes 196640 | tf_op jit(solution)/shard_map/all_to_all | solution.py:51
  193.5 3.4 %all-to-all-start.8 = ((bf16[8,16,768]{2,1,0:T(8,128)(2,1)}), bf16[8,16,768]{2,1,0:T(8,128)(2,1)S(1)}, u32[]{:S(2)}, u32[]{:S(2)}) async-start(bf16[8,16,768]{2,1,0:T(8,128)(2,1)} %broadcast_in_dim.15), calls=%async_computation.8 | async-start | bytes 393216 | tf_op jit(solution)/shard_map/all_to_all | solution.py:51
  196.9 1.3 collective-permute-done.9
  198.2 2.8 %collective-permute-done.8 = bf16[2,768,128]{2,1,0:T(8,128)(2,1)} collective-permute-done((bf16[2,768,128]{2,1,0:T(8,128)(2,1)S(1)}, bf16[2,768,128]{2,1,0:T(8,128)(2,1)}, u32[]{:S(2)}, u32[]{:S(2)}) %collective-permute-start.8) | collective-permute-done | bytes 393248 | tf_op jit(solution)/shard_map/ppermute | solution.py:499
  201.0 1.7 multiply_convert_fusion.3
  203.0 2.5 all-to-all-done.8
  205.5 11.3 %all_to_all.68.own = bf16[4,8,16,768]{3,2,1,0:T(8,128)(2,1)S(1)} all-to-all(bf16[4,8,16,768]{3,2,1,0:T(8,128)(2,1)S(1)} %broadcast_in_dim.16), channel_id=1, replica_groups=mesh['x'=4,'z'=8,'y'=4,'c'=2] {'y'}, dimensions={0} | all-to-all | bytes 1572864 | tf_op jit(solution)/shard_map/all_to_all | solution.py:51
  216.7 7.5 %collective-permute-start.11 = (bf16[4,8,16,768]{3,2,1,0:T(8,128)(2,1)S(1)}, bf16[4,8,16,768]{3,2,1,0:T(8,128)(2,1)S(1)}, u32[]{:S(2)}, u32[]{:S(2)}) collective-permute-start(bf16[4,8,16,768]{3,2,1,0:T(8,128)(2,1)S(1)} %all_to_all.68.own), channel_id=1, source_target_pairs={{0,1},{1,0},{2,3},{3,2},{4,5},{5,4},{6,7},{7,6},{8,9},{9,8},{10,11... | collective-permute-start | bytes 2359304 | tf_op jit(solution)/shard_map/ppermute | solution.py:47
  224.3 1.9 collective-permute-done.11.other
  226.3 1.9 head.1
  228.2 3.6 %all-to-all-start.10 = ((bf16[4,144,640]{2,1,0:T(8,128)(2,1)}), bf16[4,144,640]{2,1,0:T(8,128)(2,1)S(1)}, u32[]{:S(2)}, u32[]{:S(2)}) async-start(bf16[4,144,640]{2,1,0:T(8,128)(2,1)} %head.1), calls=%async_computation.10 | async-start | bytes 1474560 | tf_op jit(solution)/shard_map/all_to_all | solution.py:51
  232.1 11.2 %all-to-all-done.10.parts = bf16[4,144,640]{2,1,0:T(8,128)(2,1)S(1)} async-done(((bf16[4,144,640]{2,1,0:T(8,128)(2,1)}), bf16[4,144,640]{2,1,0:T(8,128)(2,1)S(1)}, u32[]{:S(2)}, u32[]{:S(2)}) %all-to-all-start.10) | async-done | bytes 737312 | tf_op jit(solution)/shard_map/all_to_all | solution.py:51
  244.9 7.6 %all-to-all-start.11 = ((f32[64,1,128]{2,1,0:T(1,128)}), f32[64,1,128]{2,1,0:T(1,128)S(1)}, u32[]{:S(2)}, u32[]{:S(2)}) async-start(f32[64,1,128]{2,1,0:T(1,128)} %bitcast.34), calls=%async_computation.11 | async-start | bytes 65536 | tf_op jit(solution)/shard_map/all_to_all | solution.py:51
  253.2 8.7 %all-to-all-done.11 = f32[64,1,128]{2,1,0:T(1,128)S(1)} async-done(((f32[64,1,128]{2,1,0:T(1,128)}), f32[64,1,128]{2,1,0:T(1,128)S(1)}, u32[]{:S(2)}, u32[]{:S(2)}) %all-to-all-start.11) | async-done | bytes 32800 | tf_op jit(solution)/shard_map/all_to_all | solution.py:51
  (97 shorter events, 18.3 us)
Async XLA Ops:
  0.6 231.2 %copy-start = (s32[512]{0:T(512)S(1)}, s32[512]{0:T(512)}, u32[]{:S(2)}) copy-start(s32[512]{0:T(512)} %param.34) | copy-start | bytes 6148
  4.3 12.8 %copy-start.17 = (bf16[224,768]{1,0:T(8,128)(2,1)S(1)}, bf16[224,768]{1,0:T(8,128)(2,1)}, u32[]{:S(2)}) copy-start(bf16[224,768]{1,0:T(8,128)(2,1)} %get-tuple-element.41) | copy-start | bytes 1032196
  4.3 14.1 %copy-start.16 = (bf16[224,768]{1,0:T(8,128)(2,1)S(1)}, bf16[224,768]{1,0:T(8,128)(2,1)}, u32[]{:S(2)}) copy-start(bf16[224,768]{1,0:T(8,128)(2,1)} %get-tuple-element.42) | copy-start | bytes 1032196
  4.3 16.6 %copy-start.15 = (bf16[224,768]{1,0:T(8,128)(2,1)S(1)}, bf16[224,768]{1,0:T(8,128)(2,1)}, u32[]{:S(2)}) copy-start(bf16[224,768]{1,0:T(8,128)(2,1)} %get-tuple-element.43) | copy-start | bytes 1032196
  4.3 31.1 %copy-start.6 = (bf16[224,768]{1,0:T(8,128)(2,1)S(1)}, bf16[224,768]{1,0:T(8,128)(2,1)}, u32[]{:S(2)}) copy-start(bf16[224,768]{1,0:T(8,128)(2,1)} %get-tuple-element.40.refs_0_) | copy-start | bytes 1032196
  4.3 31.1 %copy-start.7 = (s32[3]{0:T(128)S(1)}, s32[3]{0:T(128)}, u32[]{:S(2)}) copy-start(s32[3]{0:T(128)} %pad_add_fusion.place) | copy-start | bytes 40
  8.1 17.8 %all-to-all-start = ((bf16[8,16,768]{2,1,0:T(8,128)(2,1)}), bf16[8,16,768]{2,1,0:T(8,128)(2,1)S(1)}, u32[]{:S(2)}, u32[]{:S(2)}) async-start(bf16[8,16,768]{2,1,0:T(8,128)(2,1)} %attend.1), calls=%async_computation | async-start | bytes 393216 | tf_op jit(solution)/shard_map/all_to_all | solution.py:51
  17.1 47.4 %copy-start.13 = (s32[512,2]{0,1:T(2,128)S(1)}, s32[512,2]{0,1:T(2,128)}, u32[]{:S(2)}) copy-start(s32[512,2]{0,1:T(2,128)} %param.31) | copy-start | bytes 12292
  17.1 47.5 %copy-start.10 = (bf16[6144,8]{0,1:T(8,128)(2,1)S(1)}, bf16[6144,8]{0,1:T(8,128)(2,1)}, u32[]{:S(2)}) copy-start(bf16[6144,8]{0,1:T(8,128)(2,1)} %param.26) | copy-start | bytes 294916
  17.1 47.5 %copy-start.11 = (f32[6144]{0:T(1024)S(1)}, f32[6144]{0:T(1024)}, u32[]{:S(2)}) copy-start(f32[6144]{0:T(1024)} %param.27) | copy-start | bytes 73732
  17.1 9.9 %collective-permute-start = (bf16[224,768]{1,0:T(8,128)(2,1)S(1)}, bf16[224,768]{1,0:T(8,128)(2,1)S(1)}, u32[]{:S(2)}, u32[]{:S(2)}) collective-permute-start(bf16[224,768]{1,0:T(8,128)(2,1)S(1)} %copy-done.17), channel_id=1, source_target_pairs={{0,64},{64,128},{128,192},{192,0},{1,65},{65,129},{129,193},{193,1... | collective-permute-start | bytes 1032200 | tf_op jit(solution)/shard_map/ppermute | solution.py:449
  18.4 17.0 %collective-permute-start.1 = (bf16[224,768]{1,0:T(8,128)(2,1)S(1)}, bf16[224,768]{1,0:T(8,128)(2,1)S(1)}, u32[]{:S(2)}, u32[]{:S(2)}) collective-permute-start(bf16[224,768]{1,0:T(8,128)(2,1)S(1)} %copy-done.16), channel_id=1, source_target_pairs={{0,128},{64,192},{128,0},{192,64},{1,129},{65,193},{129,1},{193,65... | collective-permute-start | bytes 1032200 | tf_op jit(solution)/shard_map/ppermute | solution.py:449
  20.9 14.5 %collective-permute-start.2 = (bf16[224,768]{1,0:T(8,128)(2,1)S(1)}, bf16[224,768]{1,0:T(8,128)(2,1)S(1)}, u32[]{:S(2)}, u32[]{:S(2)}) collective-permute-start(bf16[224,768]{1,0:T(8,128)(2,1)S(1)} %copy-done.15), channel_id=1, source_target_pairs={{0,192},{64,0},{128,64},{192,128},{1,193},{65,1},{129,65},{193,129... | collective-permute-start | bytes 1032200 | tf_op jit(solution)/shard_map/ppermute | solution.py:449
  49.3 15.1 %all-to-all-start.2 = ((bf16[8,32,384]{2,1,0:T(8,128)(2,1)}), bf16[8,32,384]{2,1,0:T(8,128)(2,1)S(1)}, u32[]{:S(2)}, u32[]{:S(2)}) async-start(bf16[8,32,384]{2,1,0:T(8,128)(2,1)} %broadcast_in_dim.12), calls=%async_computation.2 | async-start | bytes 393216 | tf_op jit(solution)/shard_map/all_to_all | solution.py:51
  67.5 4.7 %copy-start.3 = (bf16[1,256,6144]{2,1,0:T(8,128)(2,1)S(1)}, bf16[1,256,6144]{2,1,0:T(8,128)(2,1)}, u32[]{:S(2)}) copy-start(bf16[1,256,6144]{2,1,0:T(8,128)(2,1)} %param.30) | copy-start | bytes 9437188
  67.5 24.2 %all-to-all-start.3 = ((bf16[16,8,16,384]{3,2,1,0:T(8,128)(2,1)}), bf16[16,8,16,384]{3,2,1,0:T(8,128)(2,1)}, u32[]{:S(2)}, u32[]{:S(2)}) async-start(bf16[16,8,16,384]{3,2,1,0:T(8,128)(2,1)} %broadcast_in_dim.13), calls=%async_computation.3 | async-start | bytes 3145728 | tf_op jit(solution)/shard_map/all_to_all | solution.py:51
  72.2 4.5 %copy-start.8 = (bf16[1,6144,256]{2,1,0:T(8,128)(2,1)S(1)}, bf16[1,6144,256]{2,1,0:T(8,128)(2,1)}, u32[]{:S(2)}) copy-start(bf16[1,6144,256]{2,1,0:T(8,128)(2,1)} %param.29) | copy-start | bytes 9437188
  73.5 18.2 %collective-permute-start.3 = (bf16[256,3072]{1,0:T(8,128)(2,1)}, bf16[256,3072]{1,0:T(8,128)(2,1)}, u32[]{:S(2)}, u32[]{:S(2)}) collective-permute-start(bf16[256,3072]{1,0:T(8,128)(2,1)} %dynamic-slice_bitcast_fusion), channel_id=1, source_target_pairs={{0,1},{1,0},{2,3},{3,2},{4,5},{5,4},{6,7},{7,6},{8,9},{9,8},{10,11... | collective-permute-start | bytes 4718600 | tf_op jit(solution)/shard_map/ppermute | solution.py:47
  91.7 11.4 %collective-permute-start.4 = (bf16[16,8,16,384]{3,2,1,0:T(8,128)(2,1)}, bf16[16,8,16,384]{3,2,1,0:T(8,128)(2,1)}, u32[]{:S(2)}, u32[]{:S(2)}) collective-permute-start(bf16[16,8,16,384]{3,2,1,0:T(8,128)(2,1)} %all-to-all-done.3.own), channel_id=1, source_target_pairs={{0,1},{1,0},{2,3},{3,2},{4,5},{5,4},{6,7},{7,6},{8,9},{9,8},{10,11... | collective-permute-start | bytes 4718600 | tf_op jit(solution)/shard_map/ppermute | solution.py:47
  97.7 28.1 %all-to-all-start.4 = ((bf16[16,8,16,384]{3,2,1,0:T(8,128)(2,1)}), bf16[16,8,16,384]{3,2,1,0:T(8,128)(2,1)}, u32[]{:S(2)}, u32[]{:S(2)}) async-start(bf16[16,8,16,384]{3,2,1,0:T(8,128)(2,1)} %broadcast_in_dim.14), calls=%async_computation.4 | async-start | bytes 3145728 | tf_op jit(solution)/shard_map/all_to_all | solution.py:51
  103.1 1.9 copy-start.1
  105.0 7.9 %copy-start.4 = (bf16[1,256,6144]{2,1,0:T(8,128)(2,1)S(1)}, bf16[1,256,6144]{2,1,0:T(8,128)(2,1)}, u32[]{:S(2)}) copy-start(bf16[1,256,6144]{2,1,0:T(8,128)(2,1)} %param.30) | copy-start | bytes 9437188
  111.4 1.4 collective-permute-start.5
  125.8 5.9 %collective-permute-start.6 = (bf16[16,8,16,384]{3,2,1,0:T(8,128)(2,1)}, bf16[16,8,16,384]{3,2,1,0:T(8,128)(2,1)}, u32[]{:S(2)}, u32[]{:S(2)}) collective-permute-start(bf16[16,8,16,384]{3,2,1,0:T(8,128)(2,1)} %all-to-all-done.4.own), channel_id=1, source_target_pairs={{0,1},{1,0},{2,3},{3,2},{4,5},{5,4},{6,7},{7,6},{8,9},{9,8},{10,11... | collective-permute-start | bytes 4718600 | tf_op jit(solution)/shard_map/ppermute | solution.py:47
  127.1 28.4 %all-to-all-start.5 = ((bf16[16,4,16,768]{3,2,1,0:T(8,128)(2,1)}), bf16[16,4,16,768]{3,2,1,0:T(8,128)(2,1)}, u32[]{:S(2)}, u32[]{:S(2)}) async-start(bf16[16,4,16,768]{3,2,1,0:T(8,128)(2,1)} %bitcast.105), calls=%async_computation.5 | async-start | bytes 3145728 | tf_op jit(solution)/shard_map/all_to_all | solution.py:51
  131.7 1.9 copy-start.2
  133.6 7.9 %copy-start.5 = (bf16[1,256,6144]{2,1,0:T(8,128)(2,1)S(1)}, bf16[1,256,6144]{2,1,0:T(8,128)(2,1)}, u32[]{:S(2)}) copy-start(bf16[1,256,6144]{2,1,0:T(8,128)(2,1)} %param.30) | copy-start | bytes 9437188
  140.0 1.4 collective-permute-start.7
  155.4 4.1 %copy-start.12 = (f32[6144]{0:T(1024)S(1)}, f32[6144]{0:T(1024)}, u32[]{:S(2)}) copy-start(f32[6144]{0:T(1024)} %param.32) | copy-start | bytes 73732
  155.4 24.3 %all-to-all-start.6 = ((bf16[16,4,16,768]{3,2,1,0:T(8,128)(2,1)}), bf16[16,4,16,768]{3,2,1,0:T(8,128)(2,1)S(1)}, u32[]{:S(2)}, u32[]{:S(2)}) async-start(bf16[16,4,16,768]{3,2,1,0:T(8,128)(2,1)} %bitcast.104), calls=%async_computation.6 | async-start | bytes 3145728 | tf_op jit(solution)/shard_map/all_to_all | solution.py:51
  161.3 23.8 %copy-start.9 = (bf16[6144,128]{1,0:T(8,128)(2,1)S(1)}, bf16[6144,128]{1,0:T(8,128)(2,1)}, u32[]{:S(2)}) copy-start(bf16[6144,128]{1,0:T(8,128)(2,1)} %param.33) | copy-start | bytes 4718596
  180.7 12.1 %all-to-all-start.7 = ((bf16[8,16,768]{2,1,0:T(8,128)(2,1)}), bf16[8,16,768]{2,1,0:T(8,128)(2,1)S(1)}, u32[]{:S(2)}, u32[]{:S(2)}) async-start(bf16[8,16,768]{2,1,0:T(8,128)(2,1)} %bitcast.22), calls=%async_computation.7 | async-start | bytes 393216 | tf_op jit(solution)/shard_map/all_to_all | solution.py:51
  185.1 11.7 %collective-permute-start.10 = (bf16[2,768,128]{2,1,0:T(8,128)(2,1)S(1)}, bf16[2,768,128]{2,1,0:T(8,128)(2,1)}, u32[]{:S(2)}, u32[]{:S(2)}) collective-permute-start(bf16[2,768,128]{2,1,0:T(8,128)(2,1)S(1)} %get-tuple-element.79), channel_id=1, source_target_pairs={{0,192},{64,0},{128,64},{192,128},{1,193},{65,1},{129,65},{193,129... | collective-permute-start | bytes 1179656 | tf_op jit(solution)/shard_map/ppermute | solution.py:499
  186.5 11.7 %collective-permute-start.9 = (bf16[2,768,128]{2,1,0:T(8,128)(2,1)S(1)}, bf16[2,768,128]{2,1,0:T(8,128)(2,1)}, u32[]{:S(2)}, u32[]{:S(2)}) collective-permute-start(bf16[2,768,128]{2,1,0:T(8,128)(2,1)S(1)} %get-tuple-element.80), channel_id=1, source_target_pairs={{0,64},{64,128},{128,192},{192,0},{1,65},{65,129},{129,193},{193,1... | collective-permute-start | bytes 1179656 | tf_op jit(solution)/shard_map/ppermute | solution.py:499
  186.7 14.3 %collective-permute-start.8 = (bf16[2,768,128]{2,1,0:T(8,128)(2,1)S(1)}, bf16[2,768,128]{2,1,0:T(8,128)(2,1)}, u32[]{:S(2)}, u32[]{:S(2)}) collective-permute-start(bf16[2,768,128]{2,1,0:T(8,128)(2,1)S(1)} %get-tuple-element.81), channel_id=1, source_target_pairs={{0,128},{64,192},{128,0},{192,64},{1,129},{65,193},{129,1},{193,65... | collective-permute-start | bytes 1179656 | tf_op jit(solution)/shard_map/ppermute | solution.py:499
  193.5 11.9 %all-to-all-start.8 = ((bf16[8,16,768]{2,1,0:T(8,128)(2,1)}), bf16[8,16,768]{2,1,0:T(8,128)(2,1)S(1)}, u32[]{:S(2)}, u32[]{:S(2)}) async-start(bf16[8,16,768]{2,1,0:T(8,128)(2,1)} %broadcast_in_dim.15), calls=%async_computation.8 | async-start | bytes 393216 | tf_op jit(solution)/shard_map/all_to_all | solution.py:51
  216.7 9.4 %collective-permute-start.11 = (bf16[4,8,16,768]{3,2,1,0:T(8,128)(2,1)S(1)}, bf16[4,8,16,768]{3,2,1,0:T(8,128)(2,1)S(1)}, u32[]{:S(2)}, u32[]{:S(2)}) collective-permute-start(bf16[4,8,16,768]{3,2,1,0:T(8,128)(2,1)S(1)} %all_to_all.68.own), channel_id=1, source_target_pairs={{0,1},{1,0},{2,3},{3,2},{4,5},{5,4},{6,7},{7,6},{8,9},{9,8},{10,11... | collective-permute-start | bytes 2359304 | tf_op jit(solution)/shard_map/ppermute | solution.py:47
  228.2 34.0 %copy-start.14 = (f32[2]{0:T(128)S(1)}, f32[2]{0:T(128)}, u32[]{:S(2)}) copy-start(f32[2]{0:T(128)} %param.35) | copy-start | bytes 28
  228.2 15.1 %all-to-all-start.10 = ((bf16[4,144,640]{2,1,0:T(8,128)(2,1)}), bf16[4,144,640]{2,1,0:T(8,128)(2,1)S(1)}, u32[]{:S(2)}, u32[]{:S(2)}) async-start(bf16[4,144,640]{2,1,0:T(8,128)(2,1)} %head.1), calls=%async_computation.10 | async-start | bytes 1474560 | tf_op jit(solution)/shard_map/all_to_all | solution.py:51
  244.9 17.0 %all-to-all-start.11 = ((f32[64,1,128]{2,1,0:T(1,128)}), f32[64,1,128]{2,1,0:T(1,128)S(1)}, u32[]{:S(2)}, u32[]{:S(2)}) async-start(f32[64,1,128]{2,1,0:T(1,128)} %bitcast.34), calls=%async_computation.11 | async-start | bytes 65536 | tf_op jit(solution)/shard_map/all_to_all | solution.py:51

commit v8 on v7

--- a/solution.py
+++ b/solution.py
@@ -449,6 +449,7 @@
         packs.append(lax.ppermute(sends[shift], "x", pairs))
 
     attended = attend(queries, new_keys, new_values, k_cache, v_cache, lengths)
+    attended, packs[1], packs[3] = lax.optimization_barrier((attended, packs[1], packs[3]))
     attended_x = exchange(attended, "z")
     partial_heads, residual_here = project(place, attended_x, packs)
     half = width_all // NC

time: 264 us -> 267 us (1.011)
  blocking collectives: 23.3 us -> 31.2 us
    all_to_all x2, blocking collectives: 23.3 us -> 31.2 us  [exchange(): return lax.all_to_all(value, axes, split_axis=0, concat_axis=0, tiled=True)]
    ppermute x3, waiting for transfers between devices: 9.48 us -> 2.06 us  [shards(): packs.append(lax.ppermute(sends[shift], 'x', pairs))]
    all_to_all x10, waiting for transfers between devices: 86 us -> 91.2 us  [exchange(): return lax.all_to_all(value, axes, split_axis=0, concat_axis=0, tiled=True)]
  transfers between devices with their start and end apart: 22 -> 22, of which waited for: 17 -> 18; matrix products, arithmetic and copies ran while one was open for 5% -> 5% of each run, Pallas kernels for 9% -> 10%
where the time goes in v8:
time: 267 us; the launch traced here: 266 us
  waiting for transfers between devices  102 us (38%)
  starting transfers between devices  73.5 us (28%)
  Pallas kernels  33 us (12%)
  blocking collectives  31.2 us (12%)
  local copies, waits for them, and re-layouts  14 us (5%)
  other arithmetic  11 us (4%)
    all_to_all x10, waiting for transfers between devices, exchange(): return lax.all_to_all(value, axes, split_axis=0, concat_axis=0, tiled=True)  91.2 us
    all_to_all x10, starting transfers between devices, exchange(): return lax.all_to_all(value, axes, split_axis=0, concat_axis=0, tiled=True)  49.1 us
    all_to_all x2, blocking collectives, exchange(): return lax.all_to_all(value, axes, split_axis=0, concat_axis=0, tiled=True)  31.2 us
    ppermute x6, starting transfers between devices, swap_cores(): return lax.ppermute(value, 'c', [(0, 1), (1, 0)])  16.6 us
    pallas_call x2, Pallas kernels, experts(): pl.pallas_call(expert_kernel, out_shape=jax.ShapeDtypeStruct((total, hidd...  12.8 us
    pallas_call x2, Pallas kernels, down(): pl.pallas_call(down_kernel, out_shape=pltpu.HBM((NX, NXY, rows, width), B...  9.77 us
  transfers between devices with their start and end apart: 22, of which 18 were waited for; matrix products, arithmetic and copies ran while one was open for 5% of the time, Pallas kernels for 10%

profile of v8, /device:TPU:1, one launch (start us, length us, event | category | flops | bytes accessed | tf_op | source)
XLA Modules:
  0.0 265.7 jit_solution(154538657824021466)
XLA Ops:
  1.2 3.0 %pack.1 = (bf16[224,768]{1,0:T(8,128)(2,1)}, bf16[224,768]{1,0:T(8,128)(2,1)}, bf16[224,768]{1,0:T(8,128)(2,1)}, bf16[224,768]{1,0:T(8,128)(2,1)}) custom-call(s32[3]{0:T(128)} %pad_add_fusion.place, bf16[192,768]{1,0:T(8,128)(2,1)} %bitcast.112, bf16[192,512]{1,0:T(8,128)(2,1)} %bitcast.114), custom_call_target="tpu_custom_call" | custom-call | tf_op jit(solution)/shard_map/pack/pallas_call | solution.py:140
  4.2 2.1 collective-permute-start
  6.4 1.4 collective-permute-start.1
  7.7 1.6 collective-permute-start.2
  9.4 3.5 %attend.1 = bf16[8,16,768]{2,1,0:T(8,128)(2,1)} custom-call(s32[16]{0:T(128)} %lengths.1, bf16[16,768]{1,0:T(8,128)(2,1)} %refs_0_, bf16[16,128]{1,0:T(8,128)(2,1)} %refs_1_.1, bf16[16,128]{1,0:T(8,128)(2,1)} %refs_2_.1, bf16[16,1,128,128]{3,2,1,0:T(8,128)(2,1)} %refs_3_.1, bf16[16,1,128,128]{3,2,1,0:T(8,128)(2,1)} %refs_4_.1), custom_call_target="tpu_custom_call" | custom-call | flops 34359738368 | bytes 2097152 | tf_op jit(solution)/shard_map/attend/pallas_call | solution.py:100
  13.3 1.5 collective-permute-done.1.refs_3_
  14.8 8.9 %all-to-all-start = ((bf16[8,16,768]{2,1,0:T(8,128)(2,1)}), bf16[8,16,768]{2,1,0:T(8,128)(2,1)S(1)}, u32[]{:S(2)}, u32[]{:S(2)}) async-start(bf16[8,16,768]{2,1,0:T(8,128)(2,1)} %attend.1), calls=%async_computation | async-start | bytes 393216 | tf_op jit(solution)/shard_map/all_to_all | solution.py:51
  23.9 8.5 %all-to-all-done.attended = bf16[8,16,768]{2,1,0:T(8,128)(2,1)S(1)} async-done(((bf16[8,16,768]{2,1,0:T(8,128)(2,1)}), bf16[8,16,768]{2,1,0:T(8,128)(2,1)S(1)}, u32[]{:S(2)}, u32[]{:S(2)}) %all-to-all-start) | async-done | bytes 196640 | tf_op jit(solution)/shard_map/all_to_all | solution.py:51
  33.5 19.9 %all_to_all.67 = bf16[8,32,384]{2,1,0:T(8,128)(2,1)S(1)} all-to-all(bf16[8,32,384]{2,1,0:T(8,128)(2,1)S(1)} %get-tuple-element.50), channel_id=1, replica_groups=mesh['x'=4,'z'=8,'y'=4,'c'=2] {'y','c'}, dimensions={0} | all-to-all | bytes 393216 | tf_op jit(solution)/shard_map/all_to_all | solution.py:51
  54.1 3.4 %all-to-all-start.2 = ((bf16[8,32,384]{2,1,0:T(8,128)(2,1)}), bf16[8,32,384]{2,1,0:T(8,128)(2,1)S(1)}, u32[]{:S(2)}, u32[]{:S(2)}) async-start(bf16[8,32,384]{2,1,0:T(8,128)(2,1)} %broadcast_in_dim.12), calls=%async_computation.2 | async-start | bytes 393216 | tf_op jit(solution)/shard_map/all_to_all | solution.py:51
  57.5 8.6 %all-to-all-done.2 = bf16[8,32,384]{2,1,0:T(8,128)(2,1)S(1)} async-done(((bf16[8,32,384]{2,1,0:T(8,128)(2,1)}), bf16[8,32,384]{2,1,0:T(8,128)(2,1)S(1)}, u32[]{:S(2)}, u32[]{:S(2)}) %all-to-all-start.2) | async-done | bytes 196640 | tf_op jit(solution)/shard_map/all_to_all | solution.py:51
  67.6 1.4 broadcast_in_dim.13
  69.0 5.6 %all-to-all-start.3 = ((bf16[16,8,16,384]{3,2,1,0:T(8,128)(2,1)}), bf16[16,8,16,384]{3,2,1,0:T(8,128)(2,1)}, u32[]{:S(2)}, u32[]{:S(2)}) async-start(bf16[16,8,16,384]{3,2,1,0:T(8,128)(2,1)} %broadcast_in_dim.13), calls=%async_computation.3 | async-start | bytes 3145728 | tf_op jit(solution)/shard_map/all_to_all | solution.py:51
  74.7 1.4 dynamic-slice_bitcast_fusion
  76.1 3.0 %collective-permute-start.3 = (bf16[256,3072]{1,0:T(8,128)(2,1)}, bf16[256,3072]{1,0:T(8,128)(2,1)}, u32[]{:S(2)}, u32[]{:S(2)}) collective-permute-start(bf16[256,3072]{1,0:T(8,128)(2,1)} %dynamic-slice_bitcast_fusion), channel_id=1, source_target_pairs={{0,1},{1,0},{2,3},{3,2},{4,5},{5,4},{6,7},{7,6},{8,9},{9,8},{10,11... | collective-permute-start | bytes 4718600 | tf_op jit(solution)/shard_map/ppermute | solution.py:47
  79.1 4.0 %fusion = (bf16[6144,256]{1,0:T(8,128)(2,1)S(1)}, bf16[6144,256]{1,0:T(8,128)(2,1)}) fusion(bf16[1,6144,256]{2,1,0:T(8,128)(2,1)S(1)} %copy-done.8, f32[6144]{0:T(1024)S(1)} %copy-done.11, bf16[1,6144,256]{2,1,0:T(8,128)(2,1)} %param.28), kind=kLoop, calls=%fused_computation.1 | loop fusion | flops 9437184 | bytes 12607488 | tf_op jit(solution)/shard_map/convert_element_type | solution.py:476
  83.1 11.5 %all-to-all-done.3.own = bf16[16,8,16,384]{3,2,1,0:T(8,128)(2,1)} async-done(((bf16[16,8,16,384]{3,2,1,0:T(8,128)(2,1)}), bf16[16,8,16,384]{3,2,1,0:T(8,128)(2,1)}, u32[]{:S(2)}, u32[]{:S(2)}) %all-to-all-start.3) | async-done | bytes 1572896 | tf_op jit(solution)/shard_map/all_to_all | solution.py:51
  94.6 4.4 %collective-permute-start.4 = (bf16[16,8,16,384]{3,2,1,0:T(8,128)(2,1)}, bf16[16,8,16,384]{3,2,1,0:T(8,128)(2,1)}, u32[]{:S(2)}, u32[]{:S(2)}) collective-permute-start(bf16[16,8,16,384]{3,2,1,0:T(8,128)(2,1)} %all-to-all-done.3.own), channel_id=1, source_target_pairs={{0,1},{1,0},{2,3},{3,2},{4,5},{5,4},{6,7},{7,6},{8,9},{9,8},{10,11... | collective-permute-start | bytes 4718600 | tf_op jit(solution)/shard_map/ppermute | solution.py:47
  98.9 1.3 broadcast_in_dim.14
  100.3 4.4 %all-to-all-start.4 = ((bf16[16,8,16,384]{3,2,1,0:T(8,128)(2,1)}), bf16[16,8,16,384]{3,2,1,0:T(8,128)(2,1)}, u32[]{:S(2)}, u32[]{:S(2)}) async-start(bf16[16,8,16,384]{3,2,1,0:T(8,128)(2,1)} %broadcast_in_dim.14), calls=%async_computation.4 | async-start | bytes 3145728 | tf_op jit(solution)/shard_map/all_to_all | solution.py:51
  105.7 1.9 copy-done.1
  107.6 6.4 %experts.2.mine = bf16[256,256]{1,0:T(8,128)(2,1)S(1)} custom-call(s32[3]{0:T(128)S(1)} %copy-done.7, bf16[16,8,16,384]{3,2,1,0:T(8,128)(2,1)} %all-to-all-done.3.own, bf16[16,8,16,384]{3,2,1,0:T(8,128)(2,1)} %collective-permute-done.4.other, bf16[4,8,192,256]{3,2,1,0:T(8,128)(2,1)S(1)} %bitcast.99, bf16[4,8,192,256]{3,2,1,0:T(8,128)(2,1)S(1)} %bitcast.97, ...), custom_call_target="tpu_custom_call" | custom-call | flops 1610612736 | bytes 10485760 | tf_op jit(solution)/shard_map/experts/pallas_call | solution.py:271
  114.1 1.3 collective-permute-done.5.theirs
  115.4 4.9 %down.2 = bf16[4,16,16,768]{3,2,1,0:T(8,128)(2,1)} custom-call(s32[3]{0:T(128)S(1)} %copy-done.7, bf16[256,256]{1,0:T(8,128)(2,1)S(1)} %experts.2.mine, bf16[256,256]{1,0:T(8,128)(2,1)S(1)} %collective-permute-done.5.theirs, bf16[256,6144]{1,0:T(8,128)(2,1)S(1)} %bitcast.101, bf16[256,3072]{1,0:T(8,128)(2,1)} %collective-permute-done.3.w_theirs), custom_call_target="tpu_custom_call" | custom-call | flops 805306368 | bytes 5242880 | tf_op jit(solution)/shard_map/down/pallas_call | solution.py:323
  120.4 8.0 %all-to-all-done.4.own = bf16[16,8,16,384]{3,2,1,0:T(8,128)(2,1)} async-done(((bf16[16,8,16,384]{3,2,1,0:T(8,128)(2,1)}), bf16[16,8,16,384]{3,2,1,0:T(8,128)(2,1)}, u32[]{:S(2)}, u32[]{:S(2)}) %all-to-all-start.4) | async-done | bytes 1572896 | tf_op jit(solution)/shard_map/all_to_all | solution.py:51
  129.6 4.6 %all-to-all-start.5 = ((bf16[16,4,16,768]{3,2,1,0:T(8,128)(2,1)}), bf16[16,4,16,768]{3,2,1,0:T(8,128)(2,1)}, u32[]{:S(2)}, u32[]{:S(2)}) async-start(bf16[16,4,16,768]{3,2,1,0:T(8,128)(2,1)} %bitcast.105), calls=%async_computation.5 | async-start | bytes 3145728 | tf_op jit(solution)/shard_map/all_to_all | solution.py:51
  134.3 1.9 copy-done.2
  136.2 6.4 %experts.3.mine = bf16[256,256]{1,0:T(8,128)(2,1)S(1)} custom-call(s32[3]{0:T(128)S(1)} %copy-done.7, bf16[16,8,16,384]{3,2,1,0:T(8,128)(2,1)} %all-to-all-done.4.own, bf16[16,8,16,384]{3,2,1,0:T(8,128)(2,1)} %collective-permute-done.6.other, bf16[4,8,192,256]{3,2,1,0:T(8,128)(2,1)S(1)} %bitcast.100, bf16[4,8,192,256]{3,2,1,0:T(8,128)(2,1)S(1)} %bitcast.98, ...), custom_call_target="tpu_custom_call" | custom-call | flops 1610612736 | bytes 10485760 | tf_op jit(solution)/shard_map/experts/pallas_call | solution.py:271
  144.0 4.9 %down.3 = bf16[4,16,16,768]{3,2,1,0:T(8,128)(2,1)} custom-call(s32[3]{0:T(128)S(1)} %copy-done.7, bf16[256,256]{1,0:T(8,128)(2,1)S(1)} %experts.3.mine, bf16[256,256]{1,0:T(8,128)(2,1)S(1)} %collective-permute-done.7.theirs, bf16[256,6144]{1,0:T(8,128)(2,1)S(1)} %bitcast.102, bf16[256,3072]{1,0:T(8,128)(2,1)} %collective-permute-done.3.w_theirs), custom_call_target="tpu_custom_call" | custom-call | flops 805306368 | bytes 5242880 | tf_op jit(solution)/shard_map/down/pallas_call | solution.py:323
  148.9 9.1 %all-to-all-done.5 = bf16[16,4,16,768]{3,2,1,0:T(8,128)(2,1)} async-done(((bf16[16,4,16,768]{3,2,1,0:T(8,128)(2,1)}), bf16[16,4,16,768]{3,2,1,0:T(8,128)(2,1)}, u32[]{:S(2)}, u32[]{:S(2)}) %all-to-all-start.5) | async-done | bytes 1572896 | tf_op jit(solution)/shard_map/all_to_all | solution.py:51
  158.0 3.9 %all-to-all-start.6 = ((bf16[16,4,16,768]{3,2,1,0:T(8,128)(2,1)}), bf16[16,4,16,768]{3,2,1,0:T(8,128)(2,1)S(1)}, u32[]{:S(2)}, u32[]{:S(2)}) async-start(bf16[16,4,16,768]{3,2,1,0:T(8,128)(2,1)} %bitcast.104), calls=%async_computation.6 | async-start | bytes 3145728 | tf_op jit(solution)/shard_map/all_to_all | solution.py:51
  162.2 1.6 reduce_sum.61
  163.9 18.5 %all-to-all-done.6 = bf16[16,4,16,768]{3,2,1,0:T(8,128)(2,1)S(1)} async-done(((bf16[16,4,16,768]{3,2,1,0:T(8,128)(2,1)}), bf16[16,4,16,768]{3,2,1,0:T(8,128)(2,1)S(1)}, u32[]{:S(2)}, u32[]{:S(2)}) %all-to-all-start.6) | async-done | bytes 1572896 | tf_op jit(solution)/shard_map/all_to_all | solution.py:51
  183.2 3.7 %all-to-all-start.7 = ((bf16[8,16,768]{2,1,0:T(8,128)(2,1)}), bf16[8,16,768]{2,1,0:T(8,128)(2,1)S(1)}, u32[]{:S(2)}, u32[]{:S(2)}) async-start(bf16[8,16,768]{2,1,0:T(8,128)(2,1)} %bitcast.22), calls=%async_computation.7 | async-start | bytes 393216 | tf_op jit(solution)/shard_map/all_to_all | solution.py:51
  188.0 1.4 collective-permute-start.10
  190.9 4.7 %all-to-all-done.7 = bf16[8,16,768]{2,1,0:T(8,128)(2,1)S(1)} async-done(((bf16[8,16,768]{2,1,0:T(8,128)(2,1)}), bf16[8,16,768]{2,1,0:T(8,128)(2,1)S(1)}, u32[]{:S(2)}, u32[]{:S(2)}) %all-to-all-start.7) | async-done | bytes 196640 | tf_op jit(solution)/shard_map/all_to_all | solution.py:51
  196.3 3.4 %all-to-all-start.8 = ((bf16[8,16,768]{2,1,0:T(8,128)(2,1)}), bf16[8,16,768]{2,1,0:T(8,128)(2,1)S(1)}, u32[]{:S(2)}, u32[]{:S(2)}) async-start(bf16[8,16,768]{2,1,0:T(8,128)(2,1)} %broadcast_in_dim.15), calls=%async_computation.8 | async-start | bytes 393216 | tf_op jit(solution)/shard_map/all_to_all | solution.py:51
  201.1 2.8 %collective-permute-done.8 = bf16[2,768,128]{2,1,0:T(8,128)(2,1)} collective-permute-done((bf16[2,768,128]{2,1,0:T(8,128)(2,1)S(1)}, bf16[2,768,128]{2,1,0:T(8,128)(2,1)}, u32[]{:S(2)}, u32[]{:S(2)}) %collective-permute-start.8) | collective-permute-done | bytes 393248 | tf_op jit(solution)/shard_map/ppermute | solution.py:500
  203.8 1.7 multiply_convert_fusion.3
  205.8 2.4 all-to-all-done.8
  208.3 11.3 %all_to_all.68.own = bf16[4,8,16,768]{3,2,1,0:T(8,128)(2,1)S(1)} all-to-all(bf16[4,8,16,768]{3,2,1,0:T(8,128)(2,1)S(1)} %broadcast_in_dim.16), channel_id=1, replica_groups=mesh['x'=4,'z'=8,'y'=4,'c'=2] {'y'}, dimensions={0} | all-to-all | bytes 1572864 | tf_op jit(solution)/shard_map/all_to_all | solution.py:51
  219.6 7.5 %collective-permute-start.11 = (bf16[4,8,16,768]{3,2,1,0:T(8,128)(2,1)S(1)}, bf16[4,8,16,768]{3,2,1,0:T(8,128)(2,1)S(1)}, u32[]{:S(2)}, u32[]{:S(2)}) collective-permute-start(bf16[4,8,16,768]{3,2,1,0:T(8,128)(2,1)S(1)} %all_to_all.68.own), channel_id=1, source_target_pairs={{0,1},{1,0},{2,3},{3,2},{4,5},{5,4},{6,7},{7,6},{8,9},{9,8},{10,11... | collective-permute-start | bytes 2359304 | tf_op jit(solution)/shard_map/ppermute | solution.py:47
  227.1 1.9 collective-permute-done.11.other
  229.2 1.9 head.1
  231.1 3.6 %all-to-all-start.10 = ((bf16[4,144,640]{2,1,0:T(8,128)(2,1)}), bf16[4,144,640]{2,1,0:T(8,128)(2,1)S(1)}, u32[]{:S(2)}, u32[]{:S(2)}) async-start(bf16[4,144,640]{2,1,0:T(8,128)(2,1)} %head.1), calls=%async_computation.10 | async-start | bytes 1474560 | tf_op jit(solution)/shard_map/all_to_all | solution.py:51
  235.0 11.2 %all-to-all-done.10.parts = bf16[4,144,640]{2,1,0:T(8,128)(2,1)S(1)} async-done(((bf16[4,144,640]{2,1,0:T(8,128)(2,1)}), bf16[4,144,640]{2,1,0:T(8,128)(2,1)S(1)}, u32[]{:S(2)}, u32[]{:S(2)}) %all-to-all-start.10) | async-done | bytes 737312 | tf_op jit(solution)/shard_map/all_to_all | solution.py:51
  247.7 7.6 %all-to-all-start.11 = ((f32[64,1,128]{2,1,0:T(1,128)}), f32[64,1,128]{2,1,0:T(1,128)S(1)}, u32[]{:S(2)}, u32[]{:S(2)}) async-start(f32[64,1,128]{2,1,0:T(1,128)} %bitcast.34), calls=%async_computation.11 | async-start | bytes 65536 | tf_op jit(solution)/shard_map/all_to_all | solution.py:51
  256.1 8.7 %all-to-all-done.11 = f32[64,1,128]{2,1,0:T(1,128)S(1)} async-done(((f32[64,1,128]{2,1,0:T(1,128)}), f32[64,1,128]{2,1,0:T(1,128)S(1)}, u32[]{:S(2)}, u32[]{:S(2)}) %all-to-all-start.11) | async-done | bytes 32800 | tf_op jit(solution)/shard_map/all_to_all | solution.py:51
  (91 shorter events, 17.7 us)
Async XLA Ops:
  0.6 234.1 %copy-start = (s32[512]{0:T(512)S(1)}, s32[512]{0:T(512)}, u32[]{:S(2)}) copy-start(s32[512]{0:T(512)} %param.34) | copy-start | bytes 6148
  4.2 28.1 %copy-start.6 = (bf16[224,768]{1,0:T(8,128)(2,1)S(1)}, bf16[224,768]{1,0:T(8,128)(2,1)}, u32[]{:S(2)}) copy-start(bf16[224,768]{1,0:T(8,128)(2,1)} %get-tuple-element.46.refs_0_) | copy-start | bytes 1032196
  4.2 28.1 %copy-start.7 = (s32[3]{0:T(128)S(1)}, s32[3]{0:T(128)}, u32[]{:S(2)}) copy-start(s32[3]{0:T(128)} %pad_add_fusion.place) | copy-start | bytes 40
  4.2 9.1 %collective-permute-start = (bf16[224,768]{1,0:T(8,128)(2,1)}, bf16[224,768]{1,0:T(8,128)(2,1)S(1)}, u32[]{:S(2)}, u32[]{:S(2)}) collective-permute-start(bf16[224,768]{1,0:T(8,128)(2,1)} %get-tuple-element.43), channel_id=1, source_target_pairs={{0,64},{64,128},{128,192},{192,0},{1,65},{65,129},{129,193},{193,1... | collective-permute-start | bytes 1032200 | tf_op jit(solution)/shard_map/ppermute | solution.py:449
  6.4 8.5 %collective-permute-start.1 = (bf16[224,768]{1,0:T(8,128)(2,1)}, bf16[224,768]{1,0:T(8,128)(2,1)S(1)}, u32[]{:S(2)}, u32[]{:S(2)}) collective-permute-start(bf16[224,768]{1,0:T(8,128)(2,1)} %get-tuple-element.44), channel_id=1, source_target_pairs={{0,192},{64,0},{128,64},{192,128},{1,193},{65,1},{129,65},{193,129... | collective-permute-start | bytes 1032200 | tf_op jit(solution)/shard_map/ppermute | solution.py:449
  7.7 16.1 %collective-permute-start.2 = (bf16[224,768]{1,0:T(8,128)(2,1)}, bf16[224,768]{1,0:T(8,128)(2,1)S(1)}, u32[]{:S(2)}, u32[]{:S(2)}) collective-permute-start(bf16[224,768]{1,0:T(8,128)(2,1)} %get-tuple-element.48), channel_id=1, source_target_pairs={{0,128},{64,192},{128,0},{192,64},{1,129},{65,193},{129,1},{193,65... | collective-permute-start | bytes 1032200 | tf_op jit(solution)/shard_map/ppermute | solution.py:449
  14.8 17.5 %all-to-all-start = ((bf16[8,16,768]{2,1,0:T(8,128)(2,1)}), bf16[8,16,768]{2,1,0:T(8,128)(2,1)S(1)}, u32[]{:S(2)}, u32[]{:S(2)}) async-start(bf16[8,16,768]{2,1,0:T(8,128)(2,1)} %attend.1), calls=%async_computation | async-start | bytes 393216 | tf_op jit(solution)/shard_map/all_to_all | solution.py:51
  23.7 42.4 %copy-start.13 = (s32[512,2]{0,1:T(2,128)S(1)}, s32[512,2]{0,1:T(2,128)}, u32[]{:S(2)}) copy-start(s32[512,2]{0,1:T(2,128)} %param.31) | copy-start | bytes 12292
  23.7 42.5 %copy-start.10 = (bf16[6144,8]{0,1:T(8,128)(2,1)S(1)}, bf16[6144,8]{0,1:T(8,128)(2,1)}, u32[]{:S(2)}) copy-start(bf16[6144,8]{0,1:T(8,128)(2,1)} %param.26) | copy-start | bytes 294916
  23.7 42.5 %copy-start.11 = (f32[6144]{0:T(1024)S(1)}, f32[6144]{0:T(1024)}, u32[]{:S(2)}) copy-start(f32[6144]{0:T(1024)} %param.27) | copy-start | bytes 73732
  54.1 12.0 %all-to-all-start.2 = ((bf16[8,32,384]{2,1,0:T(8,128)(2,1)}), bf16[8,32,384]{2,1,0:T(8,128)(2,1)S(1)}, u32[]{:S(2)}, u32[]{:S(2)}) async-start(bf16[8,32,384]{2,1,0:T(8,128)(2,1)} %broadcast_in_dim.12), calls=%async_computation.2 | async-start | bytes 393216 | tf_op jit(solution)/shard_map/all_to_all | solution.py:51
  69.0 5.6 %copy-start.3 = (bf16[1,256,6144]{2,1,0:T(8,128)(2,1)S(1)}, bf16[1,256,6144]{2,1,0:T(8,128)(2,1)}, u32[]{:S(2)}) copy-start(bf16[1,256,6144]{2,1,0:T(8,128)(2,1)} %param.30) | copy-start | bytes 9437188
  69.0 25.5 %all-to-all-start.3 = ((bf16[16,8,16,384]{3,2,1,0:T(8,128)(2,1)}), bf16[16,8,16,384]{3,2,1,0:T(8,128)(2,1)}, u32[]{:S(2)}, u32[]{:S(2)}) async-start(bf16[16,8,16,384]{3,2,1,0:T(8,128)(2,1)} %broadcast_in_dim.13), calls=%async_computation.3 | async-start | bytes 3145728 | tf_op jit(solution)/shard_map/all_to_all | solution.py:51
  74.7 4.4 %copy-start.8 = (bf16[1,6144,256]{2,1,0:T(8,128)(2,1)S(1)}, bf16[1,6144,256]{2,1,0:T(8,128)(2,1)}, u32[]{:S(2)}) copy-start(bf16[1,6144,256]{2,1,0:T(8,128)(2,1)} %param.29) | copy-start | bytes 9437188
  76.1 18.5 %collective-permute-start.3 = (bf16[256,3072]{1,0:T(8,128)(2,1)}, bf16[256,3072]{1,0:T(8,128)(2,1)}, u32[]{:S(2)}, u32[]{:S(2)}) collective-permute-start(bf16[256,3072]{1,0:T(8,128)(2,1)} %dynamic-slice_bitcast_fusion), channel_id=1, source_target_pairs={{0,1},{1,0},{2,3},{3,2},{4,5},{5,4},{6,7},{7,6},{8,9},{9,8},{10,11... | collective-permute-start | bytes 4718600 | tf_op jit(solution)/shard_map/ppermute | solution.py:47
  94.6 11.1 %collective-permute-start.4 = (bf16[16,8,16,384]{3,2,1,0:T(8,128)(2,1)}, bf16[16,8,16,384]{3,2,1,0:T(8,128)(2,1)}, u32[]{:S(2)}, u32[]{:S(2)}) collective-permute-start(bf16[16,8,16,384]{3,2,1,0:T(8,128)(2,1)} %all-to-all-done.3.own), channel_id=1, source_target_pairs={{0,1},{1,0},{2,3},{3,2},{4,5},{5,4},{6,7},{7,6},{8,9},{9,8},{10,11... | collective-permute-start | bytes 4718600 | tf_op jit(solution)/shard_map/ppermute | solution.py:47
  100.3 28.1 %all-to-all-start.4 = ((bf16[16,8,16,384]{3,2,1,0:T(8,128)(2,1)}), bf16[16,8,16,384]{3,2,1,0:T(8,128)(2,1)}, u32[]{:S(2)}, u32[]{:S(2)}) async-start(bf16[16,8,16,384]{3,2,1,0:T(8,128)(2,1)} %broadcast_in_dim.14), calls=%async_computation.4 | async-start | bytes 3145728 | tf_op jit(solution)/shard_map/all_to_all | solution.py:51
  105.7 1.9 copy-start.1
  107.6 7.9 %copy-start.4 = (bf16[1,256,6144]{2,1,0:T(8,128)(2,1)S(1)}, bf16[1,256,6144]{2,1,0:T(8,128)(2,1)}, u32[]{:S(2)}) copy-start(bf16[1,256,6144]{2,1,0:T(8,128)(2,1)} %param.30) | copy-start | bytes 9437188
  114.0 1.4 collective-permute-start.5
  128.3 5.9 %collective-permute-start.6 = (bf16[16,8,16,384]{3,2,1,0:T(8,128)(2,1)}, bf16[16,8,16,384]{3,2,1,0:T(8,128)(2,1)}, u32[]{:S(2)}, u32[]{:S(2)}) collective-permute-start(bf16[16,8,16,384]{3,2,1,0:T(8,128)(2,1)} %all-to-all-done.4.own), channel_id=1, source_target_pairs={{0,1},{1,0},{2,3},{3,2},{4,5},{5,4},{6,7},{7,6},{8,9},{9,8},{10,11... | collective-permute-start | bytes 4718600 | tf_op jit(solution)/shard_map/ppermute | solution.py:47
  129.6 28.4 %all-to-all-start.5 = ((bf16[16,4,16,768]{3,2,1,0:T(8,128)(2,1)}), bf16[16,4,16,768]{3,2,1,0:T(8,128)(2,1)}, u32[]{:S(2)}, u32[]{:S(2)}) async-start(bf16[16,4,16,768]{3,2,1,0:T(8,128)(2,1)} %bitcast.105), calls=%async_computation.5 | async-start | bytes 3145728 | tf_op jit(solution)/shard_map/all_to_all | solution.py:51
  134.3 1.9 copy-start.2
  136.2 7.9 %copy-start.5 = (bf16[1,256,6144]{2,1,0:T(8,128)(2,1)S(1)}, bf16[1,256,6144]{2,1,0:T(8,128)(2,1)}, u32[]{:S(2)}) copy-start(bf16[1,256,6144]{2,1,0:T(8,128)(2,1)} %param.30) | copy-start | bytes 9437188
  142.6 1.4 collective-permute-start.7
  158.0 4.1 %copy-start.12 = (f32[6144]{0:T(1024)S(1)}, f32[6144]{0:T(1024)}, u32[]{:S(2)}) copy-start(f32[6144]{0:T(1024)} %param.32) | copy-start | bytes 73732
  158.0 24.3 %all-to-all-start.6 = ((bf16[16,4,16,768]{3,2,1,0:T(8,128)(2,1)}), bf16[16,4,16,768]{3,2,1,0:T(8,128)(2,1)S(1)}, u32[]{:S(2)}, u32[]{:S(2)}) async-start(bf16[16,4,16,768]{3,2,1,0:T(8,128)(2,1)} %bitcast.104), calls=%async_computation.6 | async-start | bytes 3145728 | tf_op jit(solution)/shard_map/all_to_all | solution.py:51
  163.9 24.1 %copy-start.9 = (bf16[6144,128]{1,0:T(8,128)(2,1)S(1)}, bf16[6144,128]{1,0:T(8,128)(2,1)}, u32[]{:S(2)}) copy-start(bf16[6144,128]{1,0:T(8,128)(2,1)} %param.33) | copy-start | bytes 4718596
  183.2 12.4 %all-to-all-start.7 = ((bf16[8,16,768]{2,1,0:T(8,128)(2,1)}), bf16[8,16,768]{2,1,0:T(8,128)(2,1)S(1)}, u32[]{:S(2)}, u32[]{:S(2)}) async-start(bf16[8,16,768]{2,1,0:T(8,128)(2,1)} %bitcast.22), calls=%async_computation.7 | async-start | bytes 393216 | tf_op jit(solution)/shard_map/all_to_all | solution.py:51
  188.0 11.7 %collective-permute-start.10 = (bf16[2,768,128]{2,1,0:T(8,128)(2,1)S(1)}, bf16[2,768,128]{2,1,0:T(8,128)(2,1)}, u32[]{:S(2)}, u32[]{:S(2)}) collective-permute-start(bf16[2,768,128]{2,1,0:T(8,128)(2,1)S(1)} %get-tuple-element.85), channel_id=1, source_target_pairs={{0,192},{64,0},{128,64},{192,128},{1,193},{65,1},{129,65},{193,129... | collective-permute-start | bytes 1179656 | tf_op jit(solution)/shard_map/ppermute | solution.py:500
  189.4 11.7 %collective-permute-start.9 = (bf16[2,768,128]{2,1,0:T(8,128)(2,1)S(1)}, bf16[2,768,128]{2,1,0:T(8,128)(2,1)}, u32[]{:S(2)}, u32[]{:S(2)}) collective-permute-start(bf16[2,768,128]{2,1,0:T(8,128)(2,1)S(1)} %get-tuple-element.86), channel_id=1, source_target_pairs={{0,64},{64,128},{128,192},{192,0},{1,65},{65,129},{129,193},{193,1... | collective-permute-start | bytes 1179656 | tf_op jit(solution)/shard_map/ppermute | solution.py:500
  189.6 14.3 %collective-permute-start.8 = (bf16[2,768,128]{2,1,0:T(8,128)(2,1)S(1)}, bf16[2,768,128]{2,1,0:T(8,128)(2,1)}, u32[]{:S(2)}, u32[]{:S(2)}) collective-permute-start(bf16[2,768,128]{2,1,0:T(8,128)(2,1)S(1)} %get-tuple-element.87), channel_id=1, source_target_pairs={{0,128},{64,192},{128,0},{192,64},{1,129},{65,193},{129,1},{193,65... | collective-permute-start | bytes 1179656 | tf_op jit(solution)/shard_map/ppermute | solution.py:500
  196.3 11.9 %all-to-all-start.8 = ((bf16[8,16,768]{2,1,0:T(8,128)(2,1)}), bf16[8,16,768]{2,1,0:T(8,128)(2,1)S(1)}, u32[]{:S(2)}, u32[]{:S(2)}) async-start(bf16[8,16,768]{2,1,0:T(8,128)(2,1)} %broadcast_in_dim.15), calls=%async_computation.8 | async-start | bytes 393216 | tf_op jit(solution)/shard_map/all_to_all | solution.py:51
  219.6 9.4 %collective-permute-start.11 = (bf16[4,8,16,768]{3,2,1,0:T(8,128)(2,1)S(1)}, bf16[4,8,16,768]{3,2,1,0:T(8,128)(2,1)S(1)}, u32[]{:S(2)}, u32[]{:S(2)}) collective-permute-start(bf16[4,8,16,768]{3,2,1,0:T(8,128)(2,1)S(1)} %all_to_all.68.own), channel_id=1, source_target_pairs={{0,1},{1,0},{2,3},{3,2},{4,5},{5,4},{6,7},{7,6},{8,9},{9,8},{10,11... | collective-permute-start | bytes 2359304 | tf_op jit(solution)/shard_map/ppermute | solution.py:47
  231.1 34.1 %copy-start.14 = (f32[2]{0:T(128)S(1)}, f32[2]{0:T(128)}, u32[]{:S(2)}) copy-start(f32[2]{0:T(128)} %param.35) | copy-start | bytes 28
  231.1 15.1 %all-to-all-start.10 = ((bf16[4,144,640]{2,1,0:T(8,128)(2,1)}), bf16[4,144,640]{2,1,0:T(8,128)(2,1)S(1)}, u32[]{:S(2)}, u32[]{:S(2)}) async-start(bf16[4,144,640]{2,1,0:T(8,128)(2,1)} %head.1), calls=%async_computation.10 | async-start | bytes 1474560 | tf_op jit(solution)/shard_map/all_to_all | solution.py:51
  247.7 17.0 %all-to-all-start.11 = ((f32[64,1,128]{2,1,0:T(1,128)}), f32[64,1,128]{2,1,0:T(1,128)S(1)}, u32[]{:S(2)}, u32[]{:S(2)}) async-start(f32[64,1,128]{2,1,0:T(1,128)} %bitcast.34), calls=%async_computation.11 | async-start | bytes 65536 | tf_op jit(solution)/shard_map/all_to_all | solution.py:51
